TPU v7x, 32 devices: a whole 2x2x4 slice. The times are simulated.
32 devices in a mesh: dp: 2 (over x), seq: 4 (over y, core), heads: 4 (over z).
Axes of the slice: x: 2, y: 2, z: 4, core: 2. Of those that a mesh axis runs over, the one named last changes fastest.
Arguments:
- tokens: bfloat16 [8, 1024, 1024], P('dp', ('seq', 'heads')), may hold values from -6 to 6
- querymap: bfloat16 [1024, 1024], P(None, 'heads'), may hold values from -0.1875 to 0.1875
- querybias: bfloat16 [1024], P('heads'), may hold values from -2 to 2
- keymap: bfloat16 [1024, 1024], P(None, 'heads'), may hold values from -0.1875 to 0.1875
- valuemap: bfloat16 [1024, 1024], P(None, 'heads'), may hold values from -0.1875 to 0.1875
- valuebias: bfloat16 [1024], P('heads'), may hold values from -2 to 2
- mergemap: bfloat16 [1024, 1024], P('heads'), may hold values from -0.5 to 0.5
- mergebias: bfloat16 [1024], replicated, may hold values from -2 to 2
- normgain: bfloat16 [1024], replicated, may hold values from 0.69921875 to 1.296875
- normshift: bfloat16 [1024], replicated, may hold values from -2 to 2
- innermap: bfloat16 [1024, 4096], P(None, 'heads'), may hold values from -0.1875 to 0.1875
- innerbias: bfloat16 [4096], P('heads'), may hold values from -2 to 2
- outermap: bfloat16 [4096, 1024], P('heads'), may hold values from -0.09375 to 0.09375
- outerbias: bfloat16 [1024], replicated, may hold values from -2 to 2
- finalgain: bfloat16 [1024], replicated, may hold values from 0.69921875 to 1.296875
- finalshift: bfloat16 [1024], replicated, may hold values from -2 to 2
- lengths: int32 [8], P('dp'), may hold values from 16 to 1024, as said below
- cotangent: bfloat16 [8, 1024, 1024], P('dp', ('seq', 'heads')), may hold values from -6 to 6
Outputs:
- layer_output: bfloat16 [8, 1024, 1024], P('dp', ('seq', 'heads'))
- tokens_grad: bfloat16 [8, 1024, 1024], P('dp', ('seq', 'heads'))
- querymap_grad: float32 [1024, 1024], P(None, 'heads')
- querybias_grad: float32 [1024], P('heads')
- keymap_grad: float32 [1024, 1024], P(None, 'heads')
- valuemap_grad: float32 [1024, 1024], P(None, 'heads')
- valuebias_grad: float32 [1024], P('heads')
- mergemap_grad: float32 [1024, 1024], P('heads')
- mergebias_grad: float32 [1024], replicated
- normgain_grad: float32 [1024], replicated
- normshift_grad: float32 [1024], replicated
- innermap_grad: float32 [1024, 4096], P(None, 'heads')
- innerbias_grad: float32 [4096], P('heads')
- outermap_grad: float32 [4096, 1024], P('heads')
- outerbias_grad: float32 [1024], replicated
- finalgain_grad: float32 [1024], replicated
- finalshift_grad: float32 [1024], replicated
Inputs may be any that keep to these rules, and one draw needn't show every extreme that they name: `lengths`: in each aligned block of 4 proteins (those of one dp index) one protein, drawn from the seed, has length 1024; the others are mostly short.
All inputs are finite; a program needn't handle non-finite values.
Results may differ from a plain program's by a relative error of at most 0.02.
Values may be sent and summed in bfloat16 or wider, within the bound.
No kernel may reach another device: no remote copies, remote signals or barrier semaphores. Data moves between devices by JAX's collectives and lax.ppermute only.
A program may use at most 192 MiB of HBM per device.

v0:
```python
import jax
import jax.numpy as jnp
from jax import lax
from jax.sharding import PartitionSpec as P

HEAD_DIM = 64


epsilon = 1e-06
score_scale = 0.125
masked_score = -1000000000.0
floor_value = -1e30


def layer_norm_parts(values, scales, offsets):
    centered = values - jnp.mean(values, axis=-1, keepdims=True)
    variance = jnp.mean(centered * centered, axis=-1, keepdims=True)
    inverse = lax.rsqrt(variance + epsilon)
    unitized = centered * inverse
    return (unitized * scales + offsets, unitized, inverse)


def layer_norm_back(grad_rows, unitized, inverse, scales):
    scaled = grad_rows * scales
    grad_mean = jnp.mean(scaled, axis=-1, keepdims=True)
    cross_mean = jnp.mean(scaled * unitized, axis=-1, keepdims=True)
    return inverse * (scaled - grad_mean - unitized * cross_mean)


def score_grads(query_heads, key_heads, value_heads, dcontext_heads, logsum, row_delta, key_live):
    scores = (
        jnp.einsum("bqhd,bkhd->bqhk", query_heads, key_heads, preferred_element_type=jnp.float32)
        * score_scale
    )
    scores = jnp.where(key_live[:, None, None, :], scores, masked_score)
    probs = jnp.exp(scores - logsum[..., None])
    dprobs = jnp.einsum(
        "bqhd,bkhd->bqhk", dcontext_heads, value_heads, preferred_element_type=jnp.float32
    )
    dscores = (probs * (dprobs - row_delta[..., None])).astype(jnp.bfloat16)
    return (probs.astype(jnp.bfloat16), dscores)


def shards(
    tokens,
    querymap,
    querybias,
    keymap,
    valuemap,
    valuebias,
    mergemap,
    mergebias,
    normgain,
    normshift,
    innermap,
    innerbias,
    outermap,
    outerbias,
    finalgain,
    finalshift,
    lengths,
    cotangent,
):
    proteins, share_rows, model_width = tokens.shape
    group_rows = share_rows * lax.axis_size("heads")
    group_start = lax.axis_index("seq") * group_rows
    share_start = group_start + lax.axis_index("heads") * share_rows
    local_width = querymap.shape[1]
    heads_here = local_width // HEAD_DIM
    own_positions = share_start + jnp.arange(share_rows, dtype=jnp.int32)
    share_live = (own_positions[None, :] < lengths[:, None]).astype(jnp.float32)
    key_positions = group_start + jnp.arange(group_rows, dtype=jnp.int32)
    group_live = key_positions[None, :] < lengths[:, None]
    collected_rows = lax.all_gather(tokens, "heads", axis=1, tiled=True)
    queries = (
        jnp.dot(collected_rows, querymap, preferred_element_type=jnp.float32)
        + querybias.astype(jnp.float32)
    ).astype(jnp.bfloat16)
    keyrows = jnp.dot(collected_rows, keymap, preferred_element_type=jnp.float32).astype(
        jnp.bfloat16
    )
    valrows = (
        jnp.dot(collected_rows, valuemap, preferred_element_type=jnp.float32)
        + valuebias.astype(jnp.float32)
    ).astype(jnp.bfloat16)
    head_shape = (proteins, group_rows, heads_here, HEAD_DIM)
    query_heads = queries.reshape(head_shape)
    key_heads = keyrows.reshape(head_shape)
    value_heads = valrows.reshape(head_shape)
    stat_shape = (proteins, group_rows, heads_here)
    highest = jnp.full(stat_shape, floor_value, jnp.float32)
    key_portion = lax.all_gather(keyrows, "seq", axis=1, tiled=True)
    value_portion = lax.all_gather(valrows, "seq", axis=1, tiled=True)
    portion_rows = key_portion.shape[1]
    remote_keys = key_portion.reshape(proteins, portion_rows, heads_here, HEAD_DIM)
    remote_values = value_portion.reshape(proteins, portion_rows, heads_here, HEAD_DIM)
    scores = (
        jnp.einsum("bqhd,bkhd->bqhk", query_heads, remote_keys, preferred_element_type=jnp.float32)
        * score_scale
    )
    key_live = jnp.arange(portion_rows, dtype=jnp.int32)[None, :] < lengths[:, None]
    scores = jnp.where(key_live[:, None, None, :], scores, masked_score)
    new_high = jnp.maximum(highest, jnp.max(scores, axis=-1))
    weights = jnp.exp(scores - new_high[..., None])
    denominator = jnp.sum(weights, axis=-1)
    weighted = jnp.einsum(
        "bqhk,bkhd->bqhd",
        weights.astype(jnp.bfloat16),
        remote_values,
        preferred_element_type=jnp.float32,
    )
    highest, denominator, weighted = (new_high, denominator, weighted)
    logsum = highest + jnp.log(denominator)
    context_heads = weighted / denominator[..., None]
    context_reduced = context_heads.reshape(proteins, group_rows, local_width).astype(jnp.bfloat16)
    merged_part = jnp.dot(context_reduced, mergemap, preferred_element_type=jnp.float32)
    merged = lax.psum_scatter(
        merged_part, "heads", scatter_dimension=1, tiled=True
    ) + mergebias.astype(jnp.float32)
    normed, first_unit, first_inverse = layer_norm_parts(
        tokens.astype(jnp.float32) + merged,
        normgain.astype(jnp.float32),
        normshift.astype(jnp.float32),
    )
    normalized_full = lax.all_gather(normed.astype(jnp.bfloat16), "heads", axis=1, tiled=True)
    inner_pre = jnp.dot(
        normalized_full, innermap, preferred_element_type=jnp.float32
    ) + innerbias.astype(jnp.float32)

    def gelu_exact(values):
        return jax.nn.gelu(values, approximate=False)

    active_rows, gelu_pull = jax.vjp(gelu_exact, inner_pre)
    active_reduced = active_rows.astype(jnp.bfloat16)
    branch_part = jnp.dot(active_reduced, outermap, preferred_element_type=jnp.float32)
    branch = lax.psum_scatter(
        branch_part, "heads", scatter_dimension=1, tiled=True
    ) + outerbias.astype(jnp.float32)
    layer_output, final_unit, final_inverse = layer_norm_parts(
        normed + branch, finalgain.astype(jnp.float32), finalshift.astype(jnp.float32)
    )
    grad_rows = cotangent.astype(jnp.float32) * share_live[:, :, None]
    finalgain_part = jnp.sum(grad_rows * final_unit, axis=(0, 1))
    finalshift_part = jnp.sum(grad_rows, axis=(0, 1))
    dsum_final = layer_norm_back(
        grad_rows, final_unit, final_inverse, finalgain.astype(jnp.float32)
    )
    dbranch_low = dsum_final.astype(jnp.bfloat16)
    outerbias_part = jnp.sum(dbranch_low.astype(jnp.float32), axis=(0, 1))
    branch_gradient_full = lax.all_gather(dbranch_low, "heads", axis=1, tiled=True)
    outermap_part = jnp.einsum(
        "gsl,gsj->lj", active_reduced, branch_gradient_full, preferred_element_type=jnp.float32
    )
    active_gradient = jnp.einsum(
        "anj,yj->any", branch_gradient_full, outermap, preferred_element_type=jnp.float32
    )
    inner_gradient_reduced = gelu_pull(active_gradient)[0].astype(jnp.bfloat16)
    innerbias_part = jnp.sum(inner_gradient_reduced.astype(jnp.float32), axis=(0, 1))
    innermap_part = jnp.einsum(
        "rlh,rlk->hk", normalized_full, inner_gradient_reduced, preferred_element_type=jnp.float32
    )
    dnormed_part = jnp.einsum(
        "ocf,hf->och", inner_gradient_reduced, innermap, preferred_element_type=jnp.float32
    )
    dnormed = dsum_final + lax.psum_scatter(dnormed_part, "heads", scatter_dimension=1, tiled=True)
    normgain_part = jnp.sum(dnormed * first_unit, axis=(0, 1))
    normshift_part = jnp.sum(dnormed, axis=(0, 1))
    dsum_first = layer_norm_back(dnormed, first_unit, first_inverse, normgain.astype(jnp.float32))
    dmerged_low = dsum_first.astype(jnp.bfloat16)
    mergebias_part = jnp.sum(dmerged_low.astype(jnp.float32), axis=(0, 1))
    merged_gradient_full = lax.all_gather(dmerged_low, "heads", axis=1, tiled=True)
    mergemap_part = jnp.einsum(
        "ghw,gha->wa", context_reduced, merged_gradient_full, preferred_element_type=jnp.float32
    )
    dcontext = jnp.einsum(
        "sma,za->smz", merged_gradient_full, mergemap, preferred_element_type=jnp.float32
    ).astype(jnp.bfloat16)
    dcontext_heads = dcontext.reshape(head_shape)
    row_delta = jnp.sum(dcontext_heads.astype(jnp.float32) * context_heads, axis=-1)
    key_portion = lax.all_gather(keyrows, "seq", axis=1, tiled=True)
    value_portion = lax.all_gather(valrows, "seq", axis=1, tiled=True)
    portion_rows = key_portion.shape[1]
    remote_keys = key_portion.reshape(proteins, portion_rows, heads_here, HEAD_DIM)
    remote_values = value_portion.reshape(proteins, portion_rows, heads_here, HEAD_DIM)
    key_live = jnp.arange(portion_rows, dtype=jnp.int32)[None, :] < lengths[:, None]
    prob_low, dscores = score_grads(
        query_heads, remote_keys, remote_values, dcontext_heads, logsum, row_delta, key_live
    )
    dquery = (
        jnp.einsum("bqhk,bkhd->bqhd", dscores, remote_keys, preferred_element_type=jnp.float32)
        * score_scale
    )
    query_gradient_reduced = dquery.reshape(proteins, group_rows, local_width).astype(jnp.bfloat16)
    query_portion = lax.all_gather(queries.astype(jnp.float32), "seq", axis=1, tiled=True).astype(
        jnp.bfloat16
    )
    dcontext_portion = lax.all_gather(
        dcontext.astype(jnp.float32), "seq", axis=1, tiled=True
    ).astype(jnp.bfloat16)
    logsum_portion = lax.all_gather(logsum, "seq", axis=1, tiled=True)
    delta_portion = lax.all_gather(row_delta, "seq", axis=1, tiled=True)
    portion_rows = query_portion.shape[1]
    remote_queries = query_portion.reshape(proteins, portion_rows, heads_here, HEAD_DIM)
    remote_dcontext = dcontext_portion.reshape(proteins, portion_rows, heads_here, HEAD_DIM)
    prob_low, dscores = score_grads(
        remote_queries,
        key_heads,
        value_heads,
        remote_dcontext,
        logsum_portion,
        delta_portion,
        group_live,
    )
    dkey_acc = (
        jnp.einsum("bqhk,bqhd->bkhd", dscores, remote_queries, preferred_element_type=jnp.float32)
        * score_scale
    )
    dvalue_acc = jnp.einsum(
        "bqhk,bqhd->bkhd", prob_low, remote_dcontext, preferred_element_type=jnp.float32
    )
    dkey_rows = dkey_acc.reshape(proteins, group_rows, local_width)
    dvalue_rows = dvalue_acc.reshape(proteins, group_rows, local_width)
    key_gradient_reduced = dkey_rows.astype(jnp.bfloat16)
    value_gradient_reduced = dvalue_rows.astype(jnp.bfloat16)
    querymap_part = jnp.einsum(
        "icg,icr->gr", collected_rows, query_gradient_reduced, preferred_element_type=jnp.float32
    )
    key_weight_slice = jnp.einsum(
        "icg,icr->gr", collected_rows, key_gradient_reduced, preferred_element_type=jnp.float32
    )
    valuemap_part = jnp.einsum(
        "icg,icr->gr", collected_rows, value_gradient_reduced, preferred_element_type=jnp.float32
    )
    querybias_part = jnp.sum(query_gradient_reduced.astype(jnp.float32), axis=(0, 1))
    valuebias_part = jnp.sum(value_gradient_reduced.astype(jnp.float32), axis=(0, 1))
    dtokens_part = (
        jnp.einsum(
            "zov,kv->zok", query_gradient_reduced, querymap, preferred_element_type=jnp.float32
        )
        + jnp.einsum(
            "zov,kv->zok", key_gradient_reduced, keymap, preferred_element_type=jnp.float32
        )
        + jnp.einsum(
            "zov,kv->zok", value_gradient_reduced, valuemap, preferred_element_type=jnp.float32
        )
    )
    tokens_grad = (
        dsum_first + lax.psum_scatter(dtokens_part, "heads", scatter_dimension=1, tiled=True)
    ).astype(jnp.bfloat16)
    summed = lax.psum(
        (
            querymap_part,
            querybias_part,
            key_weight_slice,
            valuemap_part,
            valuebias_part,
            mergemap_part,
            innermap_part,
            innerbias_part,
            outermap_part,
        ),
        ("dp", "seq"),
    )
    norms = lax.psum(
        (
            mergebias_part,
            normgain_part,
            normshift_part,
            outerbias_part,
            finalgain_part,
            finalshift_part,
        ),
        ("dp", "seq", "heads"),
    )
    return (
        layer_output.astype(jnp.bfloat16),
        tokens_grad,
        summed[0],
        summed[1],
        summed[2],
        summed[3],
        summed[4],
        summed[5],
        norms[0],
        norms[1],
        norms[2],
        summed[6],
        summed[7],
        summed[8],
        norms[3],
        norms[4],
        norms[5],
    )


def solution(mesh):
    return jax.shard_map(
        shards,
        mesh=mesh,
        in_specs=(
            P("dp", ("seq", "heads"), None),
            P(None, "heads"),
            P("heads"),
            P(None, "heads"),
            P(None, "heads"),
            P("heads"),
            P("heads", None),
            P(),
            P(),
            P(),
            P(None, "heads"),
            P("heads"),
            P("heads", None),
            P(),
            P(),
            P(),
            P("dp"),
            P("dp", ("seq", "heads"), None),
        ),
        out_specs=(
            P("dp", ("seq", "heads"), None),
            P("dp", ("seq", "heads"), None),
            P(None, "heads"),
            P("heads"),
            P(None, "heads"),
            P(None, "heads"),
            P("heads"),
            P("heads", None),
            P(),
            P(),
            P(),
            P(None, "heads"),
            P("heads"),
            P("heads", None),
            P(),
            P(),
            P(),
        ),
        check_vma=False,
    )
```

profile of v0, /device:TPU:0, one launch (start us, length us, event | category | flops | bytes accessed | tf_op | source)
XLA Modules:
  0.0 893.4 jit_solution(3608307347786612172)
XLA Ops:
  7.3 0.7 all-gather.9.cloned.1.call-update
  8.0 50.3 %all-gather.9.cloned.1.call-done = bf16[4,256,1024]{2,1,0:T(8,128)(2,1)} async-done(((bf16[4,64,1024]{2,1,0:T(8,128)(2,1)}), bf16[4,256,1024]{2,1,0:T(8,128)(2,1)}) %all-gather.9.cloned.1.call-update) | async-done | bytes 2097168 | tf_op jit(solution)/shard_map/all_gather | solution.py:74
  58.3 3.2 convolution_convert_fusion.1
  61.6 3.1 fusion.39
  65.0 2.4 fusion.40
  67.4 15.9 %all-gather.13.cloned.1.call-done = bf16[4,1024,256]{1,2,0:T(8,128)(2,1)} async-done(((bf16[4,256,256]{1,2,0:T(8,128)(2,1)}), bf16[4,1024,256]{1,2,0:T(8,128)(2,1)}) %all-gather.13.cloned.1.call-update) | async-done | bytes 2097168 | tf_op jit(solution)/shard_map/all_gather | solution.py:92
  83.3 5.2 bitcast_reduce_fusion
  88.5 6.2 copy-done.2
  94.7 3.7 fusion.7
  98.4 9.9 %all-gather.11.cloned.1.call-done = bf16[4,1024,256]{1,2,0:T(8,128)(2,1)} async-done(((bf16[4,256,256]{1,2,0:T(8,128)(2,1)}), bf16[4,1024,256]{1,2,0:T(8,128)(2,1)}) %all-gather.11.cloned.1.call-update) | async-done | bytes 2097168 | tf_op jit(solution)/shard_map/all_gather | solution.py:93
  108.3 9.5 %fusion.80 = (bf16[4,256,4,64]{1,3,2,0:T(8,128)(2,1)S(1)}, f32[4,256,4,64]{1,3,2,0:T(8,128)}) fusion(f32[4,256,4]{1,2,0:T(4,128)S(1)} %fusion.7, bf16[4,1024,4,64]{1,3,2,0:T(8,128)(2,1)} %bitcast.206, f32[4,4,1024,256]{3,2,1,0:T(8,128)} %copy-done.2, f32[4,256,4]{1,2,0:T(4,128)S(1)} %broadcast_maximum_fusion, pred[4,1024]{1,0:T(4,128)(4,1)S(1)} %iota_compare_fusion), kind=kOutput, calls=%fused_computation.139 | convolution fusion | flops 554172416 | bytes 20484096 | tf_op jit(solution)/shard_map/bqhk,bkhd->bqhd/dot_general | solution.py:106
  117.8 0.8 copy-done.15
  118.6 2.7 fusion.53
  121.5 76.8 %reduce-scatter.5.cloned.1.call-done = f32[4,64,1024]{2,1,0:T(8,128)} async-done(((f32[4,256,1024]{2,1,0:T(8,128)}), f32[4,64,1024]{2,1,0:T(8,128)}) %reduce-scatter.5.cloned.1.call-update) | async-done | bytes 1048592 | tf_op jit(solution)/shard_map/reduce_scatter | solution.py:117
  198.3 1.6 fusion.79
  200.1 1.1 fusion.51
  201.5 46.3 %all-gather.15.cloned.1.call-done = bf16[4,256,1024]{2,1,0:T(8,128)(2,1)} async-done(((bf16[4,64,1024]{2,1,0:T(8,128)(2,1)}), bf16[4,256,1024]{2,1,0:T(8,128)(2,1)}) %all-gather.15.cloned.1.call-update) | async-done | bytes 2097168 | tf_op jit(solution)/shard_map/all_gather | solution.py:125
  247.8 5.0 fusion.47
  252.9 10.6 %multiply_convert_fusion = (bf16[4,256,1024]{2,1,0:T(8,128)(2,1)S(1)}, f32[4,256,1024]{2,1,0:T(8,128)}) fusion(f32[4,256,1024]{2,1,0:T(8,128)S(1)} %get-tuple-element.75, f32[1024]{0:T(1024)S(1)} %convert_element_type.171, u8[256,1024]{1,0:T(8,128)(4,1)S(1)} %get-tuple-element.35, u8[256,1024]{1,0:T(8,128)(4,1)S(1)} %get-tuple-element.34), kind=kLoop, calls=%fused_computation.31 | loop fusion | flops 74448896 | bytes 11014144 | tf_op jit(solution)/shard_map/convert_element_type | solution.py:134
  263.5 1.4 copy-done.13
  264.9 4.4 fusion.25
  269.3 0.6 copy-done.34
  270.0 74.9 %reduce-scatter.7.cloned.1.call-done = f32[4,64,1024]{2,1,0:T(8,128)} async-done(((f32[4,256,1024]{2,1,0:T(8,128)}), f32[4,64,1024]{2,1,0:T(8,128)}) %reduce-scatter.7.cloned.1.call-update) | async-done | bytes 1048592 | tf_op jit(solution)/shard_map/reduce_scatter | solution.py:136
  344.9 1.7 fusion.77
  347.6 1.2 convert_reduce_fusion.1
  349.3 46.1 %all-gather.17.cloned.1.call-done = bf16[4,256,1024]{2,1,0:T(8,128)(2,1)} async-done(((bf16[4,64,1024]{2,1,0:T(8,128)(2,1)}), bf16[4,256,1024]{2,1,0:T(8,128)(2,1)}) %all-gather.17.cloned.1.call-update) | async-done | bytes 2097168 | tf_op jit(solution)/shard_map/all_gather | solution.py:150
  395.4 8.3 convert_reduce_fusion
  403.8 1.3 copy-done.41
  405.1 4.4 fusion.27
  409.6 0.7 all-gather.21.cloned.1.call-update
  410.3 74.8 %reduce-scatter.9.cloned.1.call-done = f32[4,64,1024]{2,1,0:T(8,128)} async-done(((f32[4,256,1024]{2,1,0:T(8,128)}), f32[4,64,1024]{2,1,0:T(8,128)}) %reduce-scatter.9.cloned.1.call-update) | async-done | bytes 1048592 | tf_op jit(solution)/shard_map/reduce_scatter | solution.py:165
  485.1 3.2 multiply_reduce_fusion.1
  488.3 1.2 convert_reduce_fusion.2
  489.7 5.2 all_gather.39
  494.9 15.8 %all-gather.21.cloned.1.call-done = bf16[4,1024,256]{1,2,0:T(8,128)(2,1)} async-done(((bf16[4,256,256]{1,2,0:T(8,128)(2,1)}), bf16[4,1024,256]{1,2,0:T(8,128)(2,1)}) %all-gather.21.cloned.1.call-update) | async-done | bytes 2097168 | tf_op jit(solution)/shard_map/all_gather | solution.py:194
  510.7 10.1 %fusion.81 = f32[4,4,256,1024]{3,2,1,0:T(8,128)} fusion(bf16[4,256,4,64]{1,3,2,0:T(8,128)(2,1)} %bitcast.200, bf16[4,1024,4,64]{1,3,2,0:T(8,128)(2,1)} %bitcast.192), kind=kOutput, calls=%fused_computation.140 | convolution fusion | flops 536870912 | bytes 19398656 | tf_op jit(solution)/shard_map/bqhd,bkhd->bqhk/dot_general | solution.py:32
  520.9 37.9 %all-gather.19.cloned.1.call-done = bf16[4,256,1024]{2,1,0:T(8,128)(2,1)} async-done(((bf16[4,64,1024]{2,1,0:T(8,128)(2,1)}), bf16[4,256,1024]{2,1,0:T(8,128)(2,1)}) %all-gather.19.cloned.1.call-update) | async-done | bytes 2097168 | tf_op jit(solution)/shard_map/all_gather | solution.py:171
  558.8 3.4 multiply_reduce_fusion.2
  562.3 6.8 convolution_bitcast_fusion.1
  569.1 4.5 convolution_bitcast_fusion
  573.6 5.7 all_gather.41
  579.3 1.7 convolution_bitcast_fusion.2
  581.0 12.1 %convert_reduce_fusion.4 = (f32[4,64]{1,0:T(4,128)S(1)}, bf16[4,4,64,256]{3,2,1,0:T(8,128)(2,1)}) fusion(bf16[4,1024,4,64]{1,3,2,0:T(8,128)(2,1)} %bitcast.191, f32[4,4,1024,256]{3,2,1,0:T(8,128)} %copy-done.2, bf16[4,1024,4,64]{1,3,2,0:T(8,128)(2,1)} %bitcast.207, bf16[4,256,4,64]{1,3,2,0:T(8,128)(2,1)} %bitcast.202, ...), kind=kOutput, calls=%fused_computation.76 | convolution fusion | flops 1099955968 | bytes 22057984 | tf_op jit(solution)/shard_map/bqhk,bkhd->bqhd/dot_general | solution.py:190
  593.1 2.7 convolution_bitcast_fusion.5
  595.8 9.2 %convert_reduce_fusion.3 = (f32[4,64]{1,0:T(4,128)S(1)}, bf16[4,4,64,256]{3,2,1,0:T(8,128)(2,1)}) fusion(bf16[4,1024,4,64]{1,3,2,0:T(8,128)(2,1)} %bitcast.208, f32[4,4,256,1024]{3,2,1,0:T(8,128)} %fusion.81, f32[4,1024,4]{1,2,0:T(4,128)S(1)} %all_gather.39, pred[4,256]{1,0:T(4,128)(4,1)S(1)} %broadcast_compare_fusion), kind=kOutput, calls=%fused_computation.75 | convolution fusion | flops 554434304 | bytes 19466240 | tf_op jit(solution)/shard_map/bqhk,bqhd->bkhd/dot_general | solution.py:218
  605.0 12.1 %fusion.42 = bf16[4,4,64,256]{3,2,1,0:T(8,128)(2,1)} fusion(bf16[4,1024,4,64]{1,3,2,0:T(8,128)(2,1)} %bitcast.193, f32[4,4,256,1024]{3,2,1,0:T(8,128)} %fusion.81, bf16[4,256,4,64]{1,3,2,0:T(8,128)(2,1)} %bitcast.205, bf16[4,1024,4,64]{1,3,2,0:T(8,128)(2,1)} %bitcast.209, f32[4,1024,4]{1,2,0:T(4,128)S(1)} %all_gather.41, f32[4,1024,4]{1,2,0:T(4,128)S(1)} %all_gather.39, ...), kind=kOutput, calls=%fused_computation.70 | convolution fusion | flops 1099431936 | bytes 22152192 | tf_op jit(solution)/shard_map/bqhk,bqhd->bkhd/dot_general | solution.py:215
  617.1 2.7 convolution_bitcast_fusion.4
  619.9 2.7 convolution_bitcast_fusion.3
  622.9 0.7 copy-done.17
  623.8 0.8 fusion.55
  624.8 0.8 fusion.58
  625.6 3.1 add_add_fusion
  628.7 40.6 %all-reduce = (f32[1024]{0:T(1024)}, f32[1024]{0:T(1024)}, f32[1024]{0:T(1024)}, f32[1024]{0:T(1024)}, f32[1024]{0:T(1024)}, /*index=5*/f32[1024]{0:T(1024)}) all-reduce(f32[1024]{0:T(1024)S(1)} %get-tuple-element.61, f32[1024]{0:T(1024)S(1)} %get-tuple-element.36, ...), channel_id=1, replica_groups=mesh['dp'=2,'seq'=4,'heads'=4] {'dp','seq','heads'}, use_global_device_ids=true, to_apply=%region_24.25 | all-reduce | flops 6144 | bytes 49152 | tf_op jit(solution)/shard_map/psum | solution.py:264
  669.4 14.8 %all-reduce.1 = (f32[256]{0:T(256)}, f32[256]{0:T(256)}, f32[1024]{0:T(1024)}) all-reduce(f32[256]{0:T(256)S(1)} %reduce_sum.186, f32[256]{0:T(256)S(1)} %reduce_sum.188, f32[1024]{0:T(1024)S(1)} %get-tuple-element.82), channel_id=1, replica_groups=mesh['dp'=2,'seq'=4,'heads'=4] {'dp','seq'}, use_global_device_ids=true, to_apply=%region_17.18 | all-reduce | flops 1536 | bytes 12288 | tf_op jit(solution)/shard_map/psum | solution.py:250
  684.2 113.4 %all-reduce.5.cloned.1.call-done = (f32[1024,256]{0,1:T(8,128)}, f32[1024,256]{0,1:T(8,128)}, f32[1024,256]{0,1:T(8,128)}, f32[256,1024]{1,0:T(8,128)}, f32[1024,1024]{1,0:T(8,128)}, /*index=5*/f32[1024,1024]{1,0:T(8,128)}) async-done(((f32[1024,256]{0,1:T(8,128)}, f32[1024,256]{0,1:T(8,128)}, f32[1024,256]{0,1:T(8,128)}, f32[256,1024]{1,0:T(8,128)}, f32[1024,1024]{1,0:T(8,128)}, ...) | async-done | bytes 12582928 | tf_op jit(solution)/shard_map/psum | solution.py:250
  797.6 2.5 copy.47
  800.1 2.6 copy.48
  802.7 2.5 copy.49
  805.3 72.1 %reduce-scatter.11.cloned.1.call-done = f32[4,64,1024]{2,1,0:T(8,128)} async-done(((f32[4,256,1024]{2,1,0:T(8,128)}), f32[4,64,1024]{2,1,0:T(8,128)}) %reduce-scatter.11.cloned.1.call-update) | async-done | bytes 1048592 | tf_op jit(solution)/shard_map/reduce_scatter | solution.py:248
  877.4 2.5 add_convert_fusion.1
  879.9 1.0 copy.71
  880.9 2.1 copy.72
  883.1 1.6 copy-done.11
  884.6 2.0 copy.73
  (130 shorter events, 3.8 us)
Async XLA Ops:
  7.2 240.6 %copy-start = (bf16[1024,1024]{1,0:T(8,128)(2,1)S(1)}, bf16[1024,1024]{1,0:T(8,128)(2,1)}, u32[]{:S(2)}) copy-start(bf16[1024,1024]{1,0:T(8,128)(2,1)} %param.28) | copy-start | bytes 6291460
  7.2 54.4 %copy-start.39 = (bf16[256]{0:T(256)(128)(2,1)S(1)}, bf16[256]{0:T(256)(128)(2,1)}, u32[]{:S(2)}) copy-start(bf16[256]{0:T(256)(128)(2,1)} %param.23) | copy-start | bytes 1540
  7.2 54.4 %copy-start.27 = (bf16[1024,256]{1,0:T(8,128)(2,1)S(1)}, bf16[1024,256]{1,0:T(8,128)(2,1)}, u32[]{:S(2)}) copy-start(bf16[1024,256]{1,0:T(8,128)(2,1)} %param.22) | copy-start | bytes 1572868
  7.2 51.1 %all-gather.9.cloned.1.call-start = ((), (), s32[]{:S(2)}) async-start(), calls=%async_computation.4 | async-start | bytes 2621440 | tf_op jit(solution)/shard_map/all_gather | solution.py:74
  8.0 56.9 %copy-start.40 = (bf16[256]{0:T(256)(128)(2,1)S(1)}, bf16[256]{0:T(256)(128)(2,1)}, u32[]{:S(2)}) copy-start(bf16[256]{0:T(256)(128)(2,1)} %param.20) | copy-start | bytes 1540
  8.0 56.9 %copy-start.29 = (s32[4]{0:T(128)S(1)}, s32[4]{0:T(128)}, u32[]{:S(2)}) copy-start(s32[4]{0:T(128)} %param.34) | copy-start | bytes 52
  8.0 57.0 %copy-start.24 = (bf16[1024,256]{1,0:T(8,128)(2,1)S(1)}, bf16[1024,256]{1,0:T(8,128)(2,1)}, u32[]{:S(2)}) copy-start(bf16[1024,256]{1,0:T(8,128)(2,1)} %param.19) | copy-start | bytes 1572868
  8.0 75.3 %all-gather.13.cloned.1.call-start = ((), (), s32[]{:S(2)}) async-start(), calls=%async_computation.6 | async-start | bytes 2621440 | tf_op jit(solution)/shard_map/all_gather | solution.py:92
  61.6 46.7 %all-gather.11.cloned.1.call-start = ((), (), s32[]{:S(2)}) async-start(), calls=%async_computation.5 | async-start | bytes 2621440 | tf_op jit(solution)/shard_map/all_gather | solution.py:93
  64.8 133.5 %reduce-scatter.5.cloned.1.call-start = ((), (), s32[]{:S(2)}) async-start(), calls=%async_computation.7 | async-start | bytes 5242880 | tf_op jit(solution)/shard_map/reduce_scatter | solution.py:117
  67.4 21.1 %copy-start.19 = (bf16[4,256,256]{1,2,0:T(8,128)(2,1)}, bf16[4,256,256]{1,2,0:T(8,128)(2,1)S(1)}, u32[]{:S(2)}) copy-start(bf16[4,256,256]{1,2,0:T(8,128)(2,1)S(1)} %fusion.40) | copy-start | bytes 1572868
  88.5 6.2 copy-start.2
  108.3 10.3 %copy-start.20 = (bf16[256,1024]{1,0:T(8,128)(2,1)S(1)}, bf16[256,1024]{1,0:T(8,128)(2,1)}, u32[]{:S(2)}) copy-start(bf16[256,1024]{1,0:T(8,128)(2,1)} %param.24) | copy-start | bytes 1572868
  117.8 0.8 copy-start.15
  118.6 2.8 copy-start.30
  118.6 2.9 copy-start.31
  118.6 2.9 copy-start.32
  121.3 80.1 %copy-start.33 = (bf16[1024]{0:T(1024)(128)(2,1)S(1)}, bf16[1024]{0:T(1024)(128)(2,1)}, u32[]{:S(2)}) copy-start(bf16[1024]{0:T(1024)(128)(2,1)} %param.29) | copy-start | bytes 6148
  121.3 126.4 %all-gather.15.cloned.1.call-start = ((), (), s32[]{:S(2)}) async-start(), calls=%async_computation.8 | async-start | bytes 2621440 | tf_op jit(solution)/shard_map/all_gather | solution.py:125
  201.2 143.7 %reduce-scatter.7.cloned.1.call-start = ((), (), s32[]{:S(2)}) async-start(), calls=%async_computation.9 | async-start | bytes 5242880 | tf_op jit(solution)/shard_map/reduce_scatter | solution.py:136
  252.8 10.6 %copy-start.10 = (f32[4,256,1024]{2,1,0:T(8,128)}, f32[4,256,1024]{2,1,0:T(8,128)S(1)}, u32[]{:S(2)}) copy-start(f32[4,256,1024]{2,1,0:T(8,128)S(1)} %get-tuple-element.75) | copy-start | bytes 12582916
  252.8 12.0 %copy-start.37 = (bf16[1024,1024]{1,0:T(8,128)(2,1)S(1)}, bf16[1024,1024]{1,0:T(8,128)(2,1)}, u32[]{:S(2)}) copy-start(bf16[1024,1024]{1,0:T(8,128)(2,1)} %param.30) | copy-start | bytes 6291460
  263.5 1.4 copy-start.13
  269.2 0.7 copy-start.34
  269.2 0.7 copy-start.35
  269.3 126.2 %all-gather.17.cloned.1.call-start = ((), (), s32[]{:S(2)}) async-start(), calls=%async_computation.10 | async-start | bytes 2621440 | tf_op jit(solution)/shard_map/all_gather | solution.py:150
  344.9 2.0 copy-start.9
  346.6 1.0 copy-start.3
  348.8 136.3 %reduce-scatter.9.cloned.1.call-start = ((), (), s32[]{:S(2)}) async-start(), calls=%async_computation.11 | async-start | bytes 5242880 | tf_op jit(solution)/shard_map/reduce_scatter | solution.py:165
  403.8 1.3 copy-start.41
  409.5 0.8 copy-start.36
  409.5 75.7 %copy-start.4 = (f32[4,64,1024]{2,1,0:T(8,128)S(1)}, f32[4,64,1024]{2,1,0:T(8,128)}, u32[]{:S(2)}) copy-start(f32[4,64,1024]{2,1,0:T(8,128)} %copy-done.3) | copy-start | bytes 3145732
  409.5 101.2 %all-gather.21.cloned.1.call-start = ((), (), s32[]{:S(2)}) async-start(), calls=%async_computation.13 | async-start | bytes 2621440 | tf_op jit(solution)/shard_map/all_gather | solution.py:194
  410.3 148.5 %all-gather.19.cloned.1.call-start = ((), (), s32[]{:S(2)}) async-start(), calls=%async_computation.12 | async-start | bytes 2621440 | tf_op jit(solution)/shard_map/all_gather | solution.py:171
  488.3 32.6 %copy-start.6 = (f32[4,64,1024]{2,1,0:T(8,128)}, f32[4,64,1024]{2,1,0:T(8,128)S(1)}, u32[]{:S(2)}) copy-start(f32[4,64,1024]{2,1,0:T(8,128)S(1)} %get-tuple-element.63) | copy-start | bytes 3145732
  489.5 106.3 %all-gather.23.cloned.1.call-start = ((), (), s32[]{:S(2)}) async-start(), calls=%async_computation.14 | async-start | bytes 2621440 | tf_op jit(solution)/shard_map/all_gather | solution.py:197
  510.7 48.0 %copy-start.21 = (bf16[256,1024]{1,0:T(8,128)(2,1)S(1)}, bf16[256,1024]{1,0:T(8,128)(2,1)}, u32[]{:S(2)}) copy-start(bf16[256,1024]{1,0:T(8,128)(2,1)} %param.24) | copy-start | bytes 1572868
  562.2 235.4 %all-reduce.5.cloned.1.call-start = ((), (), s32[]{:S(2)}) async-start(), calls=%async_computation.16 | async-start | bytes 25165824 | tf_op jit(solution)/shard_map/psum | solution.py:250
  562.3 6.8 copy-start.14
  562.3 6.8 copy-start.38
  569.1 10.2 %copy-start.8 = (bf16[4,256,1024]{2,1,0:T(8,128)(2,1)S(1)}, bf16[4,256,1024]{2,1,0:T(8,128)(2,1)}, u32[]{:S(2)}) copy-start(bf16[4,256,1024]{2,1,0:T(8,128)(2,1)} %all-gather.19.cloned.1.call-done) | copy-start | bytes 6291460
  569.1 10.2 %copy-start.16 = (bf16[4,256,4,64]{1,3,2,0:T(8,128)(2,1)S(1)}, bf16[4,256,4,64]{1,3,2,0:T(8,128)(2,1)}, u32[]{:S(2)}) copy-start(bf16[4,256,4,64]{1,3,2,0:T(8,128)(2,1)} %copy-done.15) | copy-start | bytes 1572868
  581.0 12.1 %copy-start.5 = (bf16[4,256,1024]{2,1,0:T(8,128)(2,1)S(1)}, bf16[4,256,1024]{2,1,0:T(8,128)(2,1)}, u32[]{:S(2)}) copy-start(bf16[4,256,1024]{2,1,0:T(8,128)(2,1)} %all-gather.9.cloned.1.call-done) | copy-start | bytes 6291460
  622.6 1.0 copy-start.17
  622.6 1.2 copy-start.25
  622.6 1.9 copy-start.18
  622.6 3.0 copy-start.22
  622.6 254.8 %reduce-scatter.11.cloned.1.call-start = ((), (), s32[]{:S(2)}) async-start(), calls=%async_computation.15 | async-start | bytes 5242880 | tf_op jit(solution)/shard_map/reduce_scatter | solution.py:248
  623.8 1.0 copy-start.26
  623.8 1.8 copy-start.28
  628.7 248.7 %copy-start.7 = (f32[4,64,1024]{2,1,0:T(8,128)S(1)}, f32[4,64,1024]{2,1,0:T(8,128)}, u32[]{:S(2)}) copy-start(f32[4,64,1024]{2,1,0:T(8,128)} %copy-done.6) | copy-start | bytes 3145732
  800.1 79.8 %copy-start.23 = (f32[256,1024]{1,0:T(8,128)S(1)}, f32[256,1024]{1,0:T(8,128)}, u32[]{:S(2)}) copy-start(f32[256,1024]{1,0:T(8,128)} %get-tuple-element.93) | copy-start | bytes 3145732
  877.4 3.5 copy-start.12
  880.9 3.7 copy-start.11
  880.9 5.7 copy-start.1
Sparse Core Ops, SparseCore 0:
  9.6 48.6 all-gather.8
  61.7 21.5 all-gather.12
  85.4 22.8 all-gather.10
  121.5 76.7 reduce-scatter.4
  201.3 46.4 all-gather.14
  269.4 75.4 reduce-scatter.6
  349.0 46.4 all-gather.16
  409.6 75.4 reduce-scatter.8
  487.4 23.3 all-gather.20
  512.8 45.9 all-gather.18
  562.3 21.8 all-gather.22
  622.7 174.8 all-reduce.4
  800.4 76.8 reduce-scatter.10
where the time goes:
time: 900 us; the launch traced here: 893 us
  waiting for transfers between devices  636 us (71%)
  matrix products  121 us (13%)
  blocking collectives  66.3 us (7%)
  other arithmetic  28.2 us (3%)
  local copies, waits for them, and re-layouts  26.2 us (3%)
  between operations  14.6 us (2%)
    psum x1, waiting for transfers between devices, shards(): lax.psum((querymap_part, querybias_part, key_weight_slice, valuemap_part,...  113 us
    reduce_scatter x1, waiting for transfers between devices, shards(): lax.psum_scatter(merged_part, 'heads', scatter_dimension=1, tiled=True)  76.8 us
    reduce_scatter x1, waiting for transfers between devices, shards(): lax.psum_scatter(branch_part, 'heads', scatter_dimension=1, tiled=True)  74.9 us
    reduce_scatter x1, waiting for transfers between devices, shards(): lax.psum_scatter(dnormed_part, 'heads', scatter_dimension=1, tiled=True)  74.8 us
    reduce_scatter x1, waiting for transfers between devices, shards(): lax.psum_scatter(dtokens_part, 'heads', scatter_dimension=1, tiled=True)  72.1 us
    all_gather x1, waiting for transfers between devices, shards(): collected_rows = lax.all_gather(tokens, 'heads', axis=1, tiled=True)  50.3 us
    all_gather x1, waiting for transfers between devices, shards(): lax.all_gather(normed.astype(jnp.bfloat16), 'heads', axis=1, tiled=True)  46.3 us
    all_gather x1, waiting for transfers between devices, shards(): lax.all_gather(dbranch_low, 'heads', axis=1, tiled=True)  46.1 us
  transfers between devices with their start and end apart: 13, of which 12 were waited for; matrix products, arithmetic and copies ran while one was open for 8% of the time, Pallas kernels for 0%

commit v1 on v0

v1 whole, which is shorter than its diff:
```python
import functools

import jax
import jax.numpy as jnp
from jax import lax
from jax.experimental import pallas as pl
from jax.experimental.pallas import tpu as pltpu
from jax.sharding import PartitionSpec as P

HEAD_DIM = 64


epsilon = 1e-06
score_scale = 0.125
masked_score = -1000000000.0
low = jnp.bfloat16
wide = jnp.float32
vmem_bytes = 48 * 1024 * 1024


def dot(a, b):
    return jnp.dot(a, b, preferred_element_type=wide)


def dot_nt(a, b):
    return lax.dot_general(a, b, (((1,), (1,)), ((), ())), preferred_element_type=wide)


def dot_tn(a, b):
    return lax.dot_general(a, b, (((0,), (0,)), ((), ())), preferred_element_type=wide)


def swap(value, axis, stride):
    size = lax.axis_size(axis)
    return lax.ppermute(value, axis, [(i, i ^ stride) for i in range(size)])


def after(value, *others):
    return lax.optimization_barrier((value, *others))[0]


def bit_of(bit):
    axis, stride = bit
    return (lax.axis_index(axis) // stride) % 2


def widen(own, other, bit, axis=0):
    upper = bit_of(bit) == 1
    return jnp.concatenate(
        [jnp.where(upper, other, own), jnp.where(upper, own, other)], axis=axis
    )


def halve(value, bit, axis=0):
    half = value.shape[axis] // 2
    at = bit_of(bit) * half
    keep = lax.dynamic_slice_in_dim(value, at, half, axis)
    send = lax.dynamic_slice_in_dim(value, half - at, half, axis)
    return keep, send


def add_low(a, b):
    return (a.astype(wide) + b.astype(wide)).astype(low)


def params(mebibytes):
    return pltpu.CompilerParams(vmem_limit_bytes=mebibytes * 1024 * 1024)


in_vmem = pl.BlockSpec(memory_space=pltpu.VMEM)
in_smem = pl.BlockSpec(memory_space=pltpu.SMEM)


def kernel_call(body, name, arrays, out, flops, scalars=(), scratch=(), mebibytes=16, exps=0):
    size = lambda a: a.size * a.dtype.itemsize
    return pl.pallas_call(
        body,
        in_specs=[in_smem] * len(scalars) + [in_vmem] * len(arrays),
        out_specs=[in_vmem] * len(out),
        out_shape=[jax.ShapeDtypeStruct(*o) for o in out],
        scratch_shapes=list(scratch),
        compiler_params=params(mebibytes),
        cost_estimate=pl.CostEstimate(
            flops=flops, bytes_accessed=sum(size(a) for a in arrays), transcendentals=exps
        ),
        name=name,
    )(*scalars, *arrays)


def place(pos, proteins, groups, share, i, j):
    seq, heads = pos[proteins], pos[proteins + 1]
    return pl.multiple_of(((seq ^ i) * groups + (heads ^ j)) * share, share)


def masked(scores, length, first):
    key_at = first + lax.broadcasted_iota(jnp.int32, scores.shape, 0)
    return jnp.where(key_at < length, scores, masked_score)


def chunks(n, block):
    return [(0, n - block, False)] * (n > block) + [(n - block, n, True)]


def attend_kernel(pieces, groups, pos, *refs):
    q_refs = refs[:groups]
    kv_refs = refs[groups : groups + pieces * groups]
    ctx_refs = refs[groups + pieces * groups : -3]
    ctx_t_ref, lse_ref, kv_all = refs[-3:]
    proteins, share, width = q_refs[0].shape
    total = kv_all.shape[0]
    block = min(256, total)
    heads = range(width // HEAD_DIM)

    def protein(p, carry):
        length = pos[p]
        blocks = (length + block - 1) // block
        for i in range(pieces):
            for j in range(groups):
                at = place(pos, proteins, groups, share, i, j)

                @pl.when(at < blocks * block)
                def _():
                    kv_all[pl.ds(at, share), :] = kv_refs[i * groups + j][p]

        def body(count):
            n = count * block
            queries = jnp.concatenate([ref[p] for ref in q_refs]) * jnp.asarray(score_scale, low)
            cols = lambda h: slice(h * HEAD_DIM, (h + 1) * HEAD_DIM)
            value_cols = lambda h: slice(width + h * HEAD_DIM, width + (h + 1) * HEAD_DIM)
            cuts = chunks(n, block)
            scores = [
                [dot_nt(kv_all[a:b, cols(h)], queries[:, cols(h)]) for a, b, _ in cuts]
                for h in heads
            ]
            weights, denominators = [], []
            for h in heads:
                found = [
                    masked(value, length, a) if last else value
                    for value, (a, _, last) in zip(scores[h], cuts)
                ]
                high = functools.reduce(
                    jnp.maximum, [jnp.max(value, axis=0, keepdims=True) for value in found]
                )
                found = [jnp.exp(value - high) for value in found]
                denominator = sum(jnp.sum(value, axis=0, keepdims=True) for value in found)
                lse_ref[p, h : h + 1, :] = high + jnp.log(denominator)
                weights.append([value.astype(low) for value in found])
                denominators.append(denominator)
            context_t = jnp.concatenate(
                [
                    sum(
                        dot_tn(kv_all[a:b, value_cols(h)], value)
                        for (a, b, _), value in zip(cuts, weights[h])
                    )
                    / denominators[h]
                    for h in heads
                ]
            )
            ctx_t_ref[p] = context_t
            context = context_t.T.astype(low)
            for j, ref in enumerate(ctx_refs):
                ref[p] = context[j * share : (j + 1) * share]

        for count in range(1, total // block + 1):
            pl.when(blocks == count)(functools.partial(body, count))
        return carry

    lax.fori_loop(0, proteins, protein, 0)


def attend_back_kernel(pieces, groups, pos, *refs):
    q_refs, dctx_refs = refs[:groups], refs[groups : 2 * groups]
    ctx_t_ref, lse_ref = refs[2 * groups : 2 * groups + 2]
    refs = refs[2 * groups + 2 :]
    kv_refs, refs = refs[: pieces * groups], refs[pieces * groups :]
    dq_ref, dkv_refs, (kv_all, dkv_all) = refs[0], refs[1:-2], refs[-2:]
    _, share, width = q_refs[0].shape
    rows = groups * share
    proteins = pl.num_programs(0)
    length = pos[pl.program_id(0)]
    total = kv_all.shape[0]
    block = min(256, total)
    blocks = jnp.where(pos[proteins] * rows < length, (length + block - 1) // block, 0)

    @pl.when(blocks == 0)
    def _():
        for ref in (dq_ref, *dkv_refs):
            ref[...] = jnp.zeros(ref.shape, low)

    def body(count):
        n = count * block
        for i in range(pieces):
            for j in range(groups):
                at = place(pos, proteins, groups, share, i, j)
                kv_all[pl.ds(at, share), :] = kv_refs[i * groups + j][0]
        queries = jnp.concatenate([ref[0] for ref in q_refs]) * jnp.asarray(score_scale, low)
        dctx = jnp.concatenate([ref[0] for ref in dctx_refs])
        product = dctx.astype(wide).T * ctx_t_ref[0]
        dq, dk, dv = [], [], []
        for h in range(width // HEAD_DIM):
            cols = slice(h * HEAD_DIM, (h + 1) * HEAD_DIM)
            keys = kv_all[:n, cols]
            values = kv_all[:n, width + h * HEAD_DIM : width + (h + 1) * HEAD_DIM]
            scores = masked(dot_nt(keys, queries[:, cols]), length, 0)
            probs = jnp.exp(scores - lse_ref[0, h : h + 1, :])
            delta = jnp.sum(product[cols, :], axis=0, keepdims=True)
            dprobs = dot_nt(values, dctx[:, cols])
            dscores = (probs * (dprobs - delta)).astype(low)
            dv.append(dot(probs.astype(low), dctx[:, cols]))
            dk.append(dot(dscores, queries[:, cols]))
            dq.append(dot_tn(keys, dscores))
        dkv_all[:n, :width] = jnp.concatenate(dk, axis=1).astype(low)
        dkv_all[:n, width:] = jnp.concatenate(dv, axis=1).astype(low)
        if n < total:
            dkv_all[n:, :] = jnp.zeros((total - n, 2 * width), low)
        dq_all = jnp.concatenate(dq, axis=0).T * score_scale
        dq_ref[...] = dq_all.astype(low).reshape(groups, 1, share, width)
        for i, ref in enumerate(dkv_refs):
            for j in range(groups):
                at = place(pos, proteins, groups, share, i, j)
                ref[j, 0] = dkv_all[pl.ds(at, share), :]

    for count in range(1, total // block + 1):
        pl.when(blocks == count)(functools.partial(body, count))


def rows_spec(*shape):
    return pl.BlockSpec((1, *shape), lambda p, pos: (p, 0, 0))


def attend(pos, queries, kv_pieces):
    groups = len(queries)
    proteins, share, width = queries[0].shape
    rows = groups * share
    total = share * len(kv_pieces)
    found = kernel_call(
        functools.partial(attend_kernel, len(kv_pieces) // groups, groups),
        "attend",
        [*queries, *kv_pieces],
        [(queries[0].shape, low)] * groups
        + [((proteins, width, rows), wide), ((proteins, 8, rows), wide)],
        proteins * rows * total * width * 8,
        scalars=[pos],
        scratch=[pltpu.VMEM((total, 2 * width), low)],
        mebibytes=32,
        exps=proteins * rows * total * (width // HEAD_DIM),
    )
    return found[:groups], found[groups], found[groups + 1]


def attend_back(pos, queries, dctx, ctx_t, lse, kv_pieces):
    groups = len(queries)
    proteins, share, width = queries[0].shape
    rows = groups * share
    total = share * len(kv_pieces)
    spec, pair_spec = rows_spec(share, width), rows_spec(share, 2 * width)
    out_spec = lambda w: pl.BlockSpec((groups, 1, share, w), lambda p, pos: (0, p, 0, 0))
    out = lambda w: jax.ShapeDtypeStruct((groups, proteins, share, w), low)
    pieces = len(kv_pieces) // groups
    found = pl.pallas_call(
        functools.partial(attend_back_kernel, pieces, groups),
        grid_spec=pltpu.PrefetchScalarGridSpec(
            num_scalar_prefetch=1,
            grid=(proteins,),
            in_specs=[spec] * (2 * groups)
            + [rows_spec(width, rows), rows_spec(8, rows)]
            + [pair_spec] * len(kv_pieces),
            out_specs=[out_spec(width)] + [out_spec(2 * width)] * pieces,
            scratch_shapes=[pltpu.VMEM((total, 2 * width), low)] * 2,
        ),
        out_shape=[out(width)] + [out(2 * width)] * pieces,
        compiler_params=params(32),
        cost_estimate=pl.CostEstimate(
            flops=proteins * rows * total * width * 20,
            bytes_accessed=proteins * (rows + total) * width * 10,
            transcendentals=proteins * rows * total * (width // HEAD_DIM),
        ),
        name="attend_back",
    )(pos, *queries, *dctx, ctx_t, lse, *kv_pieces)
    return found[0], found[1:]


def unit_of(values):
    centered = values - jnp.mean(values, axis=-1, keepdims=True)
    variance = jnp.mean(centered * centered, axis=-1, keepdims=True)
    inverse = lax.rsqrt(variance + epsilon)
    return centered * inverse, inverse


def norm_back(grad_rows, unitized, inverse, scales):
    scaled = grad_rows * scales
    grad_mean = jnp.mean(scaled, axis=-1, keepdims=True)
    cross_mean = jnp.mean(scaled * unitized, axis=-1, keepdims=True)
    return inverse * (scaled - grad_mean - unitized * cross_mean)


def steps(rows):
    size = 64 if rows % 64 == 0 else rows
    return [slice(at, at + size) for at in range(0, rows, size)]


def merge_kernel(groups, parts, slot, *refs):
    ctx_refs, refs = refs[:groups], refs[groups:]
    own_map, refs = refs[0], refs[1:]
    part_refs, refs = refs[: len(parts)], refs[len(parts) :]
    tok_ref, bias_ref, gain_ref, shift_ref = refs[:4]
    normed_ref, low_ref, unit_ref, inv_ref, maps_ref, by_slot = refs[4:]
    others = groups - 1
    for masks, ref in zip(parts, part_refs):
        for k, mask in enumerate(masks):
            for j in range(others):
                by_slot[j, slot[0] ^ mask] = ref[k * others + j]
    for j in range(others):
        maps_ref[j] = by_slot[j].reshape(own_map.shape)
    merged = bias_ref[...].astype(wide) + dot(ctx_refs[0][...], own_map[...])
    for j in range(others):
        merged += dot(ctx_refs[j + 1][...], maps_ref[j])
    unit_ref[...] = tok_ref[...].astype(wide) + merged
    for rows in steps(tok_ref.shape[0]):
        unit, inverse = unit_of(unit_ref[rows, :])
        normed = unit * gain_ref[...].astype(wide) + shift_ref[...].astype(wide)
        normed_ref[rows, :] = normed
        low_ref[rows, :] = normed.astype(low)
        unit_ref[rows, :] = unit
        inv_ref[rows, :] = jnp.broadcast_to(inverse, (inverse.shape[0], 128))


def merge_norm(slot, ctx, own_map, parts, masks, tok, bias, gain, shift):
    rows, model = tok.shape
    groups = len(ctx)
    return kernel_call(
        functools.partial(merge_kernel, groups, masks),
        "merge_norm",
        [*ctx, own_map, *parts, tok, bias, gain, shift],
        [
            ((rows, model), wide),
            ((rows, model), low),
            ((rows, model), wide),
            ((rows, 128), wide),
            ((groups - 1, *own_map.shape), low),
        ],
        2 * rows * model * model,
        scalars=[slot],
        scratch=[pltpu.VMEM((groups - 1, 2 * parts[0].shape[0] // (groups - 1), *parts[0].shape[1:]), low)],
    )


def final_kernel(*refs):
    (normed_ref, near_ref, core_ref, far_ref, bias_ref, gain_ref, shift_ref, cot_ref, live_ref) = refs[:9]
    out_ref, dsum_ref, dbranch_ref, sums_ref = refs[9:]
    gain = gain_ref[...].astype(wide)
    gain_sum = shift_sum = bias_sum = 0.0
    for rows in steps(normed_ref.shape[0]):
        branch = near_ref[rows, :].astype(wide) + core_ref[rows, :].astype(wide)
        branch = branch + far_ref[rows, :].astype(wide) + bias_ref[...].astype(wide)
        unit, inverse = unit_of(normed_ref[rows, :] + branch)
        out_ref[rows, :] = (unit * gain + shift_ref[...].astype(wide)).astype(low)
        grad = cot_ref[rows, :].astype(wide) * live_ref[rows, 0:1]
        dsum = norm_back(grad, unit, inverse, gain)
        dsum_ref[rows, :] = dsum
        dbranch = dsum.astype(low)
        dbranch_ref[rows, :] = dbranch
        gain_sum += jnp.sum(grad * unit, axis=0, keepdims=True)
        shift_sum += jnp.sum(grad, axis=0, keepdims=True)
        bias_sum += jnp.sum(dbranch.astype(wide), axis=0, keepdims=True)
    sums_ref[...] = jnp.zeros(sums_ref.shape, wide)
    sums_ref[0:1, :] = bias_sum
    sums_ref[1:2, :] = gain_sum
    sums_ref[2:3, :] = shift_sum


def final_norm(normed, near, core, far, bias, gain, shift, cot, live):
    rows, model = normed.shape
    return kernel_call(
        final_kernel,
        "final_norm",
        [normed, near, core, far, bias, gain, shift, cot, live],
        [((rows, model), low), ((rows, model), wide), ((rows, model), low), ((8, model), wide)],
        40 * rows * model,
    )


def first_back_kernel(groups, *refs):
    (dsum_ref, near_ref, core_ref, far_ref, unit_ref, inv_ref, gain_ref, own_map, maps_ref) = refs[:9]
    dfirst_ref, dmerged_ref, sums_ref = refs[9:12]
    dctx_refs = refs[12:]
    gain = gain_ref[...].astype(wide)
    gain_sum = shift_sum = bias_sum = 0.0
    for rows in steps(dsum_ref.shape[0]):
        grad = near_ref[rows, :].astype(wide) + core_ref[rows, :].astype(wide)
        grad = dsum_ref[rows, :] + grad + far_ref[rows, :].astype(wide)
        unit = unit_ref[rows, :]
        dfirst = norm_back(grad, unit, inv_ref[rows, 0:1], gain)
        dfirst_ref[rows, :] = dfirst
        dmerged = dfirst.astype(low)
        dmerged_ref[rows, :] = dmerged
        gain_sum += jnp.sum(grad * unit, axis=0, keepdims=True)
        shift_sum += jnp.sum(grad, axis=0, keepdims=True)
        bias_sum += jnp.sum(dmerged.astype(wide), axis=0, keepdims=True)
    for j in range(groups):
        merge_map = maps_ref[j - 1] if j else own_map[...]
        dctx_refs[j][...] = dot_nt(dmerged_ref[...], merge_map).astype(low)
    sums_ref[...] = jnp.zeros(sums_ref.shape, wide)
    sums_ref[3:4, :] = bias_sum
    sums_ref[4:5, :] = gain_sum
    sums_ref[5:6, :] = shift_sum


def first_back(dsum, near, core, far, unit, inverse, gain, own_map, maps):
    rows, model = dsum.shape
    groups, width = maps.shape[0] + 1, own_map.shape[0]
    found = kernel_call(
        functools.partial(first_back_kernel, groups),
        "first_back",
        [dsum, near, core, far, unit, inverse, gain, own_map, maps],
        [((rows, model), wide), ((rows, model), low), ((8, model), wide)]
        + [((rows, width), low)] * groups,
        2 * rows * model * model,
    )
    return found[0], found[1], found[2], found[3:]


def forward_kernel(a_ref, b_ref, inner_ref, outer_ref, bias_ref, act_ref, slope_ref, own_ref, other_ref):
    rows = a_ref.shape[0]
    for ref, out, at in ((a_ref, own_ref, 0), (b_ref, other_ref, rows)):
        pre = dot_nt(ref[...], inner_ref[...]) + bias_ref[...]
        upper = 0.5 + 0.5 * lax.erf(pre * 0.7071067811865476)
        active = (pre * upper).astype(low)
        slope = upper + pre * (0.3989422804014327 * jnp.exp(-0.5 * pre * pre))
        act_ref[at : at + rows, :] = active
        slope_ref[at : at + rows, :] = slope.astype(low)
        out[...] = dot(active, outer_ref[...]).astype(low)


def feed_forward(a, b, inner, outer, bias):
    rows, model = a.shape
    hidden = inner.shape[0]
    return kernel_call(
        forward_kernel,
        "feed_forward",
        [a, b, inner, outer, bias],
        [((2 * rows, hidden), low)] * 2 + [((rows, model), low)] * 2,
        8 * rows * model * hidden,
        exps=4 * rows * hidden,
    )


def backward_kernel(a_ref, b_ref, inner_ref, outer_ref, slope_ref, dinner_ref, own_ref, other_ref):
    rows = a_ref.shape[0]
    for ref, out, at in ((a_ref, own_ref, 0), (b_ref, other_ref, rows)):
        dactive = dot_nt(ref[...], outer_ref[...])
        dinner = (dactive * slope_ref[at : at + rows, :].astype(wide)).astype(low)
        dinner_ref[at : at + rows, :] = dinner
        out[...] = dot(dinner, inner_ref[...]).astype(low)


def feed_backward(a, b, inner, outer, slope):
    rows, model = a.shape
    hidden = inner.shape[0]
    return kernel_call(
        backward_kernel,
        "feed_backward",
        [a, b, inner, outer, slope],
        [((2 * rows, hidden), low)] + [((rows, model), low)] * 2,
        8 * rows * model * hidden,
    )


def grad_kernel(numbers, block, bias, *refs):
    hid, row_refs, out_ref = refs[:2], refs[2:-1], refs[-1]
    model = out_ref.shape[-1]
    for k, number in enumerate(numbers):
        cols = slice(number * block, (number + 1) * block)
        total = sums = 0.0
        for i, ref in enumerate(hid):
            half = ref.shape[0] // 2
            total += dot_tn(ref[:half, cols], row_refs[2 * i][...])
            total += dot_tn(ref[half:, cols], row_refs[2 * i + 1][...])
            if bias:
                sums += jnp.sum(ref[:, cols].astype(wide), axis=0, keepdims=True)
        out_ref[k, :block, :] = total.astype(low)
        if bias:
            out_ref[k, block:, :] = jnp.pad(sums, ((0, 15), (0, model - block))).astype(low)


def weight_grad(hid, row_list, block, numbers, bias):
    rows, model = row_list[0].shape
    return kernel_call(
        functools.partial(grad_kernel, numbers, block, bias),
        "weight_grad",
        [*hid, *row_list],
        [((len(numbers), block + 16 * bias, model), low)],
        8 * rows * model * len(numbers) * block,
    )[0]


def units_kernel(units, shares, slot, inner_ref, outer_ref, bias_ref, own_inner, own_outer, own_bias):
    for m in range(shares):
        at = pl.multiple_of((slot[0] ^ (m << 1)) * units, units)
        own_inner[m] = inner_ref[:, pl.ds(at, units)].T
        own_outer[m] = outer_ref[pl.ds(at, units), :]
        own_bias[m] = jnp.broadcast_to(bias_ref[:, pl.ds(at, units)], (16, units))


def own_units(slot, shares, innermap, outermap, innerbias):
    model = innermap.shape[0]
    units = innermap.shape[1] // (2 * shares)
    if units % 128:
        found = []
        for m in range(shares):
            at = (slot[0] ^ (m << 1)) * units
            inner = lax.dynamic_slice_in_dim(innermap, at, units, 1).T
            outer = lax.dynamic_slice_in_dim(outermap, at, units, 0)
            bias = lax.dynamic_slice_in_dim(innerbias, at, units, 1)
            found.append((inner, outer, jnp.broadcast_to(bias, (16, units))))
        return [jnp.stack(pieces) for pieces in zip(*found)]
    return kernel_call(
        functools.partial(units_kernel, units, shares),
        "own_units",
        [innermap, outermap, innerbias],
        [((shares, units, model), low)] * 2 + [((shares, 16, units), innerbias.dtype)],
        shares * units * model,
        scalars=[slot],
    )


def join_kernel(units, count, *refs):
    own_inner, own_outer, own_bias = refs[:3]
    inner_parts, outer_parts = refs[3 : 3 + count], refs[3 + count : -3]
    inner_ref, outer_ref, bias_ref = refs[-3:]
    at = 0
    for ref in inner_parts:
        for k in range(ref.shape[0]):
            m = at // (2 * units)
            far = at + units
            inner_ref[at:far, :] = own_inner[m]
            inner_ref[far : far + units, :] = ref[k, :units, :]
            bias_ref[:, at:far] = own_bias[m, 0:1, :].astype(wide)
            bias_ref[:, far : far + units] = ref[k, units : units + 1, :units].astype(wide)
            at += 2 * units
    at = 0
    for ref in outer_parts:
        for k in range(ref.shape[0]):
            m = at // (2 * units)
            outer_ref[at : at + units, :] = own_outer[m]
            outer_ref[at + units : at + 2 * units, :] = ref[k]
            at += 2 * units


def join_units(own, inner_parts, outer_parts):
    own_inner, own_outer, own_bias = own
    shares, units, model = own_inner.shape
    hidden = 2 * shares * units
    return kernel_call(
        functools.partial(join_kernel, units, len(inner_parts)),
        "join_units",
        [*own, *inner_parts, *outer_parts],
        [((hidden, model), low)] * 2 + [((1, hidden), wide)],
        hidden * model,
    )


def slot_order(number, bits):
    return ((number & 1) << (bits - 1)) | (number >> 1)


def qkv_kernel(counts, slots, slot, *refs):
    out_ref, q_all, kv_all = refs[-3:]
    dq_ref, refs = refs[0], refs[1:-3]
    width, model = dq_ref.shape[-1], out_ref.shape[-1]
    q_all[...] = dq_ref[...].reshape(q_all.shape)
    q_sum = jnp.sum(q_all[...].astype(wide), axis=0, keepdims=True)
    q_grad = kv_grad = kv_sum = 0.0
    for i, count in enumerate(counts):
        dkv_ref, tok_refs, refs = refs[0], refs[1 : 1 + count], refs[1 + count :]
        kv_all[...] = dkv_ref[...].reshape(kv_all.shape)
        kv_sum += jnp.sum(kv_all[...].astype(wide), axis=0, keepdims=True)
        at = 0
        for tok_ref in tok_refs:
            there = slice(at, at + tok_ref.shape[0])
            at += tok_ref.shape[0]
            kv_grad += dot_tn(kv_all[there, :], tok_ref[...])
            if i == 0:
                q_grad += dot_tn(q_all[there, :], tok_ref[...])
    grad = jnp.concatenate([q_grad, kv_grad]).astype(low)
    sums = jnp.concatenate([q_sum, kv_sum], axis=1)
    bits = slots.bit_length() - 1
    block = 3 * width // slots
    for b in range(slots):
        at = slot_order(slot[0] ^ b, bits)
        out_ref[at, :block, :] = grad[b * block : (b + 1) * block]
        line = jnp.pad(sums[:, b * block : (b + 1) * block], ((0, 15), (0, model - block)))
        out_ref[at, block : block + 16, :] = line.astype(low)


def qkv_grads(slot, slots, dq, pairs):
    model = pairs[0][1][0].shape[-1]
    groups, width = dq.shape[0], dq.shape[-1]
    total = dq.size // width
    return kernel_call(
        functools.partial(qkv_kernel, [len(tok) for _, tok in pairs], slots),
        "qkv_grads",
        [dq] + [a for dkv, tok in pairs for a in (dkv, *tok)],
        [((slots, 3 * width // slots + 16, model), low)],
        10 * total * model * width,
        scalars=[slot],
        scratch=[pltpu.VMEM((total, width), low), pltpu.VMEM((total, 2 * width), low)],
        mebibytes=24,
    )[0]


def feed_out_kernel(units, grads_ref, inner_ref, outer_ref):
    slots = grads_ref.shape[0]
    for k in range(slots):
        cols = slice(k * units, (k + 1) * units)
        inner_ref[:, cols] = grads_ref[k, :units, :].astype(wide).T
        outer_ref[cols, :] = grads_ref[k, units : 2 * units, :].astype(wide)


def feed_out(grads, units):
    slots, _, model = grads.shape
    hidden = slots * units
    return kernel_call(
        functools.partial(feed_out_kernel, units),
        "feed_out",
        [grads],
        [((model, hidden), wide), ((hidden, model), wide)],
        slots * units * model,
        mebibytes=40,
    )


def qkv_out_kernel(block, order, slot, *refs):
    parts, refs = refs[: len(order)], refs[len(order) :]
    q_ref, k_ref, v_ref, merge_ref, bias_ref, rows_all, merge_all = refs
    width = q_ref.shape[1]
    for masks, part in zip(order, parts):
        for k, mask in enumerate(masks):
            at = slot[0] ^ mask
            rows_all[at] = part[k, :block, :]
            bias_ref[pl.ds(at, 1), :] = part[k, block : block + 1, :].astype(wide)
            merge_all[at] = part[k, block + 16 :, :]
    grad = rows_all[...].reshape(3 * width, -1)
    for i, ref in enumerate((q_ref, k_ref, v_ref)):
        ref[...] = grad[i * width : (i + 1) * width].astype(wide).T
    merge_ref[...] = merge_all[...].reshape(merge_ref.shape).astype(wide)


def qkv_out(slot, parts, order, block, width):
    model = parts[0].shape[-1]
    slots = 3 * width // block
    size = width // slots
    return kernel_call(
        functools.partial(qkv_out_kernel, block, order),
        "qkv_out",
        parts,
        [((model, width), wide)] * 3 + [((width, model), wide), ((slots, model), wide)],
        3 * width * model,
        scalars=[slot],
        scratch=[pltpu.VMEM((slots, block, model), low), pltpu.VMEM((slots, size, model), low)],
    )


def shards(
    tokens,
    querymap,
    querybias,
    keymap,
    valuemap,
    valuebias,
    mergemap,
    mergebias,
    normgain,
    normshift,
    innermap,
    innerbias,
    outermap,
    outerbias,
    finalgain,
    finalshift,
    lengths,
    cotangent,
):
    proteins, share, model = tokens.shape
    groups = lax.axis_size("heads")
    rows = proteins * share
    width = querymap.shape[1]
    seq, heads = lax.axis_index("seq"), lax.axis_index("heads")
    seq_size, dp_size = lax.axis_size("seq"), lax.axis_size("dp")
    pos = jnp.concatenate([lengths, jnp.stack([seq, heads]).astype(jnp.int32)])
    core_bit, row_bit, far_bit = ("seq", 1), ("heads", 1), ("heads", 2)
    seq_bits = [("seq", 1 << k) for k in range(1, seq_size.bit_length() - 1)]
    share_bits = seq_bits + [("dp", 1 << k) for k in range(dp_size.bit_length() - 1)]
    slot_bits = [core_bit] + share_bits
    slots = 1 << len(slot_bits)
    shares = slots // 2
    slot = lax.axis_index("dp") * seq_size + seq
    units = innermap.shape[1] // slots
    merge_units = width // slots
    row = lambda vector: vector.reshape(1, -1)

    slot_scalar = slot.reshape(1).astype(jnp.int32)

    own_rows = tokens.reshape(rows, model)
    second = swap(own_rows, *far_bit)
    first = swap(own_rows, *row_bit)
    kv_map = jnp.concatenate([keymap, valuemap], axis=1)
    kv_bias = jnp.concatenate([jnp.zeros_like(valuebias), valuebias]).astype(wide)

    def keys_values(piece):
        return (dot(piece, kv_map) + kv_bias).astype(low).reshape(proteins, share, 2 * width)

    def query_rows(piece):
        found = (dot(piece, querymap) + querybias.astype(wide)).astype(low)
        return found.reshape(proteins, share, width)

    kv_own, q_own = keys_values(own_rows), query_rows(own_rows)
    merge_own = lax.dynamic_slice_in_dim(mergemap, slot * merge_units, merge_units, 0)
    merge_first = swap(merge_own, *row_bit)
    own = own_units(slot_scalar, shares, innermap, outermap, row(innerbias))
    inner_pack = jnp.concatenate([own[0][0], jnp.pad(own[2][0], ((0, 0), (0, model - units)))])
    third = swap(after(second, inner_pack, q_own), *row_bit)
    kv_first, kv_second = keys_values(first), keys_values(second)
    q_first, q_second = query_rows(first), query_rows(second)
    merge_far = swap(after(jnp.stack([merge_own, merge_first]), kv_second), *far_bit)
    inner_pack = swap(after(inner_pack, kv_second), *far_bit)
    kv_third, q_third = keys_values(third), query_rows(third)
    outer_pack = swap(after(own[1][0], kv_third), *far_bit)
    token_pieces = [own_rows, first, second, third]
    queries = [q_own, q_first, q_second, q_third]
    kv_by_seq = {0: [kv_own, kv_first, kv_second, kv_third]}
    for axis, stride in seq_bits + [core_bit]:
        for i in list(kv_by_seq):
            kv_by_seq[i | stride] = [swap(piece, axis, stride) for piece in kv_by_seq[i]]
    kv_pieces = [piece for i in range(seq_size) for piece in kv_by_seq[i]]

    merge_parts = jnp.concatenate([merge_first[None], merge_far])
    merge_masks = [0]
    for k in reversed(range(1, len(slot_bits))):
        merge_parts = after(merge_parts, kv_third)
        merge_parts = jnp.concatenate([merge_parts, swap(merge_parts, *slot_bits[k])])
        merge_masks = merge_masks + [mask | (1 << k) for mask in merge_masks]
    inner_parts = [inner_pack[None]]
    for k, bit in enumerate(share_bits):
        if k:
            inner_parts = [after(jnp.concatenate(inner_parts), context[0])]
        inner_parts.append(swap(after(inner_parts[0], kv_third), *bit))
        if not k:
            context, context_t, logsum = attend(
                pos, after(queries, inner_parts[0]), kv_pieces
            )
    outer_parts, outer_order = after(outer_pack, context[0])[None], [0]
    for k in reversed(range(len(share_bits))):
        outer_parts = jnp.concatenate([outer_parts, swap(outer_parts, *share_bits[k])])
        outer_order = outer_order + [m | (1 << k) for m in outer_order]
    outer_parts = [outer_parts[outer_order.index(m)][None] for m in range(shares)]

    merge_core = swap(after(merge_parts, context[0]), *core_bit)
    context = [c.reshape(rows, width) for c in context]
    context = [context[0]] + [swap(context[j], "heads", j) for j in range(1, groups)]
    normed, normed_low, first_unit, first_inverse, other_maps = merge_norm(
        slot_scalar,
        context,
        mergemap,
        [merge_parts, merge_core],
        [merge_masks, [mask | 1 for mask in merge_masks]],
        own_rows,
        row(mergebias),
        row(normgain),
        row(normshift),
    )
    inner_t, outer_w, inner_b = join_units(own, inner_parts, after(outer_parts, normed_low))

    def gather_rows(own):
        across = swap(own, *row_bit)
        near = swap(own, *core_bit)
        return own, near, across, swap(across, *core_bit)

    normed_rows = gather_rows(normed_low)
    near_act, near_slope, near_own, near_other = feed_forward(
        normed_rows[0], normed_rows[1], inner_t, outer_w, inner_b
    )
    far_act, far_slope, far_own, far_other = feed_forward(
        after(normed_rows[2], near_act), normed_rows[3], inner_t, outer_w, inner_b
    )
    far_sum = swap(add_low(far_own, swap(far_other, *core_bit)), *row_bit)
    seq_tokens = {0: [jnp.concatenate(token_pieces[:2]), jnp.concatenate(token_pieces[2:])]}
    seq_tokens[0] = after(seq_tokens[0], near_act)
    for axis, stride in seq_bits:
        for i in list(seq_tokens):
            one = swap(seq_tokens[i][0], axis, stride)
            two = swap(after(seq_tokens[i][1], one), axis, stride)
            seq_tokens[i | stride] = [one, two]
    own_at = (seq * groups + heads) * share + jnp.arange(share, dtype=jnp.int32)
    live = (own_at[None, :] < lengths[:, None]).astype(wide).reshape(rows, 1)
    layer_output, dsum_final, dbranch, final_sums = final_norm(
        normed,
        near_own,
        swap(near_other, *core_bit),
        after(far_sum, seq_tokens[seq_bits[0][1]][0]),
        row(outerbias),
        row(finalgain),
        row(finalshift),
        cotangent.reshape(rows, model),
        jnp.broadcast_to(live, (rows, 128)),
    )
    dbranch_rows = gather_rows(dbranch)
    near_dinner, near_own, near_other = feed_backward(
        dbranch_rows[0], dbranch_rows[1], inner_t, outer_w, near_slope
    )
    far_dinner, far_own, far_other = feed_backward(
        after(dbranch_rows[2], near_dinner), dbranch_rows[3], inner_t, outer_w, far_slope
    )
    far_part = add_low(far_own, swap(far_other, *core_bit))
    far_sum = swap(far_part, *row_bit)

    hid_block = 2 * units
    last = len(share_bits) - 1
    numbers = lambda k, side: [m for m in range(shares) if (m >> k) & 1 == side]
    near_far = [near_act, far_act], [near_dinner, far_dinner]
    outer_send = weight_grad(
        near_far[0], after(dbranch_rows, far_part), hid_block, numbers(last, 1), 0
    )
    outer_got = swap(outer_send, *share_bits[last])
    inner_send = weight_grad(
        near_far[1], after(normed_rows, outer_send), hid_block, numbers(0, 1), 1
    )
    inner_got = swap(inner_send, *share_bits[0])
    outer_keep = weight_grad(
        near_far[0], after(dbranch_rows, inner_send), hid_block, numbers(last, 0), 0
    )
    inner_keep = weight_grad(
        near_far[1], after(normed_rows, outer_keep), hid_block, numbers(0, 0), 1
    )

    dfirst, dmerged, first_sums, dcontext = first_back(
        dsum_final,
        near_own,
        swap(near_other, *core_bit),
        after(far_sum, inner_keep),
        first_unit,
        first_inverse,
        row(normgain),
        mergemap,
        other_maps,
    )
    dcontext = [dcontext[0]] + [swap(dcontext[j], "heads", j) for j in range(1, groups)]
    dcontext = [d.reshape(proteins, share, width) for d in dcontext]

    def shared_sum(keep, got, k):
        value = add_low(keep, got)
        for bit in reversed([b for i, b in enumerate(share_bits) if i != k]):
            half = value.shape[0] // 2
            send, value = value[half:], value[:half]
            value = add_low(value, after(swap(send, *bit), dqueries) if half == 1 else swap(send, *bit))
        return value[0]

    merge_sum = jnp.stack([dot_tn(piece, dmerged) for piece in context]).astype(low)
    extra = jnp.concatenate([final_sums + first_sums, jnp.zeros((8, model), wide)])

    def merge_step(merge_sum, extra, bit, wait):
        keep, send = halve(merge_sum, bit, 1)
        size = send.shape[1]
        block = jnp.concatenate([send.reshape(-1, model), extra.astype(low)])
        block = after(swap(block, *bit), wait)
        extra = extra + block[groups * size :].astype(wide)
        return add_low(keep, block[: groups * size].reshape(keep.shape)), extra

    dqueries, dkv_by_seq = attend_back(pos, queries, dcontext, context_t, logsum, kv_pieces)
    dkv_parts = [
        add_low(dkv_by_seq[i], swap(dkv_by_seq[i + 1], *core_bit)) for i in range(0, seq_size, 2)
    ]
    far_first = dkv_parts[1]
    half = groups // 2
    dkv_halves = []
    for at in (half, 0):
        parts = [part[at : at + half] for part in dkv_parts]
        for k in reversed(range(len(seq_bits))):
            count = 1 << k
            got = [swap(parts[count + i], *seq_bits[k]) for i in range(count)]
            parts = [add_low(parts[i], got[i]) for i in range(count)]
        dkv_halves.append(parts[0].reshape(half, rows, 2 * width))

    outer_sum = shared_sum(outer_keep, after(outer_got, dmerged), last)
    inner_sum = shared_sum(inner_keep, after(inner_got, dmerged), 0)
    pack = jnp.concatenate([inner_sum[units:], outer_sum[units:]])
    block = swap(after(pack, far_first), *far_bit)

    pairs = [(dkv_parts[0], token_pieces)] + [
        (dkv_parts[i], seq_tokens[2 * i]) for i in range(1, seq_size // 2)
    ]
    slot_grads = qkv_grads(slot_scalar, slots, after(dqueries, pack), pairs)
    block = after(block, slot_grads)
    pack = jnp.concatenate(
        [
            add_low(inner_sum[:units], block[:units]),
            add_low(outer_sum[:units], block[units + 16 :]),
            jnp.pad(
                add_low(inner_sum[2 * units :, :units], block[units : units + 16, units : 2 * units]),
                ((0, 0), (0, model - units)),
            ),
        ]
    )
    grads = lax.all_gather(pack, ("dp", "seq"))
    dkv = [dkv_halves[1][0], dkv_halves[1][1], dkv_halves[0][0], dkv_halves[0][1]]
    dqs = dqueries.reshape(groups, rows, width)
    parts = [dot_nt(dqs[j], querymap) + dot_nt(dkv[j], kv_map) for j in range(groups)]
    rest = swap(parts[3].astype(low), *row_bit)
    near = swap(parts[1].astype(low), *row_bit)
    far = swap((parts[2] + rest.astype(wide)).astype(low), *far_bit)
    tokens_grad = (dfirst + parts[0] + near.astype(wide) + far.astype(wide)).astype(low)
    innermap_grad, outermap_grad = feed_out(grads, units)
    innerbias_grad = grads[:, 2 * units, :units].reshape(-1).astype(wide)

    for k, bit in reversed(list(enumerate(share_bits + [core_bit]))):
        half = 1 << k
        slot_grads = add_low(slot_grads[:half], swap(slot_grads[half:], *bit))
    waits = [dqueries, far_first] + [slot_grads] * len(slot_bits)
    for bit, wait in zip(reversed(slot_bits), waits):
        merge_sum, extra = merge_step(merge_sum, extra, bit, wait)
    block = jnp.concatenate([merge_sum[1], merge_sum[3], extra.astype(low)])
    block = swap(block, *row_bit)
    extra = extra + block[2 * merge_units :].astype(wide)
    merge_near = add_low(merge_sum[0], block[:merge_units])
    merge_far = add_low(merge_sum[2], block[merge_units : 2 * merge_units])
    block = swap(jnp.concatenate([merge_far, extra.astype(low)]), *far_bit)
    extra = extra + block[merge_units:].astype(wide)
    merge_near = add_low(merge_near, block[:merge_units])
    out_pack = jnp.concatenate([slot_grads[0], merge_near])[None]
    parts, order = [out_pack], [[0]]
    for k in range(1, len(slot_bits)):
        parts = [jnp.concatenate(parts)] if len(parts) > 1 else parts
        order = [sum(order, [])]
        parts = parts + [swap(parts[0], *slot_bits[k])]
        order = order + [[mask | (1 << k) for mask in order[0]]]
    core_parts = [swap(part, *core_bit) for part in parts]
    core_order = [[mask | 1 for mask in masks] for masks in order]
    q_grad, k_grad, v_grad, mergemap_grad, bias_rows = qkv_out(
        slot_scalar, parts + core_parts, order + core_order, 3 * width // slots, width
    )
    bias_grads = bias_rows[:, : 3 * width // slots].reshape(-1)
    shape = tokens.shape
    return (
        layer_output.reshape(shape),
        tokens_grad.reshape(shape),
        q_grad,
        bias_grads[:width],
        k_grad,
        v_grad,
        bias_grads[2 * width :],
        mergemap_grad,
        extra[3],
        extra[4],
        extra[5],
        innermap_grad,
        innerbias_grad,
        outermap_grad,
        extra[0],
        extra[1],
        extra[2],
    )


def solution(mesh):
    return jax.shard_map(
        shards,
        mesh=mesh,
        in_specs=(
            P("dp", ("seq", "heads"), None),
            P(None, "heads"),
            P("heads"),
            P(None, "heads"),
            P(None, "heads"),
            P("heads"),
            P("heads", None),
            P(),
            P(),
            P(),
            P(None, "heads"),
            P("heads"),
            P("heads", None),
            P(),
            P(),
            P(),
            P("dp"),
            P("dp", ("seq", "heads"), None),
        ),
        out_specs=(
            P("dp", ("seq", "heads"), None),
            P("dp", ("seq", "heads"), None),
            P(None, "heads"),
            P("heads"),
            P(None, "heads"),
            P(None, "heads"),
            P("heads"),
            P("heads", None),
            P(),
            P(),
            P(),
            P(None, "heads"),
            P("heads"),
            P("heads", None),
            P(),
            P(),
            P(),
        ),
        check_vma=False,
    )
```

time: 900 us -> 445 us (0.49)
  waiting for transfers between devices: 636 us -> 229 us
  matrix products: 121 us -> 9.56 us
  starting transfers between devices: 1.36 us -> 70.9 us
  blocking collectives: 66.3 us -> 0 us
  Pallas kernels: 0 us -> 55.5 us
  local copies, waits for them, and re-layouts: 26.2 us -> 38.3 us
  other arithmetic: 28.2 us -> 17.9 us
    reduce_scatter x4 -> x0, waiting for transfers between devices: 299 us -> none  [the longest x1 76.8 us: shards(): lax.psum_scatter(merged_part, 'heads', scatter_dimension=1, tiled=True)]
    ppermute x0 -> x70, waiting for transfers between devices: none -> 229 us  [swap(): return lax.ppermute(value, axis, [(i, i ^ stride) for i in range(size)])]
    all_gather x8 -> x1, waiting for transfers between devices: 222 us -> 0.01 us  [shards(): grads = lax.all_gather(pack, ('dp', 'seq'))]
    psum x1 -> x0, waiting for transfers between devices: 113 us -> none  [shards(): lax.psum((querymap_part, querybias_part, key_weight_slice, valuemap_part,...]
    dot_general x24 -> x20, matrix products: 121 us -> 9.56 us  [the longest x8 4.19 us: dot(): return jnp.dot(a, b, preferred_element_type=wide)]
    ppermute x0 -> x70, starting transfers between devices: none -> 70.8 us  [swap(): return lax.ppermute(value, axis, [(i, i ^ stride) for i in range(size)])]
    pallas_call x0 -> x18, Pallas kernels: none -> 55.5 us  [the longest x17 43.6 us: kernel_call(): pl.pallas_call(body, in_specs=[in_smem] * len(scalars) + [in_vmem] * len(...]
    psum x2 -> x0, blocking collectives: 55.3 us -> none  [the longest x1 40.6 us: shards(): lax.psum((mergebias_part, normgain_part, normshift_part, outerbias_part,...]
  transfers between devices with their start and end apart: 13 -> 71, of which waited for: 12 -> 32; matrix products, arithmetic and copies ran while one was open for 8% -> 8% of each run, Pallas kernels for 0% -> 10%
where the time goes in v1:
time: 445 us; the launch traced here: 438 us
  waiting for transfers between devices  229 us (51%)
  starting transfers between devices  70.9 us (16%)
  Pallas kernels  55.5 us (12%)
  local copies, waits for them, and re-layouts  38.3 us (9%)
  other arithmetic  17.9 us (4%)
  between operations  16.7 us (4%)
  matrix products  9.56 us (2%)
    ppermute x70, waiting for transfers between devices, swap(): return lax.ppermute(value, axis, [(i, i ^ stride) for i in range(size)])  229 us
    ppermute x70, starting transfers between devices, swap(): return lax.ppermute(value, axis, [(i, i ^ stride) for i in range(size)])  70.8 us
    pallas_call x17, Pallas kernels, kernel_call(): pl.pallas_call(body, in_specs=[in_smem] * len(scalars) + [in_vmem] * len(...  43.6 us
    unnamed x268, local copies, waits for them, and re-layouts  29.2 us
    pallas_call x1, Pallas kernels, attend_back(): pl.pallas_call(functools.partial(attend_back_kernel, pieces, groups), gri...  11.9 us
  transfers between devices with their start and end apart: 71, of which 32 were waited for; matrix products, arithmetic and copies ran while one was open for 8% of the time, Pallas kernels for 10%

profile of v1, /device:TPU:0, one launch (start us, length us, event | category | flops | bytes accessed | tf_op | source)
XLA Modules:
  0.0 437.6 jit_solution(11012936291891238736)
XLA Ops:
  7.3 3.1 collective-permute-start
  10.4 2.6 collective-permute-start.1
  18.9 1.6 copy-done.19
  20.4 1.6 copy-done.20
  25.6 9.5 %collective-permute-done.19 = bf16[32,1024]{1,0:T(8,128)(2,1)S(1)} collective-permute-done((bf16[32,1024]{1,0:T(8,128)(2,1)S(1)}, bf16[32,1024]{1,0:T(8,128)(2,1)S(1)}, u32[]{:S(2)}, u32[]{:S(2)}) %collective-permute-start.19) | collective-permute-done | bytes 65568 | tf_op jit(solution)/shard_map/ppermute | solution.py:35
  35.2 2.0 collective-permute-start.2
  37.3 1.7 fusion.14
  39.0 2.6 collective-permute-start.20
  42.1 9.6 %collective-permute-done.20 = bf16[2,32,1024]{2,1,0:T(8,128)(2,1)S(1)} collective-permute-done((bf16[2,32,1024]{2,1,0:T(8,128)(2,1)S(1)}, bf16[2,32,1024]{2,1,0:T(8,128)(2,1)S(1)}, u32[]{:S(2)}, u32[]{:S(2)}) %collective-permute-start.20) | collective-permute-done | bytes 131104 | tf_op jit(solution)/shard_map/ppermute | solution.py:35
  52.9 1.7 collective-permute-start.21
  54.9 1.6 collective-permute-start.9
  57.0 2.6 collective-permute-start.3
  61.5 2.7 collective-permute-done.9.refs_13_.refs_19_
  64.2 5.6 %collective-permute-done.10.refs_14_.refs_20_ = bf16[4,64,512]{2,1,0:T(8,128)(2,1)S(1)} collective-permute-done((bf16[4,64,512]{2,1,0:T(8,128)(2,1)S(1)}, bf16[4,64,512]{2,1,0:T(8,128)(2,1)S(1)}, u32[]{:S(2)}, u32[]{:S(2)}) %collective-permute-start.10) | collective-permute-done | bytes 262176 | tf_op jit(solution)/shard_map/ppermute | solution.py:35
  70.4 2.4 collective-permute-done.3
  75.9 8.0 %attend.1 = (bf16[4,64,256]{2,1,0:T(8,128)(2,1)S(1)}, bf16[4,64,256]{2,1,0:T(8,128)(2,1)S(1)}, bf16[4,64,256]{2,1,0:T(8,128)(2,1)S(1)}, bf16[4,64,256]{2,1,0:T(8...) custom-call(s32[6]{0:T(128)S(1)} %pad_add_fusion.1.pos, bf16[4,64,256]{2,1,0:T(8,128)(2,1)S(1)} %bitcast.160, ...), custom_call_target="tpu_custom_call" | custom-call | flops 2147483648 | bytes 4718592 | tf_op jit(solution)/shard_map/attend/pallas_call | solution.py:76
  84.3 3.6 collective-permute-start.27
  88.0 12.5 %collective-permute-done.27 = bf16[128,1024]{1,0:T(8,128)(2,1)S(1)} collective-permute-done((bf16[128,1024]{1,0:T(8,128)(2,1)S(1)}, bf16[128,1024]{1,0:T(8,128)(2,1)S(1)}, u32[]{:S(2)}, u32[]{:S(2)}) %collective-permute-start.27) | collective-permute-done | bytes 262176 | tf_op jit(solution)/shard_map/ppermute | solution.py:35
  101.4 3.1 collective-permute-start.17
  105.7 2.5 collective-permute-done.16.refs_1_
  109.8 4.6 %collective-permute-done.17.refs_2_ = bf16[256,256]{1,0:T(8,128)(2,1)S(1)} collective-permute-done((bf16[256,256]{1,0:T(8,128)(2,1)S(1)}, bf16[256,256]{1,0:T(8,128)(2,1)S(1)}, u32[]{:S(2)}, u32[]{:S(2)}) %collective-permute-start.17) | collective-permute-done | bytes 131104 | tf_op jit(solution)/shard_map/ppermute | solution.py:35
  118.3 2.0 collective-permute-start.31
  120.4 1.6 collective-permute-start.29
  123.1 8.0 %collective-permute-done.31.a_ref.refs_4_ = bf16[256,1024]{1,0:T(8,128)(2,1)S(1)} collective-permute-done((bf16[256,1024]{1,0:T(8,128)(2,1)S(1)}, bf16[256,1024]{1,0:T(8,128)(2,1)S(1)}, u32[]{:S(2)}, u32[]{:S(2)}) %collective-permute-start.31) | collective-permute-done | bytes 524320 | tf_op jit(solution)/shard_map/ppermute | solution.py:35
  131.1 1.6 collective-permute-done.29
  132.7 2.7 collective-permute-done.26.refs_4_
  135.8 3.6 feed_forward.2
  141.1 2.8 feed_forward.3
  151.6 20.4 %collective-permute-done.35.refs_7_ = bf16[512,1024]{1,0:T(8,128)(2,1)} collective-permute-done((bf16[512,1024]{1,0:T(8,128)(2,1)}, bf16[512,1024]{1,0:T(8,128)(2,1)}, u32[]{:S(2)}, u32[]{:S(2)}) %collective-permute-start.35) | collective-permute-done | bytes 1048608 | tf_op jit(solution)/shard_map/ppermute | solution.py:35
  176.1 3.2 final_norm.1
  181.2 12.9 %collective-permute-done.38.a_ref.refs_4_ = bf16[256,1024]{1,0:T(8,128)(2,1)S(1)} collective-permute-done((bf16[256,1024]{1,0:T(8,128)(2,1)S(1)}, bf16[256,1024]{1,0:T(8,128)(2,1)S(1)}, u32[]{:S(2)}, u32[]{:S(2)}) %collective-permute-start.38) | collective-permute-done | bytes 524320 | tf_op jit(solution)/shard_map/ppermute | solution.py:35
  194.1 1.9 copy-done.79
  196.1 3.3 feed_backward.2
  200.4 2.4 feed_backward.3
  204.1 1.6 collective-permute-done.40
  221.2 2.8 first_back.1
  225.4 1.7 collective-permute-start.43
  228.9 9.5 %collective-permute-done.54 = bf16[2,256,1024]{2,1,0:T(8,128)(2,1)S(1)} collective-permute-done((bf16[2,256,1024]{2,1,0:T(8,128)(2,1)S(1)}, bf16[2,256,1024]{2,1,0:T(8,128)(2,1)S(1)}, u32[]{:S(2)}, u32[]{:S(2)}) %collective-permute-start.54) | collective-permute-done | bytes 1048608 | tf_op jit(solution)/shard_map/ppermute | solution.py:35
  238.5 2.5 collective-permute-start.44
  245.6 11.9 %attend_back.1 = (bf16[4,4,64,256]{3,2,1,0:T(8,128)(2,1)S(1)}, bf16[4,4,64,512]{3,2,1,0:T(8,128)(2,1)S(1)}, bf16[4,4,64,512]{3,2,1,0:T(8,128)(2,1)S(1)}, bf16[4,...) custom-call(s32[6]{0:T(128)S(1)} %copy-done.75, bf16[4,64,256]{2,1,0:T(8,128)(2,1)S(1)} %bitcast.161, ...), custom_call_target="tpu_custom_call" | custom-call | flops 5368709120 | bytes 13107200 | tf_op jit(solution)/shard_map/attend_back/pallas_call | solution.py:260
  258.6 9.3 %collective-permute-done.55 = bf16[1,256,1024]{2,1,0:T(8,128)(2,1)S(1)} collective-permute-done((bf16[1,256,1024]{2,1,0:T(8,128)(2,1)S(1)}, bf16[1,256,1024]{2,1,0:T(8,128)(2,1)S(1)}, u32[]{:S(2)}, u32[]{:S(2)}) %collective-permute-start.55) | collective-permute-done | bytes 524320 | tf_op jit(solution)/shard_map/ppermute | solution.py:35
  270.2 11.9 %collective-permute-done.53 = bf16[1,272,1024]{2,1,0:T(8,128)(2,1)S(1)} collective-permute-done((bf16[1,272,1024]{2,1,0:T(8,128)(2,1)S(1)}, bf16[1,272,1024]{2,1,0:T(8,128)(2,1)S(1)}, u32[]{:S(2)}, u32[]{:S(2)}) %collective-permute-start.53) | collective-permute-done | bytes 557088 | tf_op jit(solution)/shard_map/ppermute | solution.py:35
  282.8 2.8 collective-permute-start.69
  286.8 4.2 qkv_grads.1
  292.3 16.8 %collective-permute-done.69 = bf16[272,1024]{1,0:T(8,128)(2,1)S(1)} collective-permute-done((bf16[272,1024]{1,0:T(8,128)(2,1)S(1)}, bf16[272,1024]{1,0:T(8,128)(2,1)S(1)}, u32[]{:S(2)}, u32[]{:S(2)}) %collective-permute-start.69) | collective-permute-done | bytes 557088 | tf_op jit(solution)/shard_map/ppermute | solution.py:35
  310.2 1.9 pad_maximum_fusion.7
  314.1 1.6 collective-permute-start.49
  316.2 17.8 %collective-permute-done.61 = bf16[272,1024]{1,0:T(8,128)(2,1)} collective-permute-done((bf16[272,1024]{1,0:T(8,128)(2,1)}, bf16[272,1024]{1,0:T(8,128)(2,1)}, u32[]{:S(2)}, u32[]{:S(2)}) %collective-permute-start.61) | collective-permute-done | bytes 557088 | tf_op jit(solution)/shard_map/ppermute | solution.py:35
  337.7 13.1 %collective-permute-done.49 = bf16[2,4,64,512]{3,2,1,0:T(8,128)(2,1)S(1)} collective-permute-done((bf16[2,4,64,512]{3,2,1,0:T(8,128)(2,1)S(1)}, bf16[2,4,64,512]{3,2,1,0:T(8,128)(2,1)S(1)}, u32[]{:S(2)}, u32[]{:S(2)}) %collective-permute-start.49) | collective-permute-done | bytes 524320 | tf_op jit(solution)/shard_map/ppermute | solution.py:35
  350.8 15.3 %collective-permute-done.47 = bf16[2,4,64,512]{3,2,1,0:T(8,128)(2,1)S(1)} collective-permute-done((bf16[2,4,64,512]{3,2,1,0:T(8,128)(2,1)S(1)}, bf16[2,4,64,512]{3,2,1,0:T(8,128)(2,1)S(1)}, u32[]{:S(2)}, u32[]{:S(2)}) %collective-permute-start.47) | collective-permute-done | bytes 524320 | tf_op jit(solution)/shard_map/ppermute | solution.py:35
  368.1 4.7 %collective-permute-done.59 = bf16[1,112,1024]{2,1,0:T(8,128)(2,1)S(1)} collective-permute-done((bf16[1,112,1024]{2,1,0:T(8,128)(2,1)S(1)}, bf16[1,112,1024]{2,1,0:T(8,128)(2,1)S(1)}, u32[]{:S(2)}, u32[]{:S(2)}) %collective-permute-start.59) | collective-permute-done | bytes 229408 | tf_op jit(solution)/shard_map/ppermute | solution.py:35
  374.2 2.1 collective-permute-start.50
  376.3 5.8 %collective-permute-done.63 = bf16[80,1024]{1,0:T(8,128)(2,1)S(1)} collective-permute-done((bf16[80,1024]{1,0:T(8,128)(2,1)S(1)}, bf16[80,1024]{1,0:T(8,128)(2,1)S(1)}, u32[]{:S(2)}, u32[]{:S(2)}) %collective-permute-start.63) | collective-permute-done | bytes 163872 | tf_op jit(solution)/shard_map/ppermute | solution.py:35
  383.8 4.7 %collective-permute-done.64 = bf16[48,1024]{1,0:T(8,128)(2,1)S(1)} collective-permute-done((bf16[48,1024]{1,0:T(8,128)(2,1)S(1)}, bf16[48,1024]{1,0:T(8,128)(2,1)S(1)}, u32[]{:S(2)}, u32[]{:S(2)}) %collective-permute-start.64) | collective-permute-done | bytes 98336 | tf_op jit(solution)/shard_map/ppermute | solution.py:35
  389.6 2.4 collective-permute-start.48
  392.4 3.0 collective-permute-done.65
  395.5 1.8 collective-permute-start.66
  397.6 3.4 collective-permute-start.51
  401.6 3.9 collective-permute-done.66.refs_1_
  405.5 2.3 collective-permute-done.48
  407.8 9.8 %collective-permute-done.51 = bf16[256,1024]{1,0:T(8,128)(2,1)S(1)} collective-permute-done((bf16[256,1024]{1,0:T(8,128)(2,1)S(1)}, bf16[256,1024]{1,0:T(8,128)(2,1)S(1)}, u32[]{:S(2)}, u32[]{:S(2)}) %collective-permute-start.51) | collective-permute-done | bytes 524320 | tf_op jit(solution)/shard_map/ppermute | solution.py:35
  420.3 2.4 qkv_out.1
  423.4 2.3 copy-done.2
  425.6 4.1 feed_out.1
  (473 shorter events, 92.5 us)
Async XLA Ops:
  7.2 416.1 %all-gather.3.cloned.1.call-start = ((), (), s32[]{:S(2)}) async-start(), calls=%async_computation | async-start | bytes 5013504 | tf_op jit(solution)/shard_map/all_gather | solution.py:904
  7.3 31.7 %collective-permute-start = (bf16[256,1024]{1,0:T(8,128)(2,1)}, bf16[256,1024]{1,0:T(8,128)(2,1)S(1)}, u32[]{:S(2)}, u32[]{:S(2)}) collective-permute-start(bf16[256,1024]{1,0:T(8,128)(2,1)} %bitcast.145), channel_id=1, source_target_pairs={{0,1},{1,0},{2,3},{3,2},{4,5},{5,4},{6,7},{7,6},{8,9},{9,8},{10,11... | collective-permute-start | bytes 1572872 | tf_op jit(solution)/shard_map/ppermute | solution.py:35
  10.4 24.8 %collective-permute-start.1 = (bf16[256,1024]{1,0:T(8,128)(2,1)}, bf16[256,1024]{1,0:T(8,128)(2,1)S(1)}, u32[]{:S(2)}, u32[]{:S(2)}) collective-permute-start(bf16[256,1024]{1,0:T(8,128)(2,1)} %bitcast.146), channel_id=1, source_target_pairs={{0,2},{1,3},{2,0},{3,1},{4,6},{5,7},{6,4},{7,5},{8,10},{9,11},{10,... | collective-permute-start | bytes 1572872 | tf_op jit(solution)/shard_map/ppermute | solution.py:35
  16.8 38.1 %collective-permute-start.4 = (bf16[4,64,512]{2,1,0:T(8,128)(2,1)S(1)}, bf16[4,64,512]{2,1,0:T(8,128)(2,1)S(1)}, u32[]{:S(2)}, u32[]{:S(2)}) collective-permute-start(bf16[4,64,512]{2,1,0:T(8,128)(2,1)S(1)} %bitcast.168), channel_id=1, source_target_pairs={{0,4},{4,0},{8,12},{12,8},{1,5},{5,1},{9,13},{13,9},{2,6},{6,2},{1... | collective-permute-start | bytes 786440 | tf_op jit(solution)/shard_map/ppermute | solution.py:35
  16.8 18.3 %collective-permute-start.8 = (bf16[4,64,512]{2,1,0:T(8,128)(2,1)S(1)}, bf16[4,64,512]{2,1,0:T(8,128)(2,1)}, u32[]{:S(2)}, u32[]{:S(2)}) collective-permute-start(bf16[4,64,512]{2,1,0:T(8,128)(2,1)S(1)} %bitcast.169), channel_id=1, source_target_pairs={{0,8},{4,12},{8,0},{12,4},{1,9},{5,13},{9,1},{13,5},{2,10},{6,14},... | collective-permute-start | bytes 786440 | tf_op jit(solution)/shard_map/ppermute | solution.py:35
  18.3 16.8 %collective-permute-start.19 = (bf16[32,1024]{1,0:T(8,128)(2,1)S(1)}, bf16[32,1024]{1,0:T(8,128)(2,1)S(1)}, u32[]{:S(2)}, u32[]{:S(2)}) collective-permute-start(bf16[32,1024]{1,0:T(8,128)(2,1)S(1)} %constant_dynamic-slice_fusion.3), channel_id=1, source_target_pairs={{0,1},{1,0},{2,3},{3,2},{4,5},{5,4},{6,7},{7,6},{8,9},{9,8},{10,11... | collective-permute-start | bytes 196616 | tf_op jit(solution)/shard_map/ppermute | solution.py:35
  35.1 21.4 %collective-permute-start.12 = (bf16[4,64,512]{2,1,0:T(8,128)(2,1)}, bf16[4,64,512]{2,1,0:T(8,128)(2,1)S(1)}, u32[]{:S(2)}, u32[]{:S(2)}) collective-permute-start(bf16[4,64,512]{2,1,0:T(8,128)(2,1)} %collective-permute-done.8.refs_12_.refs_18_), channel_id=1, source_target_pairs={{0,4},{4,0},{8,12},{12,8},{1,5},{5,1},{9,13},{13,9},{2,6},{6,2},{1... | collective-permute-start | bytes 786440 | tf_op jit(solution)/shard_map/ppermute | solution.py:35
  35.2 17.2 %collective-permute-start.2 = (bf16[256,1024]{1,0:T(8,128)(2,1)S(1)}, bf16[256,1024]{1,0:T(8,128)(2,1)S(1)}, u32[]{:S(2)}, u32[]{:S(2)}) collective-permute-start(bf16[256,1024]{1,0:T(8,128)(2,1)S(1)} %collective-permute-done.1.refs_4_), channel_id=1, source_target_pairs={{0,1},{1,0},{2,3},{3,2},{4,5},{5,4},{6,7},{7,6},{8,9},{9,8},{10,11... | collective-permute-start | bytes 1572872 | tf_op jit(solution)/shard_map/ppermute | solution.py:35
  38.9 30.9 %collective-permute-start.6 = (bf16[4,64,512]{2,1,0:T(8,128)(2,1)S(1)}, bf16[4,64,512]{2,1,0:T(8,128)(2,1)S(1)}, u32[]{:S(2)}, u32[]{:S(2)}) collective-permute-start(bf16[4,64,512]{2,1,0:T(8,128)(2,1)S(1)} %bitcast.172), channel_id=1, source_target_pairs={{0,4},{4,0},{8,12},{12,8},{1,5},{5,1},{9,13},{13,9},{2,6},{6,2},{1... | collective-permute-start | bytes 786440 | tf_op jit(solution)/shard_map/ppermute | solution.py:35
  39.0 12.7 %collective-permute-start.20 = (bf16[2,32,1024]{2,1,0:T(8,128)(2,1)S(1)}, bf16[2,32,1024]{2,1,0:T(8,128)(2,1)S(1)}, u32[]{:S(2)}, u32[]{:S(2)}) collective-permute-start(bf16[2,32,1024]{2,1,0:T(8,128)(2,1)S(1)} %pad_maximum_fusion.13), channel_id=1, source_target_pairs={{0,2},{1,3},{2,0},{3,1},{4,6},{5,7},{6,4},{7,5},{8,10},{9,11},{10,... | collective-permute-start | bytes 393224 | tf_op jit(solution)/shard_map/ppermute | solution.py:35
  52.9 6.8 %collective-permute-start.21 = (bf16[3,32,1024]{2,1,0:T(8,128)(2,1)S(1)}, bf16[3,32,1024]{2,1,0:T(8,128)(2,1)S(1)}, u32[]{:S(2)}, u32[]{:S(2)}) collective-permute-start(bf16[3,32,1024]{2,1,0:T(8,128)(2,1)S(1)} %pad_maximum_fusion.11), channel_id=1, source_target_pairs={{0,16},{16,0},{1,17},{17,1},{2,18},{18,2},{3,19},{19,3},{4,20},{20... | collective-permute-start | bytes 589832 | tf_op jit(solution)/shard_map/ppermute | solution.py:35
  54.9 9.3 %collective-permute-start.9 = (bf16[4,64,512]{2,1,0:T(8,128)(2,1)S(1)}, bf16[4,64,512]{2,1,0:T(8,128)(2,1)S(1)}, u32[]{:S(2)}, u32[]{:S(2)}) collective-permute-start(bf16[4,64,512]{2,1,0:T(8,128)(2,1)S(1)} %bitcast.177), channel_id=1, source_target_pairs={{0,8},{4,12},{8,0},{12,4},{1,9},{5,13},{9,1},{13,5},{2,10},{6,14},... | collective-permute-start | bytes 786440 | tf_op jit(solution)/shard_map/ppermute | solution.py:35
  56.5 13.3 %collective-permute-start.10 = (bf16[4,64,512]{2,1,0:T(8,128)(2,1)S(1)}, bf16[4,64,512]{2,1,0:T(8,128)(2,1)S(1)}, u32[]{:S(2)}, u32[]{:S(2)}) collective-permute-start(bf16[4,64,512]{2,1,0:T(8,128)(2,1)S(1)} %bitcast.173), channel_id=1, source_target_pairs={{0,8},{4,12},{8,0},{12,4},{1,9},{5,13},{9,1},{13,5},{2,10},{6,14},... | collective-permute-start | bytes 786440 | tf_op jit(solution)/shard_map/ppermute | solution.py:35
  57.0 15.8 %collective-permute-start.3 = (bf16[144,1024]{1,0:T(8,128)(2,1)S(1)}, bf16[144,1024]{1,0:T(8,128)(2,1)S(1)}, u32[]{:S(2)}, u32[]{:S(2)}) collective-permute-start(bf16[144,1024]{1,0:T(8,128)(2,1)S(1)} %copy-done.124), channel_id=1, source_target_pairs={{0,2},{1,3},{2,0},{3,1},{4,6},{5,7},{6,4},{7,5},{8,10},{9,11},{10,... | collective-permute-start | bytes 884744 | tf_op jit(solution)/shard_map/ppermute | solution.py:35
  59.7 14.7 %collective-permute-start.11 = (bf16[4,64,512]{2,1,0:T(8,128)(2,1)S(1)}, bf16[4,64,512]{2,1,0:T(8,128)(2,1)S(1)}, u32[]{:S(2)}, u32[]{:S(2)}) collective-permute-start(bf16[4,64,512]{2,1,0:T(8,128)(2,1)S(1)} %bitcast.180), channel_id=1, source_target_pairs={{0,8},{4,12},{8,0},{12,4},{1,9},{5,13},{9,1},{13,5},{2,10},{6,14},... | collective-permute-start | bytes 786440 | tf_op jit(solution)/shard_map/ppermute | solution.py:35
  64.2 10.5 %collective-permute-start.13 = (bf16[4,64,512]{2,1,0:T(8,128)(2,1)S(1)}, bf16[4,64,512]{2,1,0:T(8,128)(2,1)S(1)}, u32[]{:S(2)}, u32[]{:S(2)}) collective-permute-start(bf16[4,64,512]{2,1,0:T(8,128)(2,1)S(1)} %collective-permute-done.9.refs_13_.refs_19_), channel_id=1, source_target_pairs={{0,4},{4,0},{8,12},{12,8},{1,5},{5,1},{9,13},{13,9},{2,6},{6,2},{1... | collective-permute-start | bytes 786440 | tf_op jit(solution)/shard_map/ppermute | solution.py:35
  72.8 11.2 %collective-permute-start.22 = (bf16[6,32,1024]{2,1,0:T(8,128)(2,1)S(1)}, bf16[6,32,1024]{2,1,0:T(8,128)(2,1)S(1)}, u32[]{:S(2)}, u32[]{:S(2)}) collective-permute-start(bf16[6,32,1024]{2,1,0:T(8,128)(2,1)S(1)} %pad_maximum_fusion.9), channel_id=1, source_target_pairs={{0,8},{4,12},{8,0},{12,4},{1,9},{5,13},{9,1},{13,5},{2,10},{6,14},... | collective-permute-start | bytes 1179656 | tf_op jit(solution)/shard_map/ppermute | solution.py:35
  84.1 30.3 %collective-permute-start.23 = (bf16[12,32,1024]{2,1,0:T(8,128)(2,1)S(1)}, bf16[12,32,1024]{2,1,0:T(8,128)(2,1)S(1)}, u32[]{:S(2)}, u32[]{:S(2)}) collective-permute-start(bf16[12,32,1024]{2,1,0:T(8,128)(2,1)S(1)} %constant_dynamic-update-slice_fusion.2.refs_5_), channel_id=1, source_target_pairs={{0,4},{4,0},{8,12},{12,8},{1,5},{5,1},{9,13},{13,9},{2,6},{6,2},{1... | collective-permute-start | bytes 2359304 | tf_op jit(solution)/shard_map/ppermute | solution.py:35
  84.3 16.1 %collective-permute-start.27 = (bf16[128,1024]{1,0:T(8,128)(2,1)S(1)}, bf16[128,1024]{1,0:T(8,128)(2,1)S(1)}, u32[]{:S(2)}, u32[]{:S(2)}) collective-permute-start(bf16[128,1024]{1,0:T(8,128)(2,1)S(1)} %slice_bitcast_fusion.4), channel_id=1, source_target_pairs={{0,2},{1,3},{2,0},{3,1},{4,6},{5,7},{6,4},{7,5},{8,10},{9,11},{10,... | collective-permute-start | bytes 786440 | tf_op jit(solution)/shard_map/ppermute | solution.py:35
  100.4 19.9 %collective-permute-start.28 = (bf16[1,128,1024]{2,1,0:T(8,128)(2,1)S(1)}, bf16[1,128,1024]{2,1,0:T(8,128)(2,1)S(1)}, u32[]{:S(2)}, u32[]{:S(2)}) collective-permute-start(bf16[1,128,1024]{2,1,0:T(8,128)(2,1)S(1)} %bitcast.154), channel_id=1, source_target_pairs={{0,16},{16,0},{1,17},{17,1},{2,18},{18,2},{3,19},{19,3},{4,20},{20... | collective-permute-start | bytes 786440 | tf_op jit(solution)/shard_map/ppermute | solution.py:35
  101.4 6.9 %collective-permute-start.16 = (bf16[256,256]{1,0:T(8,128)(2,1)S(1)}, bf16[256,256]{1,0:T(8,128)(2,1)S(1)}, u32[]{:S(2)}, u32[]{:S(2)}) collective-permute-start(bf16[256,256]{1,0:T(8,128)(2,1)S(1)} %bitcast.190), channel_id=1, source_target_pairs={{0,1},{1,0},{2,3},{3,2},{4,5},{5,4},{6,7},{7,6},{8,9},{9,8},{10,11... | collective-permute-start | bytes 393224 | tf_op jit(solution)/shard_map/ppermute | solution.py:35
  101.4 13.0 %collective-permute-start.17 = (bf16[256,256]{1,0:T(8,128)(2,1)S(1)}, bf16[256,256]{1,0:T(8,128)(2,1)S(1)}, u32[]{:S(2)}, u32[]{:S(2)}) collective-permute-start(bf16[256,256]{1,0:T(8,128)(2,1)S(1)} %bitcast.189), channel_id=1, source_target_pairs={{0,2},{1,3},{2,0},{3,1},{4,6},{5,7},{6,4},{7,5},{8,10},{9,11},{10,... | collective-permute-start | bytes 393224 | tf_op jit(solution)/shard_map/ppermute | solution.py:35
  104.4 10.0 %collective-permute-start.18 = (bf16[256,256]{1,0:T(8,128)(2,1)S(1)}, bf16[256,256]{1,0:T(8,128)(2,1)S(1)}, u32[]{:S(2)}, u32[]{:S(2)}) collective-permute-start(bf16[256,256]{1,0:T(8,128)(2,1)S(1)} %bitcast.188), channel_id=1, source_target_pairs={{0,3},{1,2},{2,1},{3,0},{4,7},{5,6},{6,5},{7,4},{8,11},{9,10},{10,... | collective-permute-start | bytes 393224 | tf_op jit(solution)/shard_map/ppermute | solution.py:35
  108.2 13.7 %collective-permute-start.25 = (bf16[1,144,1024]{2,1,0:T(8,128)(2,1)S(1)}, bf16[1,144,1024]{2,1,0:T(8,128)(2,1)S(1)}, u32[]{:S(2)}, u32[]{:S(2)}) collective-permute-start(bf16[1,144,1024]{2,1,0:T(8,128)(2,1)S(1)} %bitcast.208), channel_id=1, source_target_pairs={{0,8},{4,12},{8,0},{12,4},{1,9},{5,13},{9,1},{13,5},{2,10},{6,14},... | collective-permute-start | bytes 884744 | tf_op jit(solution)/shard_map/ppermute | solution.py:35
  118.3 12.7 %collective-permute-start.31 = (bf16[256,1024]{1,0:T(8,128)(2,1)S(1)}, bf16[256,1024]{1,0:T(8,128)(2,1)S(1)}, u32[]{:S(2)}, u32[]{:S(2)}) collective-permute-start(bf16[256,1024]{1,0:T(8,128)(2,1)S(1)} %get-tuple-element.187.a_ref.refs_2_), channel_id=1, source_target_pairs={{0,1},{1,0},{2,3},{3,2},{4,5},{5,4},{6,7},{7,6},{8,9},{9,8},{10,11... | collective-permute-start | bytes 1572872 | tf_op jit(solution)/shard_map/ppermute | solution.py:35
  120.4 12.3 %collective-permute-start.29 = (bf16[2,128,1024]{2,1,0:T(8,128)(2,1)S(1)}, bf16[2,128,1024]{2,1,0:T(8,128)(2,1)S(1)}, u32[]{:S(2)}, u32[]{:S(2)}) collective-permute-start(bf16[2,128,1024]{2,1,0:T(8,128)(2,1)S(1)} %pad_maximum_fusion.8), channel_id=1, source_target_pairs={{0,8},{4,12},{8,0},{12,4},{1,9},{5,13},{9,1},{13,5},{2,10},{6,14},... | collective-permute-start | bytes 1572872 | tf_op jit(solution)/shard_map/ppermute | solution.py:35
  122.0 13.4 %collective-permute-start.26 = (bf16[2,144,1024]{2,1,0:T(8,128)(2,1)S(1)}, bf16[2,144,1024]{2,1,0:T(8,128)(2,1)S(1)}, u32[]{:S(2)}, u32[]{:S(2)}) collective-permute-start(bf16[2,144,1024]{2,1,0:T(8,128)(2,1)S(1)} %pad_maximum_fusion.4.refs_3_), channel_id=1, source_target_pairs={{0,16},{16,0},{1,17},{17,1},{2,18},{18,2},{3,19},{19,3},{4,20},{20... | collective-permute-start | bytes 1769480 | tf_op jit(solution)/shard_map/ppermute | solution.py:35
  123.1 12.6 %collective-permute-start.24 = (bf16[256,1024]{1,0:T(8,128)(2,1)S(1)}, bf16[256,1024]{1,0:T(8,128)(2,1)S(1)}, u32[]{:S(2)}, u32[]{:S(2)}) collective-permute-start(bf16[256,1024]{1,0:T(8,128)(2,1)S(1)} %get-tuple-element.187.a_ref.refs_2_), channel_id=1, source_target_pairs={{0,4},{4,0},{8,12},{12,8},{1,5},{5,1},{9,13},{13,9},{2,6},{6,2},{1... | collective-permute-start | bytes 1572872 | tf_op jit(solution)/shard_map/ppermute | solution.py:35
  131.1 10.1 %collective-permute-start.32 = (bf16[256,1024]{1,0:T(8,128)(2,1)S(1)}, bf16[256,1024]{1,0:T(8,128)(2,1)S(1)}, u32[]{:S(2)}, u32[]{:S(2)}) collective-permute-start(bf16[256,1024]{1,0:T(8,128)(2,1)S(1)} %collective-permute-done.31.a_ref.refs_4_), channel_id=1, source_target_pairs={{0,4},{4,0},{8,12},{12,8},{1,5},{5,1},{9,13},{13,9},{2,6},{6,2},{1... | collective-permute-start | bytes 1572872 | tf_op jit(solution)/shard_map/ppermute | solution.py:35
  146.5 25.6 %collective-permute-start.35 = (bf16[512,1024]{1,0:T(8,128)(2,1)}, bf16[512,1024]{1,0:T(8,128)(2,1)}, u32[]{:S(2)}, u32[]{:S(2)}) collective-permute-start(bf16[512,1024]{1,0:T(8,128)(2,1)} %pad_maximum_fusion.2), channel_id=1, source_target_pairs={{0,8},{4,12},{8,0},{12,4},{1,9},{5,13},{9,1},{13,5},{2,10},{6,14},... | collective-permute-start | bytes 3145736 | tf_op jit(solution)/shard_map/ppermute | solution.py:35
  148.0 24.1 %collective-permute-start.34 = (bf16[256,1024]{1,0:T(8,128)(2,1)}, bf16[256,1024]{1,0:T(8,128)(2,1)}, u32[]{:S(2)}, u32[]{:S(2)}) collective-permute-start(bf16[256,1024]{1,0:T(8,128)(2,1)} %add_convert_fusion.10), channel_id=1, source_target_pairs={{0,1},{1,0},{2,3},{3,2},{4,5},{5,4},{6,7},{7,6},{8,9},{9,8},{10,11... | collective-permute-start | bytes 1572872 | tf_op jit(solution)/shard_map/ppermute | solution.py:35
  148.3 23.8 %collective-permute-start.30 = (bf16[256,1024]{1,0:T(8,128)(2,1)}, bf16[256,1024]{1,0:T(8,128)(2,1)}, u32[]{:S(2)}, u32[]{:S(2)}) collective-permute-start(bf16[256,1024]{1,0:T(8,128)(2,1)} %get-tuple-element.155), channel_id=1, source_target_pairs={{0,4},{4,0},{8,12},{12,8},{1,5},{5,1},{9,13},{13,9},{2,6},{6,2},{1... | collective-permute-start | bytes 1572872 | tf_op jit(solution)/shard_map/ppermute | solution.py:35
  180.9 13.2 %collective-permute-start.38 = (bf16[256,1024]{1,0:T(8,128)(2,1)S(1)}, bf16[256,1024]{1,0:T(8,128)(2,1)S(1)}, u32[]{:S(2)}, u32[]{:S(2)}) collective-permute-start(bf16[256,1024]{1,0:T(8,128)(2,1)S(1)} %get-tuple-element.183.a_ref.refs_2_), channel_id=1, source_target_pairs={{0,1},{1,0},{2,3},{3,2},{4,5},{5,4},{6,7},{7,6},{8,9},{9,8},{10,11... | collective-permute-start | bytes 1572872 | tf_op jit(solution)/shard_map/ppermute | solution.py:35
  181.2 12.9 %collective-permute-start.36 = (bf16[256,1024]{1,0:T(8,128)(2,1)S(1)}, bf16[256,1024]{1,0:T(8,128)(2,1)S(1)}, u32[]{:S(2)}, u32[]{:S(2)}) collective-permute-start(bf16[256,1024]{1,0:T(8,128)(2,1)S(1)} %get-tuple-element.183.a_ref.refs_2_), channel_id=1, source_target_pairs={{0,4},{4,0},{8,12},{12,8},{1,5},{5,1},{9,13},{13,9},{2,6},{6,2},{1... | collective-permute-start | bytes 1572872 | tf_op jit(solution)/shard_map/ppermute | solution.py:35
  194.1 6.3 %collective-permute-start.39 = (bf16[256,1024]{1,0:T(8,128)(2,1)S(1)}, bf16[256,1024]{1,0:T(8,128)(2,1)S(1)}, u32[]{:S(2)}, u32[]{:S(2)}) collective-permute-start(bf16[256,1024]{1,0:T(8,128)(2,1)S(1)} %collective-permute-done.38.a_ref.refs_4_), channel_id=1, source_target_pairs={{0,4},{4,0},{8,12},{12,8},{1,5},{5,1},{9,13},{13,9},{2,6},{6,2},{1... | collective-permute-start | bytes 1572872 | tf_op jit(solution)/shard_map/ppermute | solution.py:35
  206.7 14.5 %collective-permute-start.41 = (bf16[256,1024]{1,0:T(8,128)(2,1)}, bf16[256,1024]{1,0:T(8,128)(2,1)}, u32[]{:S(2)}, u32[]{:S(2)}) collective-permute-start(bf16[256,1024]{1,0:T(8,128)(2,1)} %add_convert_fusion.9), channel_id=1, source_target_pairs={{0,1},{1,0},{2,3},{3,2},{4,5},{5,4},{6,7},{7,6},{8,9},{9,8},{10,11... | collective-permute-start | bytes 1572872 | tf_op jit(solution)/shard_map/ppermute | solution.py:35
  207.0 14.2 %collective-permute-start.37 = (bf16[256,1024]{1,0:T(8,128)(2,1)}, bf16[256,1024]{1,0:T(8,128)(2,1)}, u32[]{:S(2)}, u32[]{:S(2)}) collective-permute-start(bf16[256,1024]{1,0:T(8,128)(2,1)} %get-tuple-element.167), channel_id=1, source_target_pairs={{0,4},{4,0},{8,12},{12,8},{1,5},{5,1},{9,13},{13,9},{2,6},{6,2},{1... | collective-permute-start | bytes 1572872 | tf_op jit(solution)/shard_map/ppermute | solution.py:35
  207.0 79.7 %collective-permute-start.56 = (bf16[512,1024]{1,0:T(8,128)(2,1)}, bf16[512,1024]{1,0:T(8,128)(2,1)S(1)}, u32[]{:S(2)}, u32[]{:S(2)}) collective-permute-start(bf16[512,1024]{1,0:T(8,128)(2,1)} %pad_maximum_fusion.3), channel_id=1, source_target_pairs={{0,8},{4,12},{8,0},{12,4},{1,9},{5,13},{9,1},{13,5},{2,10},{6,14},... | collective-permute-start | bytes 3145736 | tf_op jit(solution)/shard_map/ppermute | solution.py:35
  213.0 25.3 %collective-permute-start.54 = (bf16[2,256,1024]{2,1,0:T(8,128)(2,1)S(1)}, bf16[2,256,1024]{2,1,0:T(8,128)(2,1)S(1)}, u32[]{:S(2)}, u32[]{:S(2)}) collective-permute-start(bf16[2,256,1024]{2,1,0:T(8,128)(2,1)S(1)} %weight_grad.4), channel_id=1, source_target_pairs={{0,16},{16,0},{1,17},{17,1},{2,18},{18,2},{3,19},{19,3},{4,20},{20... | collective-permute-start | bytes 3145736 | tf_op jit(solution)/shard_map/ppermute | solution.py:35
  215.6 42.0 %collective-permute-start.52 = (bf16[2,272,1024]{2,1,0:T(8,128)(2,1)S(1)}, bf16[2,272,1024]{2,1,0:T(8,128)(2,1)S(1)}, u32[]{:S(2)}, u32[]{:S(2)}) collective-permute-start(bf16[2,272,1024]{2,1,0:T(8,128)(2,1)S(1)} %weight_grad.5), channel_id=1, source_target_pairs={{0,8},{4,12},{8,0},{12,4},{1,9},{5,13},{9,1},{13,5},{2,10},{6,14},... | collective-permute-start | bytes 3342344 | tf_op jit(solution)/shard_map/ppermute | solution.py:35
  224.0 17.5 %collective-permute-start.42 = (bf16[256,256]{1,0:T(8,128)(2,1)S(1)}, bf16[256,256]{1,0:T(8,128)(2,1)S(1)}, u32[]{:S(2)}, u32[]{:S(2)}) collective-permute-start(bf16[256,256]{1,0:T(8,128)(2,1)S(1)} %get-tuple-element.197), channel_id=1, source_target_pairs={{0,1},{1,0},{2,3},{3,2},{4,5},{5,4},{6,7},{7,6},{8,9},{9,8},{10,11... | collective-permute-start | bytes 393224 | tf_op jit(solution)/shard_map/ppermute | solution.py:35
  225.4 17.3 %collective-permute-start.43 = (bf16[256,256]{1,0:T(8,128)(2,1)S(1)}, bf16[256,256]{1,0:T(8,128)(2,1)S(1)}, u32[]{:S(2)}, u32[]{:S(2)}) collective-permute-start(bf16[256,256]{1,0:T(8,128)(2,1)S(1)} %get-tuple-element.198), channel_id=1, source_target_pairs={{0,2},{1,3},{2,0},{3,1},{4,6},{5,7},{6,4},{7,5},{8,10},{9,11},{10,... | collective-permute-start | bytes 393224 | tf_op jit(solution)/shard_map/ppermute | solution.py:35
  238.5 6.9 %collective-permute-start.44 = (bf16[256,256]{1,0:T(8,128)(2,1)S(1)}, bf16[256,256]{1,0:T(8,128)(2,1)S(1)}, u32[]{:S(2)}, u32[]{:S(2)}) collective-permute-start(bf16[256,256]{1,0:T(8,128)(2,1)S(1)} %get-tuple-element.199), channel_id=1, source_target_pairs={{0,3},{1,2},{2,1},{3,0},{4,7},{5,6},{6,5},{7,4},{8,11},{9,10},{10,... | collective-permute-start | bytes 393224 | tf_op jit(solution)/shard_map/ppermute | solution.py:35
  241.5 27.7 %collective-permute-start.60 = (bf16[528,1024]{1,0:T(8,128)(2,1)S(1)}, bf16[528,1024]{1,0:T(8,128)(2,1)S(1)}, u32[]{:S(2)}, u32[]{:S(2)}) collective-permute-start(bf16[528,1024]{1,0:T(8,128)(2,1)S(1)} %pad_maximum_fusion.1), channel_id=1, source_target_pairs={{0,16},{16,0},{1,17},{17,1},{2,18},{18,2},{3,19},{19,3},{4,20},{20... | collective-permute-start | bytes 3244040 | tf_op jit(solution)/shard_map/ppermute | solution.py:35
  242.7 25.2 %collective-permute-start.55 = (bf16[1,256,1024]{2,1,0:T(8,128)(2,1)S(1)}, bf16[1,256,1024]{2,1,0:T(8,128)(2,1)S(1)}, u32[]{:S(2)}, u32[]{:S(2)}) collective-permute-start(bf16[1,256,1024]{2,1,0:T(8,128)(2,1)S(1)} %slice.272), channel_id=1, source_target_pairs={{0,8},{4,12},{8,0},{12,4},{1,9},{5,13},{9,1},{13,5},{2,10},{6,14},... | collective-permute-start | bytes 1572872 | tf_op jit(solution)/shard_map/ppermute | solution.py:35
  257.5 24.9 %collective-permute-start.46 = (bf16[4,4,64,512]{3,2,1,0:T(8,128)(2,1)S(1)}, bf16[4,4,64,512]{3,2,1,0:T(8,128)(2,1)S(1)}, u32[]{:S(2)}, u32[]{:S(2)}) collective-permute-start(bf16[4,4,64,512]{3,2,1,0:T(8,128)(2,1)S(1)} %get-tuple-element.206), channel_id=1, source_target_pairs={{0,4},{4,0},{8,12},{12,8},{1,5},{5,1},{9,13},{13,9},{2,6},{6,2},{1... | collective-permute-start | bytes 3145736 | tf_op jit(solution)/shard_map/ppermute | solution.py:35
  257.6 28.8 %collective-permute-start.45 = (bf16[4,4,64,512]{3,2,1,0:T(8,128)(2,1)S(1)}, bf16[4,4,64,512]{3,2,1,0:T(8,128)(2,1)S(1)}, u32[]{:S(2)}, u32[]{:S(2)}) collective-permute-start(bf16[4,4,64,512]{3,2,1,0:T(8,128)(2,1)S(1)} %get-tuple-element.204), channel_id=1, source_target_pairs={{0,4},{4,0},{8,12},{12,8},{1,5},{5,1},{9,13},{13,9},{2,6},{6,2},{1... | collective-permute-start | bytes 3145736 | tf_op jit(solution)/shard_map/ppermute | solution.py:35
  267.9 14.2 %collective-permute-start.53 = (bf16[1,272,1024]{2,1,0:T(8,128)(2,1)S(1)}, bf16[1,272,1024]{2,1,0:T(8,128)(2,1)S(1)}, u32[]{:S(2)}, u32[]{:S(2)}) collective-permute-start(bf16[1,272,1024]{2,1,0:T(8,128)(2,1)S(1)} %slice.269), channel_id=1, source_target_pairs={{0,16},{16,0},{1,17},{17,1},{2,18},{18,2},{3,19},{19,3},{4,20},{20... | collective-permute-start | bytes 1671176 | tf_op jit(solution)/shard_map/ppermute | solution.py:35
  282.8 26.3 %collective-permute-start.69 = (bf16[272,1024]{1,0:T(8,128)(2,1)S(1)}, bf16[272,1024]{1,0:T(8,128)(2,1)S(1)}, u32[]{:S(2)}, u32[]{:S(2)}) collective-permute-start(bf16[272,1024]{1,0:T(8,128)(2,1)S(1)} %pad_maximum_fusion.6), channel_id=1, source_target_pairs={{0,2},{1,3},{2,0},{3,1},{4,6},{5,7},{6,4},{7,5},{8,10},{9,11},{10,... | collective-permute-start | bytes 1671176 | tf_op jit(solution)/shard_map/ppermute | solution.py:35
  312.1 21.8 %collective-permute-start.61 = (bf16[272,1024]{1,0:T(8,128)(2,1)}, bf16[272,1024]{1,0:T(8,128)(2,1)}, u32[]{:S(2)}, u32[]{:S(2)}) collective-permute-start(bf16[272,1024]{1,0:T(8,128)(2,1)} %pad_maximum_fusion.7), channel_id=1, source_target_pairs={{0,8},{4,12},{8,0},{12,4},{1,9},{5,13},{9,1},{13,5},{2,10},{6,14},... | collective-permute-start | bytes 1671176 | tf_op jit(solution)/shard_map/ppermute | solution.py:35
  313.9 22.3 %collective-permute-start.57 = (bf16[4,112,1024]{2,1,0:T(8,128)(2,1)S(1)}, bf16[4,112,1024]{2,1,0:T(8,128)(2,1)S(1)}, u32[]{:S(2)}, u32[]{:S(2)}) collective-permute-start(bf16[4,112,1024]{2,1,0:T(8,128)(2,1)S(1)} %slice.275), channel_id=1, source_target_pairs={{0,4},{4,0},{8,12},{12,8},{1,5},{5,1},{9,13},{13,9},{2,6},{6,2},{1... | collective-permute-start | bytes 2752520 | tf_op jit(solution)/shard_map/ppermute | solution.py:35
  314.1 36.7 %collective-permute-start.49 = (bf16[2,4,64,512]{3,2,1,0:T(8,128)(2,1)S(1)}, bf16[2,4,64,512]{3,2,1,0:T(8,128)(2,1)S(1)}, u32[]{:S(2)}, u32[]{:S(2)}) collective-permute-start(bf16[2,4,64,512]{3,2,1,0:T(8,128)(2,1)S(1)} %get-tuple-element.231), channel_id=1, source_target_pairs={{0,8},{4,12},{8,0},{12,4},{1,9},{5,13},{9,1},{13,5},{2,10},{6,14},... | collective-permute-start | bytes 1572872 | tf_op jit(solution)/shard_map/ppermute | solution.py:35
  315.6 50.4 %collective-permute-start.47 = (bf16[2,4,64,512]{3,2,1,0:T(8,128)(2,1)S(1)}, bf16[2,4,64,512]{3,2,1,0:T(8,128)(2,1)S(1)}, u32[]{:S(2)}, u32[]{:S(2)}) collective-permute-start(bf16[2,4,64,512]{3,2,1,0:T(8,128)(2,1)S(1)} %get-tuple-element.232), channel_id=1, source_target_pairs={{0,8},{4,12},{8,0},{12,4},{1,9},{5,13},{9,1},{13,5},{2,10},{6,14},... | collective-permute-start | bytes 1572872 | tf_op jit(solution)/shard_map/ppermute | solution.py:35
  336.1 36.7 %collective-permute-start.62 = (bf16[144,1024]{1,0:T(8,128)(2,1)S(1)}, bf16[144,1024]{1,0:T(8,128)(2,1)S(1)}, u32[]{:S(2)}, u32[]{:S(2)}) collective-permute-start(bf16[144,1024]{1,0:T(8,128)(2,1)S(1)} %pad_maximum_fusion.10), channel_id=1, source_target_pairs={{0,4},{4,0},{8,12},{12,8},{1,5},{5,1},{9,13},{13,9},{2,6},{6,2},{1... | collective-permute-start | bytes 884744 | tf_op jit(solution)/shard_map/ppermute | solution.py:35
  336.6 29.9 %collective-permute-start.58 = (bf16[2,112,1024]{2,1,0:T(8,128)(2,1)S(1)}, bf16[2,112,1024]{2,1,0:T(8,128)(2,1)S(1)}, u32[]{:S(2)}, u32[]{:S(2)}) collective-permute-start(bf16[2,112,1024]{2,1,0:T(8,128)(2,1)S(1)} %slice.277), channel_id=1, source_target_pairs={{0,16},{16,0},{1,17},{17,1},{2,18},{18,2},{3,19},{19,3},{4,20},{20... | collective-permute-start | bytes 1376264 | tf_op jit(solution)/shard_map/ppermute | solution.py:35
  366.7 6.1 %collective-permute-start.59 = (bf16[1,112,1024]{2,1,0:T(8,128)(2,1)S(1)}, bf16[1,112,1024]{2,1,0:T(8,128)(2,1)S(1)}, u32[]{:S(2)}, u32[]{:S(2)}) collective-permute-start(bf16[1,112,1024]{2,1,0:T(8,128)(2,1)S(1)} %slice.279), channel_id=1, source_target_pairs={{0,8},{4,12},{8,0},{12,4},{1,9},{5,13},{9,1},{13,5},{2,10},{6,14},... | collective-permute-start | bytes 688136 | tf_op jit(solution)/shard_map/ppermute | solution.py:35
  373.8 8.3 %collective-permute-start.63 = (bf16[80,1024]{1,0:T(8,128)(2,1)S(1)}, bf16[80,1024]{1,0:T(8,128)(2,1)S(1)}, u32[]{:S(2)}, u32[]{:S(2)}) collective-permute-start(bf16[80,1024]{1,0:T(8,128)(2,1)S(1)} %pad_maximum_fusion.12), channel_id=1, source_target_pairs={{0,1},{1,0},{2,3},{3,2},{4,5},{5,4},{6,7},{7,6},{8,9},{9,8},{10,11... | collective-permute-start | bytes 491528 | tf_op jit(solution)/shard_map/ppermute | solution.py:35
  374.2 23.1 %collective-permute-start.50 = (bf16[256,1024]{1,0:T(8,128)(2,1)S(1)}, bf16[256,1024]{1,0:T(8,128)(2,1)S(1)}, u32[]{:S(2)}, u32[]{:S(2)}) collective-permute-start(bf16[256,1024]{1,0:T(8,128)(2,1)S(1)} %fusion.8), channel_id=1, source_target_pairs={{0,1},{1,0},{2,3},{3,2},{4,5},{5,4},{6,7},{7,6},{8,9},{9,8},{10,11... | collective-permute-start | bytes 1572872 | tf_op jit(solution)/shard_map/ppermute | solution.py:35
  388.6 6.8 %collective-permute-start.65 = (bf16[1,144,1024]{2,1,0:T(8,128)(2,1)S(1)}, bf16[1,144,1024]{2,1,0:T(8,128)(2,1)S(1)}, u32[]{:S(2)}, u32[]{:S(2)}) collective-permute-start(bf16[1,144,1024]{2,1,0:T(8,128)(2,1)S(1)} %maximum_bitcast_fusion), channel_id=1, source_target_pairs={{0,8},{4,12},{8,0},{12,4},{1,9},{5,13},{9,1},{13,5},{2,10},{6,14},... | collective-permute-start | bytes 884744 | tf_op jit(solution)/shard_map/ppermute | solution.py:35
  389.6 18.3 %collective-permute-start.48 = (bf16[256,1024]{1,0:T(8,128)(2,1)S(1)}, bf16[256,1024]{1,0:T(8,128)(2,1)S(1)}, u32[]{:S(2)}, u32[]{:S(2)}) collective-permute-start(bf16[256,1024]{1,0:T(8,128)(2,1)S(1)} %fusion.7), channel_id=1, source_target_pairs={{0,1},{1,0},{2,3},{3,2},{4,5},{5,4},{6,7},{7,6},{8,9},{9,8},{10,11... | collective-permute-start | bytes 1572872 | tf_op jit(solution)/shard_map/ppermute | solution.py:35
  395.5 10.1 %collective-permute-start.66 = (bf16[2,144,1024]{2,1,0:T(8,128)(2,1)S(1)}, bf16[2,144,1024]{2,1,0:T(8,128)(2,1)S(1)}, u32[]{:S(2)}, u32[]{:S(2)}) collective-permute-start(bf16[2,144,1024]{2,1,0:T(8,128)(2,1)S(1)} %pad_maximum_fusion.5.refs_0_), channel_id=1, source_target_pairs={{0,16},{16,0},{1,17},{17,1},{2,18},{18,2},{3,19},{19,3},{4,20},{20... | collective-permute-start | bytes 1769480 | tf_op jit(solution)/shard_map/ppermute | solution.py:35
  397.6 20.0 %collective-permute-start.51 = (bf16[256,1024]{1,0:T(8,128)(2,1)S(1)}, bf16[256,1024]{1,0:T(8,128)(2,1)S(1)}, u32[]{:S(2)}, u32[]{:S(2)}) collective-permute-start(bf16[256,1024]{1,0:T(8,128)(2,1)S(1)} %fusion.6), channel_id=1, source_target_pairs={{0,2},{1,3},{2,0},{3,1},{4,6},{5,7},{6,4},{7,5},{8,10},{9,11},{10,... | collective-permute-start | bytes 1572872 | tf_op jit(solution)/shard_map/ppermute | solution.py:35
  401.6 18.8 %collective-permute-start.67 = (bf16[2,144,1024]{2,1,0:T(8,128)(2,1)S(1)}, bf16[2,144,1024]{2,1,0:T(8,128)(2,1)S(1)}, u32[]{:S(2)}, u32[]{:S(2)}) collective-permute-start(bf16[2,144,1024]{2,1,0:T(8,128)(2,1)S(1)} %pad_maximum_fusion.5.refs_0_), channel_id=1, source_target_pairs={{0,4},{4,0},{8,12},{12,8},{1,5},{5,1},{9,13},{13,9},{2,6},{6,2},{1... | collective-permute-start | bytes 1769480 | tf_op jit(solution)/shard_map/ppermute | solution.py:35
  405.5 14.8 %collective-permute-start.68 = (bf16[2,144,1024]{2,1,0:T(8,128)(2,1)S(1)}, bf16[2,144,1024]{2,1,0:T(8,128)(2,1)S(1)}, u32[]{:S(2)}, u32[]{:S(2)}) collective-permute-start(bf16[2,144,1024]{2,1,0:T(8,128)(2,1)S(1)} %collective-permute-done.66.refs_1_), channel_id=1, source_target_pairs={{0,4},{4,0},{8,12},{12,8},{1,5},{5,1},{9,13},{13,9},{2,6},{6,2},{1... | collective-permute-start | bytes 1769480 | tf_op jit(solution)/shard_map/ppermute | solution.py:35
  (140 other events, 1497.3 us)
Sparse Core Ops, SparseCore 0:
  310.3 54.6 all-gather.2

commit v2 on v1

v2 whole, which is shorter than its diff:
```python
import functools

import jax
import jax.numpy as jnp
from jax import lax
from jax.experimental import pallas as pl
from jax.experimental.pallas import tpu as pltpu
from jax.sharding import PartitionSpec as P

HEAD_DIM = 64


epsilon = 1e-06
score_scale = 0.125
masked_score = -1000000000.0
low = jnp.bfloat16
wide = jnp.float32
vmem_bytes = 48 * 1024 * 1024


def dot(a, b):
    return jnp.dot(a, b, preferred_element_type=wide)


def dot_nt(a, b):
    return lax.dot_general(a, b, (((1,), (1,)), ((), ())), preferred_element_type=wide)


def dot_tn(a, b):
    return lax.dot_general(a, b, (((0,), (0,)), ((), ())), preferred_element_type=wide)


def swap(value, axis, stride):
    size = lax.axis_size(axis)
    return lax.ppermute(value, axis, [(i, i ^ stride) for i in range(size)])


def swap_slots(value, mask):
    size = lax.axis_size("dp") * lax.axis_size("seq")
    return lax.ppermute(value, ("dp", "seq"), [(i, i ^ mask) for i in range(size)])


def bit_of(bit):
    axis, stride = bit
    return (lax.axis_index(axis) // stride) % 2


def add_low(a, b):
    return (a.astype(wide) + b.astype(wide)).astype(low)


def params(mebibytes):
    return pltpu.CompilerParams(vmem_limit_bytes=mebibytes * 1024 * 1024)


in_vmem = pl.BlockSpec(memory_space=pltpu.VMEM)
in_smem = pl.BlockSpec(memory_space=pltpu.SMEM)
anywhere = pl.BlockSpec(memory_space=pl.ANY)
in_hbm = pl.BlockSpec(memory_space=pltpu.HBM)
hbm = True
kernels_alone = ("attend", "attend_back", "merge_norm", "project", "join_units", "stack_pairs")


def kernel_call(
    body, name, arrays, out, scalars=(), scratch=(), mebibytes=16, waits=(), far_in=(), local=(), flops=1
):
    ns, na, nw, no, nl = len(scalars), len(arrays), len(waits), len(out), len(local)
    alone = name in kernels_alone
    far_in = [i for i in range(na) if alone and (far_in is hbm or i in far_in)]
    far_out = [i for i, o in enumerate(out) if alone and len(o) > 2 and o[2]]
    buffers = [pltpu.VMEM(arrays[i].shape, arrays[i].dtype) for i in far_in]
    buffers += [pltpu.VMEM(out[i][0], out[i][1]) for i in far_out]
    count = len(buffers)

    def whole(*refs):
        here = list(refs[: ns + na])
        at = ns + na + nw
        kept, outs, rest = refs[at : at + nl], list(refs[at + nl : at + nl + no]), refs[at + nl + no :]
        rest, (*held_refs, sems) = (rest[: len(rest) - count - 1], rest[len(rest) - count - 1 :])
        copies = []
        for k, i in enumerate(far_in):
            copies.append(pltpu.make_async_copy(here[ns + i], held_refs[k], sems.at[k]))
            copies[-1].start()
            here[ns + i] = held_refs[k]
        for copy in copies:
            copy.wait()
        copies = []
        for k, i in enumerate(far_out, len(far_in)):
            copies.append(pltpu.make_async_copy(held_refs[k], outs[i], sems.at[k]))
            outs[i] = held_refs[k]
        body(*here, *kept, *outs, *rest)
        for copy in copies:
            copy.start()
        for copy in copies:
            copy.wait()

    return pl.pallas_call(
        whole,
        in_specs=[in_smem] * ns
        + [in_hbm if i in far_in else in_vmem for i in range(na)]
        + [anywhere] * nw
        + [in_hbm] * nl,
        out_specs=[in_hbm if i in far_out else in_vmem for i in range(no)],
        out_shape=[jax.ShapeDtypeStruct(o[0], o[1]) for o in out],
        scratch_shapes=list(scratch) + buffers + [pltpu.SemaphoreType.DMA((max(count, 1),))],
        compiler_params=params(60 if alone else mebibytes),
        cost_estimate=pl.CostEstimate(flops=flops, bytes_accessed=1, transcendentals=0),
        name=name,
    )(*scalars, *arrays, *waits, *local)


def nothing(*refs):
    pass


def gate(values, waits):
    found = pl.pallas_call(
        nothing,
        in_specs=[anywhere] * (len(values) + len(waits)),
        out_specs=[anywhere] * len(values),
        out_shape=[jax.ShapeDtypeStruct(v.shape, v.dtype) for v in values],
        input_output_aliases={i: i for i in range(len(values))},
        compiler_params=params(1),
        name="gate",
    )(*values, *waits)
    return list(found)


def pad16(count):
    return -(-count // 16) * 16


def place(pos, proteins, groups, share, i, j):
    seq, heads = pos[proteins], pos[proteins + 1]
    return pl.multiple_of(((seq ^ i) * groups + (heads ^ j)) * share, share)


def masked(scores, length, first):
    key_at = first + lax.broadcasted_iota(jnp.int32, scores.shape, 0)
    return jnp.where(key_at < length, scores, masked_score)


def chunks(n, block):
    return [(0, n - block, False)] * (n > block) + [(n - block, n, True)]


def piece_list(refs, groups):
    found, count = [], 0
    for ref in refs:
        for n in range(ref.shape[0]):
            found.append((ref, count // groups, count % groups, n))
            count += 1
    return found


def start_keys(pos, p, proteins, groups, kv_refs, kv_all, sems, blocks, block, wait):
    share = kv_refs[0].shape[2]
    for k, (ref, i, j, n) in enumerate(piece_list(kv_refs, groups)):
        at = place(pos, proteins, groups, share, i, j)

        @pl.when(at < blocks * block)
        def _():
            copy = pltpu.make_async_copy(ref.at[n, p], kv_all.at[p, pl.ds(at, share), :], sems.at[p])
            if wait:
                copy.wait()
            else:
                copy.start()


def query_rows(refs, p):
    found = [ref[n, p] for ref in refs for n in range(ref.shape[0])]
    return jnp.concatenate(found) * jnp.asarray(score_scale, low)


def attend_kernel(counts, pos, *refs):
    stacks, arrays, groups = counts
    q_refs, kv_refs = refs[:stacks], refs[stacks : stacks + arrays]
    ctx_refs, (ctx_t_ref, lse_ref, kv_all, sems) = refs[stacks + arrays : -4], refs[-4:]
    _, proteins, share, width = q_refs[0].shape
    total = kv_all.shape[1]
    block = min(256, total)
    heads = range(width // HEAD_DIM)

    def keys_of(p, wait):
        blocks = (pos[p] + block - 1) // block
        start_keys(pos, p, proteins, groups, kv_refs, kv_all, sems, blocks, block, wait)
        return blocks

    for p in range(proteins):
        keys_of(p, False)

    def protein(p, carry):
        length = pos[p]
        blocks = keys_of(p, True)

        def body(count):
            n = count * block
            queries = query_rows(q_refs, p)
            cols = lambda h: slice(h * HEAD_DIM, (h + 1) * HEAD_DIM)
            value_cols = lambda h: slice(width + h * HEAD_DIM, width + (h + 1) * HEAD_DIM)
            cuts = chunks(n, block)
            scores = [
                [dot_nt(kv_all[p, a:b, cols(h)], queries[:, cols(h)]) for a, b, _ in cuts]
                for h in heads
            ]
            weights, denominators = [], []
            for h in heads:
                found = [
                    masked(value, length, a) if last else value
                    for value, (a, _, last) in zip(scores[h], cuts)
                ]
                high = functools.reduce(
                    jnp.maximum, [jnp.max(value, axis=0, keepdims=True) for value in found]
                )
                found = [jnp.exp(value - high) for value in found]
                denominator = sum(jnp.sum(value, axis=0, keepdims=True) for value in found)
                lse_ref[p, h : h + 1, :] = high + jnp.log(denominator)
                weights.append([value.astype(low) for value in found])
                denominators.append(denominator)
            context_t = jnp.concatenate(
                [
                    sum(
                        dot_tn(kv_all[p, a:b, value_cols(h)], value)
                        for (a, b, _), value in zip(cuts, weights[h])
                    )
                    / denominators[h]
                    for h in heads
                ]
            )
            ctx_t_ref[p] = context_t
            context = context_t.T.astype(low)
            for j, ref in enumerate(ctx_refs):
                ref[p] = context[j * share : (j + 1) * share]

        for count in range(1, total // block + 1):
            pl.when(blocks == count)(functools.partial(body, count))
        return carry

    lax.fori_loop(0, proteins, protein, 0)


def attend_back_kernel(counts, pos, *refs):
    stacks, arrays, groups = counts
    q_refs, dctx_refs, refs = refs[:stacks], refs[stacks : stacks + groups], refs[stacks + groups :]
    ctx_t_ref, lse_ref, kv_refs, refs = refs[0], refs[1], refs[2 : 2 + arrays], refs[2 + arrays :]
    dq_ref, dkv_refs, (kv_all, dkv_all, sems) = refs[0], refs[1:-3], refs[-3:]
    _, proteins, share, width = q_refs[0].shape
    rows = groups * share
    total = kv_all.shape[1]
    block = min(256, total)
    heads = range(width // HEAD_DIM)

    def keys_of(p, wait):
        blocks = jnp.where(pos[proteins] * rows < pos[p], (pos[p] + block - 1) // block, 0)
        start_keys(pos, p, proteins, groups, kv_refs, kv_all, sems, blocks, block, wait)
        return blocks

    for p in range(proteins):
        keys_of(p, False)

    def protein(p, carry):
        length = pos[p]
        blocks = keys_of(p, True)

        @pl.when(blocks == 0)
        def _():
            for ref in (dq_ref, *dkv_refs):
                ref[:, p] = jnp.zeros((groups, share, ref.shape[-1]), low)

        def body(count):
            n = count * block
            queries = query_rows(q_refs, p)
            dctx = jnp.concatenate([ref[p] for ref in dctx_refs])
            product = dctx.astype(wide).T * ctx_t_ref[p]
            cols = lambda h: slice(h * HEAD_DIM, (h + 1) * HEAD_DIM)
            value_cols = lambda h: slice(width + h * HEAD_DIM, width + (h + 1) * HEAD_DIM)
            deltas = [jnp.sum(product[cols(h), :], axis=0, keepdims=True) for h in heads]
            dq = []
            for a, b, last in chunks(n, block):
                scores = [dot_nt(kv_all[p, a:b, cols(h)], queries[:, cols(h)]) for h in heads]
                dprobs = [dot_nt(kv_all[p, a:b, value_cols(h)], dctx[:, cols(h)]) for h in heads]
                probs, dscores = [], []
                for h in heads:
                    score = masked(scores[h], length, a) if last else scores[h]
                    prob = jnp.exp(score - lse_ref[p, h : h + 1, :])
                    probs.append(prob.astype(low))
                    dscores.append((prob * (dprobs[h] - deltas[h])).astype(low))
                dv = [dot(probs[h], dctx[:, cols(h)]) for h in heads]
                dk = [dot(dscores[h], queries[:, cols(h)]) for h in heads]
                dq.append(
                    jnp.concatenate([dot_tn(kv_all[p, a:b, cols(h)], dscores[h]) for h in heads])
                )
                dkv_all[a:b, :width] = jnp.concatenate(dk, axis=1).astype(low)
                dkv_all[a:b, width:] = jnp.concatenate(dv, axis=1).astype(low)
            if n < total:
                dkv_all[n:, :] = jnp.zeros((total - n, 2 * width), low)
            dq_all = (sum(dq).T * score_scale).astype(low)
            for j in range(groups):
                dq_ref[j, p] = dq_all[j * share : (j + 1) * share]
            for i, ref in enumerate(dkv_refs):
                for j in range(groups):
                    at = place(pos, proteins, groups, share, i, j)
                    ref[j, p] = dkv_all[pl.ds(at, share), :]

        for count in range(1, total // block + 1):
            pl.when(blocks == count)(functools.partial(body, count))
        return carry

    lax.fori_loop(0, proteins, protein, 0)


def attend(pos, queries, kv_pieces, waits):
    groups = sum(q.shape[0] for q in queries)
    _, proteins, share, width = queries[0].shape
    rows = groups * share
    total = share * sum(piece.shape[0] for piece in kv_pieces)
    found = kernel_call(
        functools.partial(attend_kernel, (len(queries), len(kv_pieces), groups)),
        "attend",
        queries,
        [((proteins, share, width), low, hbm)] * groups
        + [((proteins, width, rows), wide, hbm), ((proteins, 8, rows), wide, hbm)],
        scalars=[pos],
        scratch=[
            pltpu.VMEM((proteins, total, 2 * width), low),
            pltpu.SemaphoreType.DMA((proteins,)),
        ],
        mebibytes=32,
        far_in=hbm,
        local=kv_pieces,
        waits=waits,
        flops=int(1e10),
    )
    return found[:groups], found[groups], found[groups + 1]


def attend_back(pos, queries, dctx, ctx_t, lse, kv_pieces, waits):
    groups = len(dctx)
    _, proteins, share, width = queries[0].shape
    total = share * sum(piece.shape[0] for piece in kv_pieces)
    pieces = total // (groups * share)
    arrays = [*queries, *dctx, ctx_t, lse]
    found = kernel_call(
        functools.partial(attend_back_kernel, (len(queries), len(kv_pieces), groups)),
        "attend_back",
        arrays,
        [((groups, proteins, share, width), low)]
        + [((groups, proteins, share, 2 * width), low)] * pieces,
        scalars=[pos],
        scratch=[
            pltpu.VMEM((proteins, total, 2 * width), low),
            pltpu.VMEM((total, 2 * width), low),
            pltpu.SemaphoreType.DMA((proteins,)),
        ],
        mebibytes=32,
        far_in=[i for i in range(len(arrays)) if not 0 <= i - len(queries) < groups],
        local=kv_pieces,
        waits=waits,
        flops=int(2e10),
    )
    return found[0], found[1:]


def project_kernel(count, *refs):
    tok_refs, (qmap_ref, kmap_ref, vmap_ref, qbias_ref, vbias_ref, q_ref, kv_ref) = refs[:count], refs[count:]
    width = q_ref.shape[-1]
    for j, tok_ref in enumerate(tok_refs):
        shape = q_ref.shape[1:]
        queries = dot(tok_ref[...], qmap_ref[...]) + qbias_ref[...].astype(wide)
        q_ref[j] = queries.astype(low).reshape(shape)
        kv_ref[j, :, :, :width] = dot(tok_ref[...], kmap_ref[...]).astype(low).reshape(shape)
        values = dot(tok_ref[...], vmap_ref[...]) + vbias_ref[...].astype(wide)
        kv_ref[j, :, :, width:] = values.astype(low).reshape(shape)


def project(tok, maps, proteins, waits=()):
    width = maps[0].shape[1]
    share = tok[0].shape[0] // proteins
    return kernel_call(
        functools.partial(project_kernel, len(tok)),
        "project",
        [*tok, *maps],
        [
            ((len(tok), proteins, share, width), low, hbm),
            ((len(tok), proteins, share, 2 * width), low, hbm),
        ],
        waits=waits,
        far_in=hbm,
    )


def unit_of(values):
    centered = values - jnp.mean(values, axis=-1, keepdims=True)
    variance = jnp.mean(centered * centered, axis=-1, keepdims=True)
    inverse = lax.rsqrt(variance + epsilon)
    return centered * inverse, inverse


def norm_back(grad_rows, unitized, inverse, scales):
    scaled = grad_rows * scales
    grad_mean = jnp.mean(scaled, axis=-1, keepdims=True)
    cross_mean = jnp.mean(scaled * unitized, axis=-1, keepdims=True)
    return inverse * (scaled - grad_mean - unitized * cross_mean)


def steps(rows):
    size = 64 if rows % 64 == 0 else rows
    return [slice(at, at + size) for at in range(0, rows, size)]


def merge_kernel(groups, heads, *refs):
    ctx_refs, refs = refs[:groups], refs[groups:]
    own_map, maps_all, tok_ref, small_ref = refs[:4]
    normed_ref, low_ref, unit_ref, inv_ref, maps_ref = refs[4:]
    others = groups - 1
    slots, _, size, _ = maps_all.shape
    for j in range(others):
        for k in range(slots):
            maps_ref[j, k * size : (k + 1) * size, :] = maps_all[k, heads[0] ^ (j + 1)]
    merged = small_ref[0:1, :] + dot(ctx_refs[0][...], own_map[...])
    for j in range(others):
        merged += dot(ctx_refs[j + 1][...], maps_ref[j])
    unit_ref[...] = tok_ref[...].astype(wide) + merged
    for rows in steps(tok_ref.shape[0]):
        unit, inverse = unit_of(unit_ref[rows, :])
        normed = unit * small_ref[1:2, :] + small_ref[2:3, :]
        normed_ref[rows, :] = normed
        low_ref[rows, :] = normed.astype(low)
        unit_ref[rows, :] = unit
        inv_ref[rows, :] = jnp.broadcast_to(inverse, (inverse.shape[0], 128))


def merge_norm(heads, ctx, own_map, maps_all, tok, small, waits):
    rows, model = tok.shape
    groups = len(ctx)
    return kernel_call(
        functools.partial(merge_kernel, groups),
        "merge_norm",
        [*ctx, own_map, maps_all, tok, small],
        [
            ((rows, model), wide, hbm),
            ((rows, model), low, hbm),
            ((rows, model), wide, hbm),
            ((rows, 128), wide, hbm),
            ((groups - 1, *own_map.shape), low, hbm),
        ],
        scalars=[heads],
        waits=waits,
        far_in=hbm,
    )


def final_kernel(*refs):
    normed_ref, near_ref, core_ref, far_ref, small_ref, cot_ref, live_ref = refs[:7]
    out_ref, dsum_ref, dbranch_ref, sums_ref = refs[7:]
    gain = small_ref[4:5, :]
    gain_sum = shift_sum = bias_sum = 0.0
    for rows in steps(normed_ref.shape[0]):
        branch = near_ref[rows, :].astype(wide) + core_ref[rows, :].astype(wide)
        branch = branch + far_ref[rows, :].astype(wide) + small_ref[3:4, :]
        unit, inverse = unit_of(normed_ref[rows, :] + branch)
        out_ref[rows, :] = (unit * gain + small_ref[5:6, :]).astype(low)
        grad = cot_ref[rows, :].astype(wide) * live_ref[rows, 0:1]
        dsum = norm_back(grad, unit, inverse, gain)
        dsum_ref[rows, :] = dsum
        dbranch = dsum.astype(low)
        dbranch_ref[rows, :] = dbranch
        gain_sum += jnp.sum(grad * unit, axis=0, keepdims=True)
        shift_sum += jnp.sum(grad, axis=0, keepdims=True)
        bias_sum += jnp.sum(dbranch.astype(wide), axis=0, keepdims=True)
    sums_ref[...] = jnp.zeros(sums_ref.shape, wide)
    sums_ref[0:1, :] = bias_sum
    sums_ref[1:2, :] = gain_sum
    sums_ref[2:3, :] = shift_sum


def final_norm(normed, near, core, across, small, cot, live, waits):
    rows, model = normed.shape
    return kernel_call(
        final_kernel,
        "final_norm",
        [normed, near, core, across, small, cot, live],
        [
            ((rows, model), low, hbm),
            ((rows, model), wide, hbm),
            ((rows, model), low),
            ((8, model), wide, hbm),
        ],
        far_in=[0, 4, 5, 6],
        waits=waits,
    )


def first_back_kernel(groups, *refs):
    dsum_ref, near_ref, core_ref, far_ref, unit_ref, inv_ref, small_ref, own_map, maps_ref = refs[:9]
    dfirst_ref, dmerged_ref, sums_ref = refs[9:12]
    dctx_refs = refs[12:]
    gain = small_ref[1:2, :]
    gain_sum = shift_sum = bias_sum = 0.0
    for rows in steps(dsum_ref.shape[0]):
        grad = near_ref[rows, :].astype(wide) + core_ref[rows, :].astype(wide)
        grad = dsum_ref[rows, :] + grad + far_ref[rows, :].astype(wide)
        unit = unit_ref[rows, :]
        dfirst = norm_back(grad, unit, inv_ref[rows, 0:1], gain)
        dfirst_ref[rows, :] = dfirst
        dmerged = dfirst.astype(low)
        dmerged_ref[rows, :] = dmerged
        gain_sum += jnp.sum(grad * unit, axis=0, keepdims=True)
        shift_sum += jnp.sum(grad, axis=0, keepdims=True)
        bias_sum += jnp.sum(dmerged.astype(wide), axis=0, keepdims=True)
    for j in range(groups):
        merge_map = maps_ref[j - 1] if j else own_map[...]
        dctx_refs[j][...] = dot_nt(dmerged_ref[...], merge_map).astype(low)
    sums_ref[...] = jnp.zeros(sums_ref.shape, wide)
    sums_ref[3:4, :] = bias_sum
    sums_ref[4:5, :] = gain_sum
    sums_ref[5:6, :] = shift_sum


def first_back(dsum, near, core, across, unit, inverse, small, own_map, maps, waits):
    rows, model = dsum.shape
    groups, width = maps.shape[0] + 1, own_map.shape[0]
    found = kernel_call(
        functools.partial(first_back_kernel, groups),
        "first_back",
        [dsum, near, core, across, unit, inverse, small, own_map, maps],
        [((rows, model), wide, hbm), ((rows, model), low), ((8, model), wide, hbm)]
        + [((rows, width), low)] * groups,
        waits=waits,
        far_in=[0, 4, 5, 6, 7, 8],
    )
    return found[0], found[1], found[2], found[3:]


def forward_kernel(a_ref, b_ref, inner_ref, outer_ref, bias_ref, act_ref, slope_ref, own_ref, other_ref):
    rows = a_ref.shape[0]
    for ref, out, at in ((a_ref, own_ref, 0), (b_ref, other_ref, rows)):
        pre = dot_nt(ref[...], inner_ref[...]) + bias_ref[...]
        upper = 0.5 + 0.5 * lax.erf(pre * 0.7071067811865476)
        active = (pre * upper).astype(low)
        slope = upper + pre * (0.3989422804014327 * jnp.exp(-0.5 * pre * pre))
        act_ref[at : at + rows, :] = active
        slope_ref[at : at + rows, :] = slope.astype(low)
        out[...] = dot(active, outer_ref[...]).astype(low)


def feed_forward(a, b, inner, outer, bias, waits=()):
    rows, model = a.shape
    hidden = inner.shape[0]
    return kernel_call(
        forward_kernel,
        "feed_forward",
        [a, b, inner, outer, bias],
        [((2 * rows, hidden), low, hbm)] * 2 + [((rows, model), low)] * 2,
        waits=waits,
        far_in=[0, 1],
    )


def backward_kernel(a_ref, b_ref, inner_ref, outer_ref, slope_ref, dinner_ref, own_ref, other_ref):
    rows = a_ref.shape[0]
    for ref, out, at in ((a_ref, own_ref, 0), (b_ref, other_ref, rows)):
        dactive = dot_nt(ref[...], outer_ref[...])
        dinner = (dactive * slope_ref[at : at + rows, :].astype(wide)).astype(low)
        dinner_ref[at : at + rows, :] = dinner
        out[...] = dot(dinner, inner_ref[...]).astype(low)


def feed_backward(a, b, inner, outer, slope, waits=()):
    rows, model = a.shape
    hidden = inner.shape[0]
    return kernel_call(
        backward_kernel,
        "feed_backward",
        [a, b, inner, outer, slope],
        [((2 * rows, hidden), low, hbm)] + [((rows, model), low)] * 2,
        waits=waits,
        far_in=[4],
    )


def grad_kernel(numbers, block, bias, split, *refs):
    hid, row_refs, refs = refs[:2], refs[2:6], refs[6:]
    got_ref, out_refs = (refs[0], refs[1:]) if split else (None, refs)
    model = out_refs[0].shape[-1]
    half = len(numbers) // len(out_refs)
    for k, number in enumerate(numbers):
        cols = slice(number * block, (number + 1) * block)
        total = sums = 0.0
        for i, ref in enumerate(hid):
            rows = ref.shape[0] // 2
            total += dot_tn(ref[:rows, cols], row_refs[2 * i][...])
            total += dot_tn(ref[rows:, cols], row_refs[2 * i + 1][...])
            if bias:
                sums += jnp.sum(ref[:, cols].astype(wide), axis=0, keepdims=True)
        out_ref, at = out_refs[k // half], k % half
        if split:
            total += got_ref[k, :block, :].astype(wide)
        out_ref[at, :block, :] = total.astype(low)
        if bias:
            sums = jnp.pad(sums, ((0, 15), (0, model - block)))
            if split:
                sums += got_ref[k, block:, :].astype(wide)
            out_ref[at, block:, :] = sums.astype(low)


def weight_grad(hid, row_list, block, numbers, bias, waits, got=None):
    model = row_list[0].shape[1]
    split = got is not None
    count = len(numbers) // (1 + split)
    found = kernel_call(
        functools.partial(grad_kernel, numbers, block, bias, split),
        "weight_grad",
        [*hid, *row_list] + [got] * split,
        [((count, block + 16 * bias, model), low)] * (1 + split),
        waits=waits,
    )
    return found if split else found[0]


def units_kernel(units, shares, slot, inner_ref, outer_ref, bias_ref, own_inner, own_outer, own_bias):
    for m in range(shares):
        at = pl.multiple_of((slot[0] ^ (m << 1)) * units, units)
        own_inner[m] = inner_ref[:, pl.ds(at, units)].T
        own_outer[m] = outer_ref[pl.ds(at, units), :]
        own_bias[m] = jnp.broadcast_to(bias_ref[:, pl.ds(at, units)], (16, units))


def own_units(slot, shares, innermap, outermap, innerbias, waits):
    model = innermap.shape[0]
    units = innermap.shape[1] // (2 * shares)
    if units % 128:
        found = []
        for m in range(shares):
            at = (slot[0] ^ (m << 1)) * units
            inner = lax.dynamic_slice_in_dim(innermap, at, units, 1).T
            outer = lax.dynamic_slice_in_dim(outermap, at, units, 0)
            bias = lax.dynamic_slice_in_dim(innerbias, at, units, 1)
            found.append((inner, outer, jnp.broadcast_to(bias, (16, units))))
        return [jnp.stack(pieces) for pieces in zip(*found)]
    return kernel_call(
        functools.partial(units_kernel, units, shares),
        "own_units",
        [innermap, outermap, innerbias],
        [((shares, units, model), low, hbm)] * 2 + [((shares, 16, units), innerbias.dtype, hbm)],
        scalars=[slot],
        waits=waits,
        far_in=[0, 1],
    )


def pack_kernel(own_inner, own_outer, own_bias, pack_ref):
    units = own_inner.shape[1]
    pack_ref[:units, :] = own_inner[0]
    pack_ref[units : 2 * units, :] = own_outer[0]
    pack_ref[2 * units :, :] = jnp.zeros((16, pack_ref.shape[1]), low)
    pack_ref[2 * units :, :units] = own_bias[0]


def pack_units(own, waits):
    _, units, model = own[0].shape
    return kernel_call(
        pack_kernel, "pack_units", own, [((2 * units + 16, model), low)], waits=waits, far_in=hbm
    )[0]


def split_kernel(units, pack_ref, inner_ref, outer_ref):
    inner_ref[0, :units, :] = pack_ref[:units, :]
    inner_ref[0, units:, :] = pack_ref[2 * units :, :]
    outer_ref[0] = pack_ref[units : 2 * units, :]


def split_units(units, pack, waits):
    model = pack.shape[1]
    return kernel_call(
        functools.partial(split_kernel, units),
        "split_units",
        [pack],
        [((1, units + 16, model), low), ((1, units, model), low)],
        waits=waits,
    )


def stack_kernel(*refs):
    count = len(refs) // 3
    for k in range(count):
        a_ref, b_ref, out_ref = refs[2 * k], refs[2 * k + 1], refs[2 * count + k]
        out_ref[: a_ref.shape[0]] = a_ref[...]
        out_ref[a_ref.shape[0] :] = b_ref[...]


def stack_pairs(pairs):
    return kernel_call(
        stack_kernel,
        "stack_pairs",
        [value for pair in pairs for value in pair],
        [((2 * a.shape[0], *a.shape[1:]), a.dtype) for a, _ in pairs],
    )


def join_kernel(units, masks, own_inner, own_outer, own_bias, *refs):
    parts, (inner_ref, outer_ref, bias_ref) = refs[:-3], refs[-3:]
    for m in range(own_inner.shape[0]):
        at, far = 2 * m * units, (2 * m + 1) * units
        inner_ref[at:far, :] = own_inner[m]
        outer_ref[at:far, :] = own_outer[m]
        bias_ref[:, at:far] = own_bias[m, 0:1, :].astype(wide)
    for which, (ref, order) in enumerate(zip(parts, masks)):
        for k, m in enumerate(order):
            far = (2 * m + 1) * units
            if which < 2:
                inner_ref[far : far + units, :] = ref[k, :units, :]
                bias_ref[:, far : far + units] = ref[k, units : units + 16, :units].astype(wide)[:1]
            else:
                outer_ref[far : far + units, :] = ref[k]


def join_units(own, parts, masks, waits):
    shares, units, model = own[0].shape
    hidden = 2 * shares * units
    return kernel_call(
        functools.partial(join_kernel, units, masks),
        "join_units",
        [*own, *parts],
        [((hidden, model), low)] * 2 + [((1, hidden), wide)],
        waits=waits,
        far_in=hbm,
    )


def slot_order(number, bits):
    return ((number & 1) << (bits - 1)) | (number >> 1)


def qkv_kernel(counts, slots, slot, *refs):
    out_ref, q_all, kv_all = refs[-3:]
    dq_ref, refs = refs[0], refs[1:-3]
    width, model = dq_ref.shape[-1], out_ref.shape[-1]
    q_all[...] = dq_ref[...].reshape(q_all.shape)
    q_sum = jnp.sum(q_all[...].astype(wide), axis=0, keepdims=True)
    q_grad = kv_grad = kv_sum = 0.0
    for i, count in enumerate(counts):
        dkv_ref, tok_refs, refs = refs[0], refs[1 : 1 + count], refs[1 + count :]
        kv_all[...] = dkv_ref[...].reshape(kv_all.shape)
        kv_sum += jnp.sum(kv_all[...].astype(wide), axis=0, keepdims=True)
        at = 0
        for tok_ref in tok_refs:
            there = slice(at, at + tok_ref.shape[0])
            at += tok_ref.shape[0]
            kv_grad += dot_tn(kv_all[there, :], tok_ref[...])
            if i == 0:
                q_grad += dot_tn(q_all[there, :], tok_ref[...])
    grad = jnp.concatenate([q_grad, kv_grad]).astype(low)
    sums = jnp.concatenate([q_sum, kv_sum], axis=1)
    bits = slots.bit_length() - 1
    block = 3 * width // slots
    for b in range(slots):
        at = slot_order(slot[0] ^ b, bits)
        out_ref[at, :block, :] = grad[b * block : (b + 1) * block]
        line = jnp.pad(sums[:, b * block : (b + 1) * block], ((0, 15), (0, model - block)))
        out_ref[at, pad16(block) :, :] = line.astype(low)


def qkv_grads(slot, slots, dq, pairs, waits):
    model = pairs[0][1][0].shape[-1]
    groups, width = dq.shape[0], dq.shape[-1]
    total = dq.size // width
    far_at, at = [], 1
    for dkv, tok in pairs:
        far_at += range(at + 1, at + 1 + len(tok))
        at += 1 + len(tok)
    return kernel_call(
        functools.partial(qkv_kernel, [len(tok) for _, tok in pairs], slots),
        "qkv_grads",
        [dq] + [a for dkv, tok in pairs for a in (dkv, *tok)],
        [((slots, pad16(3 * width // slots) + 16, model), low)],
        far_in=far_at,
        scalars=[slot],
        waits=waits,
        scratch=[pltpu.VMEM((total, width), low), pltpu.VMEM((total, 2 * width), low)],
        mebibytes=24,
    )[0]


def hold_kernel(value_ref, out_ref):
    out_ref[...] = value_ref[...]


def hold(value, waits):
    out = [(value.shape, value.dtype)]
    return kernel_call(hold_kernel, "hold", [value], out, waits=waits)[0]


def add_kernel(a_ref, b_ref, *out_refs):
    at = 0
    for ref in out_refs:
        there = slice(at, at + ref.shape[0])
        at += ref.shape[0]
        ref[...] = (a_ref[there].astype(wide) + b_ref[there].astype(wide)).astype(ref.dtype)


def add_split(a, b, counts, waits=(), kind=low):
    out = [((count, *a.shape[1:]), kind) for count in counts]
    return kernel_call(add_kernel, "add_split", [a, b], out, waits=waits)


def dtokens_kernel(dq_ref, own_ref, got_ref, q_ref, k_ref, v_ref, *out_refs):
    width = dq_ref.shape[-1]
    rows = dq_ref.shape[1] * dq_ref.shape[2]
    for j, ref in enumerate(out_refs):
        dkv = (own_ref[j].astype(wide) + got_ref[j].astype(wide)).astype(low)
        dkv = dkv.reshape(rows, 2 * width)
        total = dot_nt(dq_ref[j].reshape(rows, width), q_ref[...])
        total += dot_nt(dkv[:, :width], k_ref[...]) + dot_nt(dkv[:, width:], v_ref[...])
        ref[...] = total.astype(ref.dtype)


def dtokens(dq, own, got, maps, waits):
    rows, model = dq.shape[1] * dq.shape[2], maps[0].shape[0]
    return kernel_call(
        dtokens_kernel,
        "dtokens",
        [dq, own, got, *maps],
        [((rows, model), wide), ((rows, model), low)] * (dq.shape[0] // 2),
        waits=waits,
    )


def tokens_kernel(dfirst_ref, part_ref, near_ref, far_ref, out_ref):
    total = dfirst_ref[...] + part_ref[...] + near_ref[...].astype(wide)
    out_ref[...] = (total + far_ref[...].astype(wide)).astype(low)


def pack_sums_kernel(units, inner_ref, inner_got, outer_ref, outer_got, own_ref, send_ref):
    model = own_ref.shape[1]
    inner = inner_ref[0].astype(wide) + inner_got[0].astype(wide)
    outer = outer_ref[0].astype(wide) + outer_got[0].astype(wide)
    sums = inner[2 * units :, : 2 * units].astype(low)
    for k, ref in enumerate((own_ref, send_ref)):
        there = slice(k * units, (k + 1) * units)
        ref[:units, :] = inner[there].astype(low)
        ref[units : 2 * units, :] = outer[there].astype(low)
        ref[2 * units :, :] = jnp.zeros((16, model), low)
        ref[2 * units :, :units] = sums[:, there]


def pack_sums(units, inner, inner_got, outer, outer_got, waits):
    model = inner.shape[-1]
    return kernel_call(
        functools.partial(pack_sums_kernel, units),
        "pack_sums",
        [inner, inner_got, outer, outer_got],
        [((2 * units + 16, model), low)] * 2,
        waits=waits,
    )


def merge_grad_kernel(groups, core, *refs):
    ctx_refs, (dmerged_ref, a_ref, b_ref, keep_ref, send_ref, grad_all) = refs[:groups], refs[groups:]
    half = keep_ref.shape[1]
    for j, ref in enumerate(ctx_refs):
        grad_all[...] = dot_tn(ref[...], dmerged_ref[...]).astype(low)
        keep = pl.multiple_of(core[0] * half, half)
        send = pl.multiple_of((1 - core[0]) * half, half)
        keep_ref[j] = grad_all[pl.ds(keep, half), :]
        send_ref[j * half : (j + 1) * half, :] = grad_all[pl.ds(send, half), :]
    sums = a_ref[...] + b_ref[...]
    send_ref[groups * half :, :] = jnp.concatenate([sums, jnp.zeros_like(sums)]).astype(low)


def merge_grads(core, ctx, dmerged, a, b):
    rows, width = ctx[0].shape
    model = dmerged.shape[1]
    groups, half = len(ctx), width // 2
    return kernel_call(
        functools.partial(merge_grad_kernel, groups),
        "merge_grads",
        [*ctx, dmerged, a, b],
        [((groups, half, model), low), ((groups * half + 16, model), low)],
        far_in=[i for i in range(groups + 3) if i != groups],
        scalars=[core],
        scratch=[pltpu.VMEM((width, model), low)],
    )


def merge_heads_kernel(groups, a_ref, b_ref, keep_ref, got_ref, near_ref, send_ref, sums_ref):
    half = keep_ref.shape[1]
    total = lambda j: keep_ref[j].astype(wide) + got_ref[j * half : (j + 1) * half, :].astype(wide)
    for k in range(groups // 2):
        near_ref[k] = total(2 * k).astype(low)
        send_ref[k * half : (k + 1) * half, :] = total(2 * k + 1).astype(low)
    sums = a_ref[...] + b_ref[...] + got_ref[groups * half : groups * half + 16, :].astype(wide)[:8]
    sums_ref[...] = sums
    at = groups // 2 * half
    send_ref[at:, :] = jnp.concatenate([sums, jnp.zeros_like(sums)]).astype(low)


def merge_heads(a, b, keep, got):
    groups, half, model = keep.shape
    count = groups // 2
    return kernel_call(
        functools.partial(merge_heads_kernel, groups),
        "merge_heads",
        [a, b, keep, got],
        [((count, half, model), low), ((count * half + 16, model), low), ((8, model), wide)],
    )


def merge_far_kernel(keep_ref, got_ref, sums_ref, near_ref, send_ref, out_sums_ref):
    half = keep_ref.shape[1]
    near_ref[...] = (keep_ref[0].astype(wide) + got_ref[:half, :].astype(wide)).astype(low)
    far = keep_ref[1].astype(wide) + got_ref[half : 2 * half, :].astype(wide)
    send_ref[:half, :] = far.astype(low)
    sums = sums_ref[...] + got_ref[2 * half :, :].astype(wide)[:8]
    out_sums_ref[...] = sums
    send_ref[half:, :] = jnp.concatenate([sums, jnp.zeros_like(sums)]).astype(low)


def merge_far(keep, got, sums, waits):
    _, half, model = keep.shape
    return kernel_call(
        merge_far_kernel,
        "merge_far",
        [keep, got, sums],
        [((half, model), low), ((half + 16, model), low), ((8, model), wide)],
        waits=waits,
    )


def slots_kernel(block, size, slot, grad_ref, core_ref, near_ref, far_ref, sums_ref, *refs):
    own_ref, send_refs, (out_sums_ref, rows_all) = refs[0], refs[1:-2], refs[-2:]
    shares = len(send_refs) + 1
    half = near_ref.shape[0]
    merged = (near_ref[...].astype(wide) + far_ref[:half, :].astype(wide)).astype(low)
    for k in range(shares):
        rows_all[k] = merged[k * size : (k + 1) * size]
    sums = sums_ref[...] + far_ref[half:, :].astype(wide)[:8]
    out_sums_ref[...] = sums
    start = pad16(block) + 16
    for m, ref in enumerate((own_ref, *send_refs)):
        ref[:start, :] = (grad_ref[m].astype(wide) + core_ref[m].astype(wide)).astype(low)
        ref[start : start + size, :] = rows_all[(slot[0] >> 1) ^ m]
        if m:
            both = jnp.concatenate([sums, jnp.zeros_like(sums)]).astype(low)
            ref[start + pad16(size) :, :] = both


def slot_parts(slot, block, size, grads, core, near, far, sums, waits):
    shares, _, model = core.shape
    rows = pad16(block) + 16 + pad16(size)
    return kernel_call(
        functools.partial(slots_kernel, block, size),
        "slot_parts",
        [grads, core, near, far, sums],
        [((rows, model), low)]
        + [((rows + 16, model), low)] * (shares - 1)
        + [((8, model), wide)],
        scalars=[slot],
        scratch=[pltpu.VMEM((shares, size, model), low)],
        waits=waits,
    )


def slot_sum_kernel(own_ref, sums_ref, *refs):
    got_refs, (out_ref, out_sums_ref) = refs[:-2], refs[-2:]
    rows = own_ref.shape[0]
    total, sums = own_ref[...].astype(wide), sums_ref[...]
    for ref in got_refs:
        total += ref[:rows, :].astype(wide)
        sums += ref[rows:, :].astype(wide)[:8]
    out_ref[...] = total.astype(low)
    out_sums_ref[...] = sums


def slot_sum(own, sums, got, waits):
    return kernel_call(
        slot_sum_kernel,
        "slot_sum",
        [own, sums, *got],
        [(own.shape, low), (sums.shape, wide)],
        waits=waits,
    )


def feed_out_kernel(units, grads_ref, inner_ref, outer_ref, bias_ref, here, inner, outer, bias, sems):
    slots, rows, model = grads_ref.shape
    copies = [pltpu.make_async_copy(grads_ref.at[k], here.at[k], sems.at[0, k]) for k in range(slots)]
    for copy in copies:
        copy.start()
    done = []
    for k, copy in enumerate(copies):
        copy.wait()
        cols = slice(k * units, (k + 1) * units)
        inner[:, cols] = here[k, :units, :].astype(wide).T
        outer[cols, :] = here[k, units : 2 * units, :].astype(wide)
        bias[k : k + 1, :] = here[k, 2 * units : 2 * units + 16, :units].astype(wide)[:1]
        done.append(pltpu.make_async_copy(inner.at[:, cols], inner_ref.at[:, cols], sems.at[1, k]))
        done.append(pltpu.make_async_copy(outer.at[cols, :], outer_ref.at[cols, :], sems.at[2, k]))
        done[-2].start()
        done[-1].start()
    done.append(pltpu.make_async_copy(bias, bias_ref, sems.at[0, 0]))
    done[-1].start()
    for copy in done:
        copy.wait()


def feed_out(grads, units):
    slots, rows, model = grads.shape
    hidden = slots * units
    if units % 128:
        inner = grads[:, :units].reshape(hidden, model).astype(wide).T
        outer = grads[:, units : 2 * units].reshape(hidden, model).astype(wide)
        return inner, outer, grads[:, 2 * units, :units].astype(wide)
    shapes = [(model, hidden), (hidden, model), (slots, units)]
    return pl.pallas_call(
        functools.partial(feed_out_kernel, units),
        in_specs=[in_hbm],
        out_specs=[in_hbm] * 3,
        out_shape=[jax.ShapeDtypeStruct(shape, wide) for shape in shapes],
        scratch_shapes=[pltpu.VMEM(grads.shape, low)]
        + [pltpu.VMEM(shape, wide) for shape in shapes]
        + [pltpu.SemaphoreType.DMA((3, slots))],
        compiler_params=params(60),
        name="feed_out",
    )(grads)


def qkv_out_kernel(block, order, slot, *refs):
    parts, refs = refs[: len(order)], refs[len(order) :]
    q_ref, k_ref, v_ref, merge_ref, bias_ref, rows_all, merge_all = refs
    start, size = pad16(block), merge_all.shape[1]
    width = q_ref.shape[1]
    slots = merge_all.shape[0]
    for mask, part in zip(order, parts):
        at = slot[0] ^ mask
        rows_all[at] = part[:block, :]
        bias_ref[pl.ds(at, 1), :] = part[start : start + 16, :].astype(wide)[:1]
        at = (at & 1) * (slots // 2) + (at >> 1)
        merge_all[at] = part[start + 16 : start + 16 + size, :]
    grad = rows_all[...].reshape(3 * width, -1)
    for i, ref in enumerate((q_ref, k_ref, v_ref)):
        ref[...] = grad[i * width : (i + 1) * width].astype(wide).T
    merge_ref[...] = merge_all[...].reshape(merge_ref.shape).astype(wide)


def qkv_out(slot, parts, order, block, width):
    model = parts[0].shape[-1]
    slots = 3 * width // block
    size = width // slots
    return kernel_call(
        functools.partial(qkv_out_kernel, block, order),
        "qkv_out",
        parts,
        [((model, width), wide)] * 3 + [((width, model), wide), ((slots, model), wide)],
        scalars=[slot],
        scratch=[pltpu.VMEM((slots, block, model), low), pltpu.VMEM((slots, size, model), low)],
    )


def shards(
    tokens,
    querymap,
    querybias,
    keymap,
    valuemap,
    valuebias,
    mergemap,
    mergebias,
    normgain,
    normshift,
    innermap,
    innerbias,
    outermap,
    outerbias,
    finalgain,
    finalshift,
    lengths,
    cotangent,
):
    proteins, share, model = tokens.shape
    groups = lax.axis_size("heads")
    rows = proteins * share
    width = querymap.shape[1]
    seq, heads = lax.axis_index("seq"), lax.axis_index("heads")
    seq_size, dp_size = lax.axis_size("seq"), lax.axis_size("dp")
    pos = jnp.concatenate([lengths, jnp.stack([seq, heads]).astype(jnp.int32)])
    core_bit, row_bit, far_bit = ("seq", 1), ("heads", 1), ("heads", 2)
    seq_bits = [("seq", 1 << k) for k in range(1, seq_size.bit_length() - 1)]
    share_bits = seq_bits + [("dp", 1 << k) for k in range(dp_size.bit_length() - 1)]
    slot_bits = [core_bit] + share_bits
    slots = 1 << len(slot_bits)
    shares = slots // 2
    slot = lax.axis_index("dp") * seq_size + seq
    units = innermap.shape[1] // slots
    merge_units = width // slots
    row = lambda vector: vector.reshape(1, -1)

    slot_scalar = slot.reshape(1).astype(jnp.int32)

    own_rows = tokens.reshape(rows, model)
    small = jnp.stack([mergebias, normgain, normshift, outerbias, finalgain, finalshift])
    small = jnp.pad(small.astype(wide), ((0, 2), (0, 0)))
    second = swap(own_rows, *far_bit)
    first = swap(own_rows, *row_bit)
    maps = [querymap, keymap, valuemap]
    biases = [row(querybias), row(valuebias)]
    merge_own = lax.dynamic_slice_in_dim(mergemap, slot * merge_units, merge_units, 0)
    merge_all = lax.all_gather(merge_own, ("dp", "seq", "heads"))
    merge_all = merge_all.reshape(slots, groups, merge_units, model)
    own = own_units(slot_scalar, shares, innermap, outermap, row(innerbias), [small])

    def exchange_keys(piece):
        found = {0: piece}
        for axis, stride in seq_bits + [core_bit]:
            for i in list(found):
                found[i | stride] = swap(found[i], axis, stride)
        return found

    maps_biases = [*maps, *biases]
    seq_tokens = {i: [] for i in range(0, seq_size, 2)}

    def exchange_tokens(piece):
        found = {0: piece}
        for axis, stride in seq_bits:
            for i in list(found):
                found[i | stride] = swap(found[i], axis, stride)
        for i in found:
            seq_tokens[i].append(found[i])
        return [found[i] for i in found if i]

    far_tokens = [exchange_tokens(own_rows)]
    far_units = swap(pack_units(own, []), *far_bit)
    second_held = hold(second, [first, own[0], *far_tokens[0]])
    third = swap(second_held, *row_bit)
    q_three, kv_three = project([own_rows, first, second_held], maps_biases, proteins)
    kv_three = exchange_keys(kv_three)
    q_last, kv_last = project([third], maps_biases, proteins, [q_three])
    kv_last = exchange_keys(kv_last)
    queries = [q_three, q_last]
    kv_pieces = [stack[i] for i in range(seq_size) for stack in (kv_three, kv_last)]
    token_pieces = [own_rows, first, second, third]
    pairs = split_units(units, far_units, [q_last])
    order = list(range(len(share_bits)))
    masks = [[0], [0]]
    for k, bits in enumerate(zip(order, order[::-1])):
        if k:
            pairs = stack_pairs(pairs)
        pairs = [(p, swap(p, *share_bits[bit])) for p, bit in zip(pairs, bits)]
        masks = [(have, [m | (1 << bit) for m in have]) for have, bit in zip(masks, bits)]
        if k < len(order) - 1:
            masks = [a + b for a, b in masks]
    far_tokens += [exchange_tokens(piece) for piece in token_pieces[1:]]

    stacked = [p for pair in pairs for p in pair[:1]]
    context, context_t, logsum = attend(pos, queries, kv_pieces, stacked)
    context = [c.reshape(rows, width) for c in context]
    context = [context[0]] + [swap(context[j], "heads", j) for j in range(1, groups)]
    normed, normed_low, first_unit, first_inverse, other_maps = merge_norm(
        heads.reshape(1).astype(jnp.int32),
        context,
        mergemap,
        merge_all,
        own_rows,
        small,
        [],
    )
    inner_t, outer_w, inner_b = join_units(
        own, [p for pair in pairs for p in pair], [m for pair in masks for m in pair], [normed_low]
    )

    normed_near, normed_across = swap(normed_low, *core_bit), swap(normed_low, *row_bit)
    near_act, near_slope, near_own, near_other = feed_forward(
        normed_low, normed_near, inner_t, outer_w, inner_b
    )
    normed_across = hold(normed_across, [near_act, *far_tokens[1]])
    normed_both = swap(normed_across, *core_bit)
    normed_rows = [normed_low, normed_near, normed_across, normed_both]
    far_act, far_slope, far_own, far_other = feed_forward(
        normed_across, normed_both, inner_t, outer_w, inner_b, [near_act]
    )
    (far_part,) = add_split(far_own, swap(far_other, *core_bit), [rows])
    far_sum = swap(far_part, *row_bit)
    own_at = (seq * groups + heads) * share + jnp.arange(share, dtype=jnp.int32)
    live = (own_at[None, :] < lengths[:, None]).astype(wide).reshape(rows, 1)
    layer_output, dsum_final, dbranch, final_sums = final_norm(
        normed,
        near_own,
        swap(near_other, *core_bit),
        far_sum,
        small,
        cotangent.reshape(rows, model),
        jnp.broadcast_to(live, (rows, 128)),
        far_tokens[2],
    )
    dbranch_near, dbranch_across = swap(dbranch, *core_bit), swap(dbranch, *row_bit)
    near_dinner, near_own, near_other = feed_backward(
        dbranch, dbranch_near, inner_t, outer_w, near_slope
    )
    dbranch_across = hold(dbranch_across, [near_dinner, *far_tokens[3]])
    dbranch_both = swap(dbranch_across, *core_bit)
    dbranch_rows = [dbranch, dbranch_near, dbranch_across, dbranch_both]
    hid_block = 2 * units
    last = len(share_bits) - 1
    numbers = lambda k, side: [m for m in range(shares) if (m >> k) & 1 == side]
    acts = [near_act, far_act]
    outer_send = weight_grad(acts, dbranch_rows, hid_block, numbers(last, 1), 0, [near_dinner])
    outer_got = swap(outer_send, *share_bits[last])
    far_dinner, far_own, far_other = feed_backward(
        dbranch_across,
        dbranch_both,
        inner_t,
        outer_w,
        far_slope,
        [outer_send, near_dinner],
    )
    (far_part,) = add_split(far_own, swap(far_other, *core_bit), [rows])
    far_sum = swap(far_part, *row_bit)

    dinners = [near_dinner, far_dinner]
    inner_send = weight_grad(dinners, normed_rows, hid_block, numbers(0, 1), 1, [far_part])
    inner_got = swap(inner_send, *share_bits[0])
    dfirst, dmerged, first_sums, dcontext = first_back(
        dsum_final,
        near_own,
        swap(near_other, *core_bit),
        far_sum,
        first_unit,
        first_inverse,
        small,
        mergemap,
        other_maps,
        [inner_send],
    )
    dcontext = [dcontext[0]] + [swap(dcontext[j], "heads", j) for j in range(1, groups)]
    dcontext = [d.reshape(proteins, share, width) for d in dcontext]
    core = bit_of(core_bit).reshape(1).astype(jnp.int32)
    merge_keep, merge_send = merge_grads(core, context, dmerged, final_sums, first_sums)
    merge_keep, merge_send, sums = merge_heads(
        final_sums, first_sums, merge_keep, swap(merge_send, *core_bit)
    )
    merge_got = swap(merge_send, *row_bit)
    merge_near, merge_send, sums = merge_far(merge_keep, merge_got, sums, [])
    merge_got = swap(merge_send, *far_bit)

    def shared_sum(hid, row_list, got, k, bias, waits):
        bits = [b for i, b in enumerate(share_bits) if i != k]
        if not bits:
            (keep,) = weight_grad(hid, row_list, hid_block, numbers(k, 0), bias, waits)
            return keep, got
        keep, send = weight_grad(hid, row_list, hid_block, numbers(k, 0), bias, waits, got)
        got = swap(send, *bits[-1])
        for bit in reversed(bits[:-1]):
            half = keep.shape[0] // 2
            keep, send = add_split(keep, got, [half, half])
            got = swap(send, *bit)
        return keep, got

    outer_sums = shared_sum(acts, dbranch_rows, outer_got, last, 0, [merge_send])
    inner_sums = shared_sum(dinners, normed_rows, inner_got, 0, 1, [merge_send])

    dqueries, dkv_by_seq = attend_back(
        pos, queries, dcontext, context_t, logsum, kv_pieces, [outer_sums[0], inner_sums[0], merge_send]
    )
    half = groups // 2
    dkv_by_seq = list(dkv_by_seq)
    dkv_by_seq[1::2] = gate(dkv_by_seq[1::2], [inner_sums[1], outer_sums[1], merge_got])
    own_pack, send_pack = pack_sums(units, *inner_sums, *outer_sums, [dqueries])
    far_pack = swap(send_pack, *far_bit)
    dkv_parts = [
        add_split(dkv_by_seq[i], swap(dkv_by_seq[i + 1], *core_bit), [groups])[0]
        for i in range(0, seq_size, 2)
    ]
    pairs = list(zip(dkv_parts, [seq_tokens[i] for i in range(0, seq_size, 2)]))
    slot_grads = qkv_grads(slot_scalar, slots, dqueries, pairs, [send_pack])
    block = 3 * width // slots
    slot_send = slot_parts(
        slot_scalar,
        block,
        merge_units,
        slot_grads,
        swap(slot_grads[shares:], *core_bit),
        merge_near,
        merge_got,
        sums,
        [],
    )
    slot_got = [swap_slots(slot_send[m], m << 1) for m in range(1, shares)]
    parts = dkv_parts
    for k in reversed(range(len(seq_bits))):
        count = 1 << k
        got = [swap(parts[count + i], *seq_bits[k]) for i in range(count)]
        if k:
            parts = [add_split(parts[i], got[i], [groups])[0] for i in range(count)]

    got[:1] = gate(got[:1], slot_got)

    part_none, part_one, part_two, part_three = dtokens(
        dqueries, parts[0], got[0], maps, [slot_send[0]]
    )
    rest = swap(part_three, *row_bit)
    near = swap(part_one, *row_bit)
    out_pack, extra = slot_sum(slot_send[0], slot_send[-1], slot_got, [part_three])
    (far_send,) = add_split(part_two, rest, [rows], [out_pack])
    far = swap(far_send, *far_bit)

    (pack,) = add_split(own_pack, far_pack, [own_pack.shape[0]], [part_three])
    grads = lax.all_gather(pack, ("dp", "seq"))

    parts = [out_pack] + [swap_slots(out_pack, m << 1) for m in range(1, shares)]
    order = [m << 1 for m in range(shares)]
    q_grad, k_grad, v_grad, mergemap_grad, bias_rows = qkv_out(
        slot_scalar,
        parts + [swap(part, *core_bit) for part in parts],
        order + [m | 1 for m in order],
        block,
        width,
    )
    tokens_grad = kernel_call(
        tokens_kernel, "tokens_grad", [dfirst, part_none, near, far], [((rows, model), low)]
    )[0]
    innermap_grad, outermap_grad, innerbias_grad = feed_out(grads, units)
    innerbias_grad = innerbias_grad.reshape(-1)
    bias_grads = bias_rows[:, :block].reshape(-1)
    shape = tokens.shape
    return (
        layer_output.reshape(shape),
        tokens_grad.reshape(shape),
        q_grad,
        bias_grads[:width],
        k_grad,
        v_grad,
        bias_grads[2 * width :],
        mergemap_grad,
        extra[3],
        extra[4],
        extra[5],
        innermap_grad,
        innerbias_grad,
        outermap_grad,
        extra[0],
        extra[1],
        extra[2],
    )


def solution(mesh):
    return jax.shard_map(
        shards,
        mesh=mesh,
        in_specs=(
            P("dp", ("seq", "heads"), None),
            P(None, "heads"),
            P("heads"),
            P(None, "heads"),
            P(None, "heads"),
            P("heads"),
            P("heads", None),
            P(),
            P(),
            P(),
            P(None, "heads"),
            P("heads"),
            P("heads", None),
            P(),
            P(),
            P(),
            P("dp"),
            P("dp", ("seq", "heads"), None),
        ),
        out_specs=(
            P("dp", ("seq", "heads"), None),
            P("dp", ("seq", "heads"), None),
            P(None, "heads"),
            P("heads"),
            P(None, "heads"),
            P(None, "heads"),
            P("heads"),
            P("heads", None),
            P(),
            P(),
            P(),
            P(None, "heads"),
            P("heads"),
            P("heads", None),
            P(),
            P(),
            P(),
        ),
        check_vma=False,
    )
```

time: 445 us -> 393 us (0.88)
  waiting for transfers between devices: 229 us -> 167 us
  Pallas kernels: 55.5 us -> 88 us
  other arithmetic: 17.9 us -> 0.68 us
  matrix products: 9.56 us -> 0 us
  local copies, waits for them, and re-layouts: 38.3 us -> 47 us
    ppermute x70 -> x55, waiting for transfers between devices: 229 us -> 146 us  [swap(): return lax.ppermute(value, axis, [(i, i ^ stride) for i in range(size)])]
    pallas_call x18 -> x42, Pallas kernels: 55.5 us -> 88 us  [the longest x39 83.3 us: kernel_call(): pl.pallas_call(whole, in_specs=[in_smem] * ns + [in_hbm if i in far_in el...]
    ppermute x0 -> x6, waiting for transfers between devices: none -> 16.3 us  [swap_slots(): lax.ppermute(value, ('dp', 'seq'), [(i, i ^ mask) for i in range(size)])]
    ppermute x70 -> x55, starting transfers between devices: 70.8 us -> 55.2 us  [swap(): return lax.ppermute(value, axis, [(i, i ^ stride) for i in range(size)])]
    ppermute x0 -> x6, starting transfers between devices: none -> 11.7 us  [swap_slots(): lax.ppermute(value, ('dp', 'seq'), [(i, i ^ mask) for i in range(size)])]
    dot_general x20 -> x0, matrix products: 9.56 us -> none  [the longest x8 4.19 us: dot(): return jnp.dot(a, b, preferred_element_type=wide)]
    convert_element_type x26 -> x0, other arithmetic: 9.39 us -> none  [the longest x19 5.74 us: add_low(): return (a.astype(wide) + b.astype(wide)).astype(low)]
    unnamed x268 -> x242, local copies, waits for them, and re-layouts: 29.2 us -> 37.9 us
  transfers between devices with their start and end apart: 71 -> 63, of which waited for: 32 -> 33; matrix products, arithmetic and copies ran while one was open for 8% -> 2% of each run, Pallas kernels for 10% -> 16%
where the time goes in v2:
time: 393 us; the launch traced here: 385 us
  waiting for transfers between devices  167 us (42%)
  Pallas kernels  88 us (22%)
  starting transfers between devices  66.9 us (17%)
  local copies, waits for them, and re-layouts  47 us (12%)
  between operations  15.8 us (4%)
    ppermute x55, waiting for transfers between devices, swap(): return lax.ppermute(value, axis, [(i, i ^ stride) for i in range(size)])  146 us
    pallas_call x39, Pallas kernels, kernel_call(): pl.pallas_call(whole, in_specs=[in_smem] * ns + [in_hbm if i in far_in el...  83.3 us
    ppermute x55, starting transfers between devices, swap(): return lax.ppermute(value, axis, [(i, i ^ stride) for i in range(size)])  55.2 us
    unnamed x242, local copies, waits for them, and re-layouts  37.9 us
    ppermute x6, waiting for transfers between devices, swap_slots(): lax.ppermute(value, ('dp', 'seq'), [(i, i ^ mask) for i in range(size)])  16.3 us
    ppermute x6, starting transfers between devices, swap_slots(): lax.ppermute(value, ('dp', 'seq'), [(i, i ^ mask) for i in range(size)])  11.7 us
  transfers between devices with their start and end apart: 63, of which 33 were waited for; matrix products, arithmetic and copies ran while one was open for 2% of the time, Pallas kernels for 16%

profile of v2, /device:TPU:0, one launch (start us, length us, event | category | flops | bytes accessed | tf_op | source)
XLA Modules:
  0.0 385.2 jit_solution(10960263332233239096)
XLA Ops:
  8.8 3.0 collective-permute-start.2
  11.8 2.6 collective-permute-start.1
  14.4 1.6 collective-permute-start
  20.9 1.6 copy-done.50
  22.5 1.6 copy-done.51
  26.0 13.1 %collective-permute-done.1.refs_0_.refs_5_ = bf16[256,1024]{1,0:T(8,128)(2,1)} collective-permute-done((bf16[256,1024]{1,0:T(8,128)(2,1)}, bf16[256,1024]{1,0:T(8,128)(2,1)}, u32[]{:S(2)}, u32[]{:S(2)}) %collective-permute-start.1) | collective-permute-done | bytes 524320 | tf_op jit(solution)/shard_map/ppermute | solution.py:35
  41.2 4.3 %project.2 = (bf16[3,4,64,256]{3,2,1,0:T(8,128)(2,1)}, bf16[3,4,64,512]{3,2,1,0:T(8,128)(2,1)}) custom-call(bf16[256,1024]{1,0:T(8,128)(2,1)} %bitcast.28, bf16[256,1024]{1,0:T(8,128)(2,1)} %copy-done.22, bf16[256,1024]{1,0:T(8,128)(2,1)} %copy-done.56, bf16[1024,256]{1,0:T(8,128)(2,1)} %refs_3_.5, bf16[1024,256]{1,0:T(8,128)(2,1)} %refs_4_.3, ...), custom_call_target="tpu_custom_call" | custom-call | flops 1 | bytes 1 | tf_op jit(solution)/shard_map/project/pallas_call | solution.py:97
  46.7 1.5 collective-permute-start.4
  48.2 2.5 collective-permute-start.3
  50.7 13.5 %collective-permute-done.9.refs_9_.refs_16_ = bf16[3,4,64,512]{3,2,1,0:T(8,128)(2,1)} collective-permute-done((bf16[3,4,64,512]{3,2,1,0:T(8,128)(2,1)}, bf16[3,4,64,512]{3,2,1,0:T(8,128)(2,1)}, u32[]{:S(2)}, u32[]{:S(2)}) %collective-permute-start.9) | collective-permute-done | bytes 786464 | tf_op jit(solution)/shard_map/ppermute | solution.py:35
  64.2 9.4 %collective-permute-done.3.refs_0_.refs_6_ = bf16[256,1024]{1,0:T(8,128)(2,1)} collective-permute-done((bf16[256,1024]{1,0:T(8,128)(2,1)S(1)}, bf16[256,1024]{1,0:T(8,128)(2,1)}, u32[]{:S(2)}, u32[]{:S(2)}) %collective-permute-start.3) | collective-permute-done | bytes 524320 | tf_op jit(solution)/shard_map/ppermute | solution.py:35
  73.6 2.9 project.3
  78.7 1.9 collective-permute-start.10
  80.7 3.2 collective-permute-done.6.refs_3_
  83.9 3.2 collective-permute-done.10.refs_10_.refs_17_
  87.7 2.6 collective-permute-done.5.refs_1_
  91.0 2.2 stack_pairs.1
  94.3 8.7 %attend.1 = (bf16[4,64,256]{2,1,0:T(8,128)(2,1)}, bf16[4,64,256]{2,1,0:T(8,128)(2,1)}, bf16[4,64,256]{2,1,0:T(8,128)(2,1)}, bf16[4,64,256]{2,1,0:T(8,128)(2,1)},...) custom-call(s32[6]{0:T(128)} %pad_add_fusion.refs_0_, bf16[3,4,64,256]{3,2,1,0:T(8,128)(2,1)} %get-tuple-element.108.refs_6_.refs_1_, ...), custom_call_target="tpu_custom_call" | custom-call | flops 10000000000 | bytes 1 | tf_op jit(solution)/shard_map/attend/pallas_call | solution.py:97
  103.1 2.7 collective-permute-start.13
  105.7 3.4 collective-permute-start.14
  110.0 2.4 collective-permute-start.17
  113.6 4.8 %collective-permute-done.14.refs_3_ = bf16[256,256]{1,0:T(8,128)(2,1)S(1)} collective-permute-done((bf16[256,256]{1,0:T(8,128)(2,1)}, bf16[256,256]{1,0:T(8,128)(2,1)S(1)}, u32[]{:S(2)}, u32[]{:S(2)}) %collective-permute-start.14) | collective-permute-done | bytes 131104 | tf_op jit(solution)/shard_map/ppermute | solution.py:35
  119.2 5.3 %merge_norm.1 = (f32[256,1024]{1,0:T(8,128)}, bf16[256,1024]{1,0:T(8,128)(2,1)}, f32[256,1024]{1,0:T(8,128)}, f32[256,128]{1,0:T(8,128)}, bf16[3,256,1024]{2,1,0:T(8,128)(2,1)}) custom-call(s32[1]{0:T(128)} %bitcast.refs_0_, bf16[256,256]{1,0:T(8,128)(2,1)} %bitcast.31, bf16[256,256]{1,0:T(8,128)(2,1)} %copy-done.87, bf16[256,256]{1,0:T(8,128)(2,1)} %copy-done.89, ...), custom_call_target="tpu_custom_call" | custom-call | flops 1 | bytes 1 | tf_op jit(solution)/shard_map/merge_norm/pallas_call | solution.py:97
  124.6 1.8 collective-permute-start.21
  126.4 2.1 collective-permute-start.20
  129.3 4.4 %join_units.1 = (bf16[1024,1024]{1,0:T(8,128)(2,1)}, bf16[1024,1024]{1,0:T(8,128)(2,1)}, f32[1,1024]{1,0:T(1,128)}) custom-call(bf16[4,128,1024]{2,1,0:T(8,128)(2,1)} %copy-done.8, bf16[4,128,1024]{2,1,0:T(8,128)(2,1)} %copy-done.37, bf16[4,16,128]{2,1,0:T(8,128)(2,1)} %copy-done.104, bf16[2,144,1024]{2,1,0:T(8,128)(2,1)} %get-tuple-element.114.refs_3_, ...), custom_call_target="tpu_custom_call" | custom-call | flops 1 | bytes 1 | tf_op jit(solution)/shard_map/join_units/pallas_call | solution.py:97
  133.7 1.6 copy-done
  135.3 1.6 copy-done.2
  137.6 3.6 feed_forward.2
  142.0 1.6 hold.4.refs_0_.refs_4_
  143.7 1.9 collective-permute-done.22.refs_1_.refs_5_
  145.7 2.8 feed_forward.3
  154.8 10.2 %collective-permute-done.25.refs_7_.refs_10_ = bf16[256,1024]{1,0:T(8,128)(2,1)S(1)} collective-permute-done((bf16[256,1024]{1,0:T(8,128)(2,1)}, bf16[256,1024]{1,0:T(8,128)(2,1)S(1)}, u32[]{:S(2)}, u32[]{:S(2)}) %collective-permute-start.25) | collective-permute-done | bytes 524320 | tf_op jit(solution)/shard_map/ppermute | solution.py:35
  165.1 2.6 collective-permute-done.24.refs_3_
  172.9 2.9 final_norm.1
  178.7 3.2 feed_backward.2
  182.7 8.6 %collective-permute-done.29.refs_2_.refs_11_ = bf16[256,1024]{1,0:T(8,128)(2,1)S(1)} collective-permute-done((bf16[256,1024]{1,0:T(8,128)(2,1)}, bf16[256,1024]{1,0:T(8,128)(2,1)S(1)}, u32[]{:S(2)}, u32[]{:S(2)}) %collective-permute-start.29) | collective-permute-done | bytes 524320 | tf_op jit(solution)/shard_map/ppermute | solution.py:35
  192.4 1.9 collective-permute-done.30.refs_5_.refs_1_
  195.8 2.4 feed_backward.3
  208.1 7.3 %collective-permute-done.32.refs_3_ = bf16[256,1024]{1,0:T(8,128)(2,1)} collective-permute-done((bf16[256,1024]{1,0:T(8,128)(2,1)S(1)}, bf16[256,1024]{1,0:T(8,128)(2,1)}, u32[]{:S(2)}, u32[]{:S(2)}) %collective-permute-start.32) | collective-permute-done | bytes 524320 | tf_op jit(solution)/shard_map/ppermute | solution.py:35
  215.5 2.7 first_back.1
  221.6 2.1 collective-permute-start.36
  226.1 2.3 collective-permute-start.34
  228.4 14.0 %collective-permute-done.38.refs_1_ = bf16[272,1024]{1,0:T(8,128)(2,1)S(1)} collective-permute-done((bf16[272,1024]{1,0:T(8,128)(2,1)S(1)}, bf16[272,1024]{1,0:T(8,128)(2,1)S(1)}, u32[]{:S(2)}, u32[]{:S(2)}) %collective-permute-start.38) | collective-permute-done | bytes 557088 | tf_op jit(solution)/shard_map/ppermute | solution.py:35
  242.4 2.4 collective-permute-start.35
  245.0 2.2 collective-permute-done.36.refs_6_
  247.2 2.3 collective-permute-start.42
  249.6 2.1 weight_grad.6
  252.5 2.1 weight_grad.7
  255.5 1.8 collective-permute-start.40
  258.0 12.4 %attend_back.1 = (bf16[4,4,64,256]{3,2,1,0:T(8,128)(2,1)}, bf16[4,4,64,512]{3,2,1,0:T(8,128)(2,1)}, bf16[4,4,64,512]{3,2,1,0:T(8,128)(2,1)}, bf16[4,4,64,512]{3,2,1,0:T(8,128)(2,1)}, bf16[4,4,64,512]{3,2,1,0:T(8,128)(2,1)}) custom-call(s32[6]{0:T(128)} %pad_add_fusion.refs_0_, bf16[3,4,64,256]{3,2,1,0:T(8,128)(2,1)} %get-tuple-element.108.refs_6_.refs_1_, ...), custom_call_target="tpu_custom_call" | custom-call | flops 20000000000 | bytes 1 | tf_op jit(solution)/shard_map/attend_back/pallas_call | solution.py:97
  279.9 4.2 %qkv_grads.1.refs_1_ = bf16[8,112,1024]{2,1,0:T(8,128)(2,1)S(1)} custom-call(s32[1]{0:T(128)} %bitcast.3.refs_0_, bf16[4,4,64,256]{3,2,1,0:T(8,128)(2,1)S(1)} %copy-done.17, bf16[4,4,64,512]{3,2,1,0:T(8,128)(2,1)S(1)} %add_split.8.refs_2_.refs_1_, bf16[256,1024]{1,0:T(8,128)(2,1)S(1)} %bitcast.30, bf16[256,1024]{1,0:T(8,128)(2,1)S(1)} %copy-done.24, ...), custom_call_target="tpu_custom_call" | custom-call | flops 1 | bytes 1 | tf_op jit(solution)/shard_map/qkv_grads/pallas_call | solution.py:97
  288.2 3.7 collective-permute-start.48
  293.1 24.3 %collective-permute-done.45.refs_0_ = bf16[4,4,64,512]{3,2,1,0:T(8,128)(2,1)S(1)} collective-permute-done((bf16[4,4,64,512]{3,2,1,0:T(8,128)(2,1)S(1)}, bf16[4,4,64,512]{3,2,1,0:T(8,128)(2,1)S(1)}, u32[]{:S(2)}, u32[]{:S(2)}) %collective-permute-start.45) | collective-permute-done | bytes 1048608 | tf_op jit(solution)/shard_map/ppermute | solution.py:35
  317.4 6.5 %collective-permute-done.47.refs_1_.refs_2_ = bf16[160,1024]{1,0:T(8,128)(2,1)S(1)} collective-permute-done((bf16[160,1024]{1,0:T(8,128)(2,1)S(1)}, bf16[160,1024]{1,0:T(8,128)(2,1)S(1)}, u32[]{:S(2)}, u32[]{:S(2)}) %collective-permute-start.47) | collective-permute-done | bytes 327712 | tf_op jit(solution)/shard_map/ppermute | solution.py:40
  323.9 1.8 dtokens.1
  328.7 5.1 %collective-permute-start.55 = (bf16[144,1024]{1,0:T(8,128)(2,1)S(1)}, bf16[144,1024]{1,0:T(8,128)(2,1)S(1)}, u32[]{:S(2)}, u32[]{:S(2)}) collective-permute-start(bf16[144,1024]{1,0:T(8,128)(2,1)S(1)} %get-tuple-element.186.refs_2_.refs_1_), channel_id=1, source_target_pairs={{0,24},{4,28},{8,16},{12,20},{16,8},{20,12},{24,0},{28,4},{1,25},{... | collective-permute-start | bytes 884744 | tf_op jit(solution)/shard_map/ppermute | solution.py:40
  334.6 6.6 %collective-permute-done.51.refs_1_ = bf16[256,1024]{1,0:T(8,128)(2,1)S(1)} collective-permute-done((bf16[256,1024]{1,0:T(8,128)(2,1)S(1)}, bf16[256,1024]{1,0:T(8,128)(2,1)S(1)}, u32[]{:S(2)}, u32[]{:S(2)}) %collective-permute-start.51) | collective-permute-done | bytes 524320 | tf_op jit(solution)/shard_map/ppermute | solution.py:35
  345.4 7.6 %collective-permute-done.54.refs_3_ = bf16[144,1024]{1,0:T(8,128)(2,1)S(1)} collective-permute-done((bf16[144,1024]{1,0:T(8,128)(2,1)S(1)}, bf16[144,1024]{1,0:T(8,128)(2,1)S(1)}, u32[]{:S(2)}, u32[]{:S(2)}) %collective-permute-start.54) | collective-permute-done | bytes 294944 | tf_op jit(solution)/shard_map/ppermute | solution.py:40
  355.3 2.4 qkv_out.1
  358.3 4.5 %collective-permute-done.50.refs_2_ = bf16[256,1024]{1,0:T(8,128)(2,1)S(1)} collective-permute-done((bf16[256,1024]{1,0:T(8,128)(2,1)}, bf16[256,1024]{1,0:T(8,128)(2,1)S(1)}, u32[]{:S(2)}, u32[]{:S(2)}) %collective-permute-start.50) | collective-permute-done | bytes 524320 | tf_op jit(solution)/shard_map/ppermute | solution.py:35
  362.8 4.7 %collective-permute-done.52.refs_3_ = bf16[256,1024]{1,0:T(8,128)(2,1)S(1)} collective-permute-done((bf16[256,1024]{1,0:T(8,128)(2,1)}, bf16[256,1024]{1,0:T(8,128)(2,1)S(1)}, u32[]{:S(2)}, u32[]{:S(2)}) %collective-permute-start.52) | collective-permute-done | bytes 524320 | tf_op jit(solution)/shard_map/ppermute | solution.py:35
  368.5 4.9 %all-gather.7.cloned.1.call-done = bf16[2176,1024]{1,0:T(8,128)(2,1)} async-done(((bf16[272,1024]{1,0:T(8,128)(2,1)}), bf16[2176,1024]{1,0:T(8,128)(2,1)}) %all-gather.7.cloned.1.call-update) | async-done | bytes 4456464 | tf_op jit(solution)/shard_map/all_gather | solution.py:1307
  373.4 4.7 %feed_out.1 = (f32[1024,1024]{1,0:T(8,128)}, f32[1024,1024]{1,0:T(8,128)}, f32[8,128]{1,0:T(8,128)}) custom-call(bf16[8,272,1024]{2,1,0:T(8,128)(2,1)} %bitcast.35), custom_call_target="tpu_custom_call" | custom-call | tf_op jit(solution)/shard_map/feed_out/pallas_call | solution.py:1015
  (370 shorter events, 83.5 us)
Async XLA Ops:
  7.2 111.3 %all-gather.5.cloned.1.call-start = ((), (), s32[]{:S(2)}) async-start(), calls=%async_computation | async-start | bytes 2162688 | tf_op jit(solution)/shard_map/all_gather | solution.py:1108
  8.7 364.6 %all-gather.7.cloned.1.call-start = ((), (), s32[]{:S(2)}) async-start(), calls=%async_computation.1 | async-start | bytes 5013504 | tf_op jit(solution)/shard_map/all_gather | solution.py:1307
  8.8 17.2 %collective-permute-start.2 = (bf16[256,1024]{1,0:T(8,128)(2,1)}, bf16[256,1024]{1,0:T(8,128)(2,1)S(1)}, u32[]{:S(2)}, u32[]{:S(2)}) collective-permute-start(bf16[256,1024]{1,0:T(8,128)(2,1)} %bitcast.25), channel_id=1, source_target_pairs={{0,8},{4,12},{8,0},{12,4},{1,9},{5,13},{9,1},{13,5},{2,10},{6,14},... | collective-permute-start | bytes 1572872 | tf_op jit(solution)/shard_map/ppermute | solution.py:35
  11.8 27.3 %collective-permute-start.1 = (bf16[256,1024]{1,0:T(8,128)(2,1)}, bf16[256,1024]{1,0:T(8,128)(2,1)}, u32[]{:S(2)}, u32[]{:S(2)}) collective-permute-start(bf16[256,1024]{1,0:T(8,128)(2,1)} %bitcast.26), channel_id=1, source_target_pairs={{0,2},{1,3},{2,0},{3,1},{4,6},{5,7},{6,4},{7,5},{8,10},{9,11},{10,... | collective-permute-start | bytes 1572872 | tf_op jit(solution)/shard_map/ppermute | solution.py:35
  14.4 24.7 %collective-permute-start = (bf16[256,1024]{1,0:T(8,128)(2,1)}, bf16[256,1024]{1,0:T(8,128)(2,1)S(1)}, u32[]{:S(2)}, u32[]{:S(2)}) collective-permute-start(bf16[256,1024]{1,0:T(8,128)(2,1)} %bitcast.27), channel_id=1, source_target_pairs={{0,1},{1,0},{2,3},{3,2},{4,5},{5,4},{6,7},{7,6},{8,9},{9,8},{10,11... | collective-permute-start | bytes 1572872 | tf_op jit(solution)/shard_map/ppermute | solution.py:35
  45.5 18.7 %collective-permute-start.9 = (bf16[3,4,64,512]{3,2,1,0:T(8,128)(2,1)}, bf16[3,4,64,512]{3,2,1,0:T(8,128)(2,1)}, u32[]{:S(2)}, u32[]{:S(2)}) collective-permute-start(bf16[3,4,64,512]{3,2,1,0:T(8,128)(2,1)} %get-tuple-element.116.refs_5_.refs_12_), channel_id=1, source_target_pairs={{0,8},{4,12},{8,0},{12,4},{1,9},{5,13},{9,1},{13,5},{2,10},{6,14},... | collective-permute-start | bytes 2359304 | tf_op jit(solution)/shard_map/ppermute | solution.py:35
  46.7 40.4 %copy-start.111 = (s32[4]{0:T(128)S(1)}, s32[4]{0:T(128)}, u32[]{:S(2)}) copy-start(s32[4]{0:T(128)} %param.34) | copy-start | bytes 52
  46.7 29.8 %collective-permute-start.4 = (bf16[272,1024]{1,0:T(8,128)(2,1)S(1)}, bf16[272,1024]{1,0:T(8,128)(2,1)S(1)}, u32[]{:S(2)}, u32[]{:S(2)}) collective-permute-start(bf16[272,1024]{1,0:T(8,128)(2,1)S(1)} %pack_units.1), channel_id=1, source_target_pairs={{0,2},{1,3},{2,0},{3,1},{4,6},{5,7},{6,4},{7,5},{8,10},{9,11},{10,... | collective-permute-start | bytes 1671176 | tf_op jit(solution)/shard_map/ppermute | solution.py:35
  48.2 25.4 %collective-permute-start.3 = (bf16[256,1024]{1,0:T(8,128)(2,1)S(1)}, bf16[256,1024]{1,0:T(8,128)(2,1)}, u32[]{:S(2)}, u32[]{:S(2)}) collective-permute-start(bf16[256,1024]{1,0:T(8,128)(2,1)S(1)} %copy-done.57), channel_id=1, source_target_pairs={{0,1},{1,0},{2,3},{3,2},{4,5},{5,4},{6,7},{7,6},{8,9},{9,8},{10,11... | collective-permute-start | bytes 1572872 | tf_op jit(solution)/shard_map/ppermute | solution.py:35
  50.7 42.6 %collective-permute-start.7 = (bf16[3,4,64,512]{3,2,1,0:T(8,128)(2,1)}, bf16[3,4,64,512]{3,2,1,0:T(8,128)(2,1)S(1)}, u32[]{:S(2)}, u32[]{:S(2)}) collective-permute-start(bf16[3,4,64,512]{3,2,1,0:T(8,128)(2,1)} %get-tuple-element.116.refs_5_.refs_12_), channel_id=1, source_target_pairs={{0,4},{4,0},{8,12},{12,8},{1,5},{5,1},{9,13},{13,9},{2,6},{6,2},{1... | collective-permute-start | bytes 2359304 | tf_op jit(solution)/shard_map/ppermute | solution.py:35
  64.2 29.1 %collective-permute-start.11 = (bf16[3,4,64,512]{3,2,1,0:T(8,128)(2,1)}, bf16[3,4,64,512]{3,2,1,0:T(8,128)(2,1)}, u32[]{:S(2)}, u32[]{:S(2)}) collective-permute-start(bf16[3,4,64,512]{3,2,1,0:T(8,128)(2,1)} %collective-permute-done.9.refs_9_.refs_16_), channel_id=1, source_target_pairs={{0,4},{4,0},{8,12},{12,8},{1,5},{5,1},{9,13},{13,9},{2,6},{6,2},{1... | collective-permute-start | bytes 2359304 | tf_op jit(solution)/shard_map/ppermute | solution.py:35
  77.5 6.4 %collective-permute-start.6 = (bf16[1,128,1024]{2,1,0:T(8,128)(2,1)S(1)}, bf16[1,128,1024]{2,1,0:T(8,128)(2,1)S(1)}, u32[]{:S(2)}, u32[]{:S(2)}) collective-permute-start(bf16[1,128,1024]{2,1,0:T(8,128)(2,1)S(1)} %get-tuple-element.113.refs_2_), channel_id=1, source_target_pairs={{0,16},{16,0},{1,17},{17,1},{2,18},{18,2},{3,19},{19,3},{4,20},{20... | collective-permute-start | bytes 786440 | tf_op jit(solution)/shard_map/ppermute | solution.py:35
  78.7 8.4 %collective-permute-start.10 = (bf16[1,4,64,512]{3,2,1,0:T(8,128)(2,1)}, bf16[1,4,64,512]{3,2,1,0:T(8,128)(2,1)S(1)}, u32[]{:S(2)}, u32[]{:S(2)}) collective-permute-start(bf16[1,4,64,512]{3,2,1,0:T(8,128)(2,1)} %get-tuple-element.117.refs_6_.refs_13_), channel_id=1, source_target_pairs={{0,8},{4,12},{8,0},{12,4},{1,9},{5,13},{9,1},{13,5},{2,10},{6,14},... | collective-permute-start | bytes 786440 | tf_op jit(solution)/shard_map/ppermute | solution.py:35
  80.6 9.6 %collective-permute-start.5 = (bf16[1,144,1024]{2,1,0:T(8,128)(2,1)S(1)}, bf16[1,144,1024]{2,1,0:T(8,128)(2,1)S(1)}, u32[]{:S(2)}, u32[]{:S(2)}) collective-permute-start(bf16[1,144,1024]{2,1,0:T(8,128)(2,1)S(1)} %get-tuple-element.112.refs_0_), channel_id=1, source_target_pairs={{0,8},{4,12},{8,0},{12,4},{1,9},{5,13},{9,1},{13,5},{2,10},{6,14},... | collective-permute-start | bytes 884744 | tf_op jit(solution)/shard_map/ppermute | solution.py:35
  83.9 9.3 %collective-permute-start.8 = (bf16[1,4,64,512]{3,2,1,0:T(8,128)(2,1)}, bf16[1,4,64,512]{3,2,1,0:T(8,128)(2,1)S(1)}, u32[]{:S(2)}, u32[]{:S(2)}) collective-permute-start(bf16[1,4,64,512]{3,2,1,0:T(8,128)(2,1)} %get-tuple-element.117.refs_6_.refs_13_), channel_id=1, source_target_pairs={{0,4},{4,0},{8,12},{12,8},{1,5},{5,1},{9,13},{13,9},{2,6},{6,2},{1... | collective-permute-start | bytes 786440 | tf_op jit(solution)/shard_map/ppermute | solution.py:35
  87.1 6.2 %collective-permute-start.12 = (bf16[1,4,64,512]{3,2,1,0:T(8,128)(2,1)S(1)}, bf16[1,4,64,512]{3,2,1,0:T(8,128)(2,1)S(1)}, u32[]{:S(2)}, u32[]{:S(2)}) collective-permute-start(bf16[1,4,64,512]{3,2,1,0:T(8,128)(2,1)S(1)} %collective-permute-done.10.refs_10_.refs_17_), channel_id=1, source_target_pairs={{0,4},{4,0},{8,12},{12,8},{1,5},{5,1},{9,13},{13,9},{2,6},{6,2},{1... | collective-permute-start | bytes 786440 | tf_op jit(solution)/shard_map/ppermute | solution.py:35
  103.1 10.5 %collective-permute-start.13 = (bf16[256,256]{1,0:T(8,128)(2,1)}, bf16[256,256]{1,0:T(8,128)(2,1)S(1)}, u32[]{:S(2)}, u32[]{:S(2)}) collective-permute-start(bf16[256,256]{1,0:T(8,128)(2,1)} %bitcast.50), channel_id=1, source_target_pairs={{0,1},{1,0},{2,3},{3,2},{4,5},{5,4},{6,7},{7,6},{8,9},{9,8},{10,11... | collective-permute-start | bytes 393224 | tf_op jit(solution)/shard_map/ppermute | solution.py:35
  105.7 12.7 %collective-permute-start.14 = (bf16[256,256]{1,0:T(8,128)(2,1)}, bf16[256,256]{1,0:T(8,128)(2,1)S(1)}, u32[]{:S(2)}, u32[]{:S(2)}) collective-permute-start(bf16[256,256]{1,0:T(8,128)(2,1)} %bitcast.49), channel_id=1, source_target_pairs={{0,2},{1,3},{2,0},{3,1},{4,6},{5,7},{6,4},{7,5},{8,10},{9,11},{10,... | collective-permute-start | bytes 393224 | tf_op jit(solution)/shard_map/ppermute | solution.py:35
  109.1 9.3 %collective-permute-start.15 = (bf16[256,256]{1,0:T(8,128)(2,1)}, bf16[256,256]{1,0:T(8,128)(2,1)S(1)}, u32[]{:S(2)}, u32[]{:S(2)}) collective-permute-start(bf16[256,256]{1,0:T(8,128)(2,1)} %bitcast.48), channel_id=1, source_target_pairs={{0,3},{1,2},{2,1},{3,0},{4,7},{5,6},{6,5},{7,4},{8,11},{9,10},{10,... | collective-permute-start | bytes 393224 | tf_op jit(solution)/shard_map/ppermute | solution.py:35
  110.0 18.5 %collective-permute-start.17 = (bf16[2,144,1024]{2,1,0:T(8,128)(2,1)S(1)}, bf16[2,144,1024]{2,1,0:T(8,128)(2,1)S(1)}, u32[]{:S(2)}, u32[]{:S(2)}) collective-permute-start(bf16[2,144,1024]{2,1,0:T(8,128)(2,1)S(1)} %copy-done.107), channel_id=1, source_target_pairs={{0,16},{16,0},{1,17},{17,1},{2,18},{18,2},{3,19},{19,3},{4,20},{20... | collective-permute-start | bytes 1769480 | tf_op jit(solution)/shard_map/ppermute | solution.py:35
  112.4 16.0 %collective-permute-start.18 = (bf16[2,128,1024]{2,1,0:T(8,128)(2,1)}, bf16[2,128,1024]{2,1,0:T(8,128)(2,1)}, u32[]{:S(2)}, u32[]{:S(2)}) collective-permute-start(bf16[2,128,1024]{2,1,0:T(8,128)(2,1)} %get-tuple-element.115.refs_4_.refs_5_), channel_id=1, source_target_pairs={{0,8},{4,12},{8,0},{12,4},{1,9},{5,13},{9,1},{13,5},{2,10},{6,14},... | collective-permute-start | bytes 1572872 | tf_op jit(solution)/shard_map/ppermute | solution.py:35
  124.5 9.2 %collective-permute-start.16 = (bf16[256,1024]{1,0:T(8,128)(2,1)}, bf16[256,1024]{1,0:T(8,128)(2,1)S(1)}, u32[]{:S(2)}, u32[]{:S(2)}) collective-permute-start(bf16[256,1024]{1,0:T(8,128)(2,1)} %get-tuple-element.123.refs_7_.refs_0_.refs_2_), channel_id=1, source_target_pairs={{0,4},{4,0},{8,12},{12,8},{1,5},{5,1},{9,13},{13,9},{2,6},{6,2},{1... | collective-permute-start | bytes 1572872 | tf_op jit(solution)/shard_map/ppermute | solution.py:35
  124.6 17.4 %collective-permute-start.21 = (bf16[256,1024]{1,0:T(8,128)(2,1)S(1)}, bf16[256,1024]{1,0:T(8,128)(2,1)S(1)}, u32[]{:S(2)}, u32[]{:S(2)}) collective-permute-start(bf16[256,1024]{1,0:T(8,128)(2,1)S(1)} %copy-done.23), channel_id=1, source_target_pairs={{0,8},{4,12},{8,0},{12,4},{1,9},{5,13},{9,1},{13,5},{2,10},{6,14},... | collective-permute-start | bytes 1572872 | tf_op jit(solution)/shard_map/ppermute | solution.py:35
  126.4 15.6 %collective-permute-start.20 = (bf16[256,1024]{1,0:T(8,128)(2,1)}, bf16[256,1024]{1,0:T(8,128)(2,1)}, u32[]{:S(2)}, u32[]{:S(2)}) collective-permute-start(bf16[256,1024]{1,0:T(8,128)(2,1)} %get-tuple-element.123.refs_7_.refs_0_.refs_2_), channel_id=1, source_target_pairs={{0,1},{1,0},{2,3},{3,2},{4,5},{5,4},{6,7},{7,6},{8,9},{9,8},{10,11... | collective-permute-start | bytes 1572872 | tf_op jit(solution)/shard_map/ppermute | solution.py:35
  143.7 2.0 collective-permute-start.22
  150.5 1.9 collective-permute-start.23
  150.6 14.4 %collective-permute-start.25 = (bf16[256,1024]{1,0:T(8,128)(2,1)}, bf16[256,1024]{1,0:T(8,128)(2,1)S(1)}, u32[]{:S(2)}, u32[]{:S(2)}) collective-permute-start(bf16[256,1024]{1,0:T(8,128)(2,1)} %collective-permute-done.1.refs_0_.refs_5_), channel_id=1, source_target_pairs={{0,8},{4,12},{8,0},{12,4},{1,9},{5,13},{9,1},{13,5},{2,10},{6,14},... | collective-permute-start | bytes 1572872 | tf_op jit(solution)/shard_map/ppermute | solution.py:35
  150.8 14.2 %collective-permute-start.19 = (bf16[256,1024]{1,0:T(8,128)(2,1)}, bf16[256,1024]{1,0:T(8,128)(2,1)}, u32[]{:S(2)}, u32[]{:S(2)}) collective-permute-start(bf16[256,1024]{1,0:T(8,128)(2,1)} %get-tuple-element.128), channel_id=1, source_target_pairs={{0,4},{4,0},{8,12},{12,8},{1,5},{5,1},{9,13},{13,9},{2,6},{6,2},{1... | collective-permute-start | bytes 1572872 | tf_op jit(solution)/shard_map/ppermute | solution.py:35
  153.4 14.2 %collective-permute-start.24 = (bf16[256,1024]{1,0:T(8,128)(2,1)}, bf16[256,1024]{1,0:T(8,128)(2,1)S(1)}, u32[]{:S(2)}, u32[]{:S(2)}) collective-permute-start(bf16[256,1024]{1,0:T(8,128)(2,1)} %add_split.6), channel_id=1, source_target_pairs={{0,1},{1,0},{2,3},{3,2},{4,5},{5,4},{6,7},{7,6},{8,9},{9,8},{10,11... | collective-permute-start | bytes 1572872 | tf_op jit(solution)/shard_map/ppermute | solution.py:35
  176.8 1.9 collective-permute-start.26
  176.8 14.5 %collective-permute-start.29 = (bf16[256,1024]{1,0:T(8,128)(2,1)}, bf16[256,1024]{1,0:T(8,128)(2,1)S(1)}, u32[]{:S(2)}, u32[]{:S(2)}) collective-permute-start(bf16[256,1024]{1,0:T(8,128)(2,1)} %collective-permute-done.3.refs_0_.refs_6_), channel_id=1, source_target_pairs={{0,8},{4,12},{8,0},{12,4},{1,9},{5,13},{9,1},{13,5},{2,10},{6,14},... | collective-permute-start | bytes 1572872 | tf_op jit(solution)/shard_map/ppermute | solution.py:35
  177.5 14.1 %collective-permute-start.28 = (bf16[256,1024]{1,0:T(8,128)(2,1)S(1)}, bf16[256,1024]{1,0:T(8,128)(2,1)S(1)}, u32[]{:S(2)}, u32[]{:S(2)}) collective-permute-start(bf16[256,1024]{1,0:T(8,128)(2,1)S(1)} %get-tuple-element.134.refs_0_.refs_2_), channel_id=1, source_target_pairs={{0,1},{1,0},{2,3},{3,2},{4,5},{5,4},{6,7},{7,6},{8,9},{9,8},{10,11... | collective-permute-start | bytes 1572872 | tf_op jit(solution)/shard_map/ppermute | solution.py:35
  192.4 1.9 collective-permute-start.30
  199.2 1.9 collective-permute-start.31
  199.4 8.7 %collective-permute-start.27 = (bf16[256,1024]{1,0:T(8,128)(2,1)}, bf16[256,1024]{1,0:T(8,128)(2,1)S(1)}, u32[]{:S(2)}, u32[]{:S(2)}) collective-permute-start(bf16[256,1024]{1,0:T(8,128)(2,1)} %get-tuple-element.137), channel_id=1, source_target_pairs={{0,4},{4,0},{8,12},{12,8},{1,5},{5,1},{9,13},{13,9},{2,6},{6,2},{1... | collective-permute-start | bytes 1572872 | tf_op jit(solution)/shard_map/ppermute | solution.py:35
  201.3 14.1 %collective-permute-start.32 = (bf16[256,1024]{1,0:T(8,128)(2,1)S(1)}, bf16[256,1024]{1,0:T(8,128)(2,1)}, u32[]{:S(2)}, u32[]{:S(2)}) collective-permute-start(bf16[256,1024]{1,0:T(8,128)(2,1)S(1)} %add_split.7.refs_6_), channel_id=1, source_target_pairs={{0,1},{1,0},{2,3},{3,2},{4,5},{5,4},{6,7},{7,6},{8,9},{9,8},{10,11... | collective-permute-start | bytes 1572872 | tf_op jit(solution)/shard_map/ppermute | solution.py:35
  220.1 3.6 collective-permute-start.37
  220.2 31.5 %collective-permute-start.39 = (bf16[2,272,1024]{2,1,0:T(8,128)(2,1)S(1)}, bf16[2,272,1024]{2,1,0:T(8,128)(2,1)S(1)}, u32[]{:S(2)}, u32[]{:S(2)}) collective-permute-start(bf16[2,272,1024]{2,1,0:T(8,128)(2,1)S(1)} %weight_grad.5.refs_9_), channel_id=1, source_target_pairs={{0,8},{4,12},{8,0},{12,4},{1,9},{5,13},{9,1},{13,5},{2,10},{6,14},... | collective-permute-start | bytes 3342344 | tf_op jit(solution)/shard_map/ppermute | solution.py:35
  221.6 25.6 %collective-permute-start.36 = (bf16[2,256,1024]{2,1,0:T(8,128)(2,1)S(1)}, bf16[2,256,1024]{2,1,0:T(8,128)(2,1)S(1)}, u32[]{:S(2)}, u32[]{:S(2)}) collective-permute-start(bf16[2,256,1024]{2,1,0:T(8,128)(2,1)S(1)} %copy-done.44), channel_id=1, source_target_pairs={{0,16},{16,0},{1,17},{17,1},{2,18},{18,2},{3,19},{19,3},{4,20},{20... | collective-permute-start | bytes 3145736 | tf_op jit(solution)/shard_map/ppermute | solution.py:35
  224.0 18.4 %collective-permute-start.38 = (bf16[272,1024]{1,0:T(8,128)(2,1)S(1)}, bf16[272,1024]{1,0:T(8,128)(2,1)S(1)}, u32[]{:S(2)}, u32[]{:S(2)}) collective-permute-start(bf16[272,1024]{1,0:T(8,128)(2,1)S(1)} %get-tuple-element.160), channel_id=1, source_target_pairs={{0,1},{1,0},{2,3},{3,2},{4,5},{5,4},{6,7},{7,6},{8,9},{9,8},{10,11... | collective-permute-start | bytes 1671176 | tf_op jit(solution)/shard_map/ppermute | solution.py:35
  225.3 30.2 %collective-permute-start.33 = (bf16[256,256]{1,0:T(8,128)(2,1)S(1)}, bf16[256,256]{1,0:T(8,128)(2,1)S(1)}, u32[]{:S(2)}, u32[]{:S(2)}) collective-permute-start(bf16[256,256]{1,0:T(8,128)(2,1)S(1)} %get-tuple-element.149), channel_id=1, source_target_pairs={{0,1},{1,0},{2,3},{3,2},{4,5},{5,4},{6,7},{7,6},{8,9},{9,8},{10,11... | collective-permute-start | bytes 393224 | tf_op jit(solution)/shard_map/ppermute | solution.py:35
  226.1 31.2 %collective-permute-start.34 = (bf16[256,256]{1,0:T(8,128)(2,1)S(1)}, bf16[256,256]{1,0:T(8,128)(2,1)S(1)}, u32[]{:S(2)}, u32[]{:S(2)}) collective-permute-start(bf16[256,256]{1,0:T(8,128)(2,1)S(1)} %get-tuple-element.150), channel_id=1, source_target_pairs={{0,2},{1,3},{2,0},{3,1},{4,6},{5,7},{6,4},{7,5},{8,10},{9,11},{10,... | collective-permute-start | bytes 393224 | tf_op jit(solution)/shard_map/ppermute | solution.py:35
  242.4 14.9 %collective-permute-start.35 = (bf16[256,256]{1,0:T(8,128)(2,1)S(1)}, bf16[256,256]{1,0:T(8,128)(2,1)S(1)}, u32[]{:S(2)}, u32[]{:S(2)}) collective-permute-start(bf16[256,256]{1,0:T(8,128)(2,1)S(1)} %get-tuple-element.151), channel_id=1, source_target_pairs={{0,3},{1,2},{2,1},{3,0},{4,7},{5,6},{6,5},{7,4},{8,11},{9,10},{10,... | collective-permute-start | bytes 393224 | tf_op jit(solution)/shard_map/ppermute | solution.py:35
  247.2 23.2 %collective-permute-start.42 = (bf16[144,1024]{1,0:T(8,128)(2,1)S(1)}, bf16[144,1024]{1,0:T(8,128)(2,1)S(1)}, u32[]{:S(2)}, u32[]{:S(2)}) collective-permute-start(bf16[144,1024]{1,0:T(8,128)(2,1)S(1)} %get-tuple-element.162.refs_7_.refs_11_), channel_id=1, source_target_pairs={{0,2},{1,3},{2,0},{3,1},{4,6},{5,7},{6,4},{7,5},{8,10},{9,11},{10,... | collective-permute-start | bytes 884744 | tf_op jit(solution)/shard_map/ppermute | solution.py:35
  251.7 18.7 %collective-permute-start.41 = (bf16[1,256,1024]{2,1,0:T(8,128)(2,1)}, bf16[1,256,1024]{2,1,0:T(8,128)(2,1)S(1)}, u32[]{:S(2)}, u32[]{:S(2)}) collective-permute-start(bf16[1,256,1024]{2,1,0:T(8,128)(2,1)} %get-tuple-element.170), channel_id=1, source_target_pairs={{0,8},{4,12},{8,0},{12,4},{1,9},{5,13},{9,1},{13,5},{2,10},{6,14},... | collective-permute-start | bytes 1572872 | tf_op jit(solution)/shard_map/ppermute | solution.py:35
  255.5 14.9 %collective-permute-start.40 = (bf16[1,272,1024]{2,1,0:T(8,128)(2,1)}, bf16[1,272,1024]{2,1,0:T(8,128)(2,1)S(1)}, u32[]{:S(2)}, u32[]{:S(2)}) collective-permute-start(bf16[1,272,1024]{2,1,0:T(8,128)(2,1)} %get-tuple-element.169), channel_id=1, source_target_pairs={{0,16},{16,0},{1,17},{17,1},{2,18},{18,2},{3,19},{19,3},{4,20},{20... | collective-permute-start | bytes 1671176 | tf_op jit(solution)/shard_map/ppermute | solution.py:35
  274.9 2.9 collective-permute-start.43
  274.9 4.4 %collective-permute-start.44 = (bf16[4,4,64,512]{3,2,1,0:T(8,128)(2,1)}, bf16[4,4,64,512]{3,2,1,0:T(8,128)(2,1)S(1)}, u32[]{:S(2)}, u32[]{:S(2)}) collective-permute-start(bf16[4,4,64,512]{3,2,1,0:T(8,128)(2,1)} %copy-done.72), channel_id=1, source_target_pairs={{0,4},{4,0},{8,12},{12,8},{1,5},{5,1},{9,13},{13,9},{2,6},{6,2},{1... | collective-permute-start | bytes 3145736 | tf_op jit(solution)/shard_map/ppermute | solution.py:35
  284.1 2.5 collective-permute-start.46
  284.3 33.0 %collective-permute-start.45 = (bf16[4,4,64,512]{3,2,1,0:T(8,128)(2,1)S(1)}, bf16[4,4,64,512]{3,2,1,0:T(8,128)(2,1)S(1)}, u32[]{:S(2)}, u32[]{:S(2)}) collective-permute-start(bf16[4,4,64,512]{3,2,1,0:T(8,128)(2,1)S(1)} %add_split.9.refs_7_), channel_id=1, source_target_pairs={{0,8},{4,12},{8,0},{12,4},{1,9},{5,13},{9,1},{13,5},{2,10},{6,14},... | collective-permute-start | bytes 3145736 | tf_op jit(solution)/shard_map/ppermute | solution.py:35
  285.2 41.5 %collective-permute-start.60 = (bf16[272,1024]{1,0:T(8,128)(2,1)S(1)}, bf16[272,1024]{1,0:T(8,128)(2,1)S(1)}, u32[]{:S(2)}, u32[]{:S(2)}) collective-permute-start(bf16[272,1024]{1,0:T(8,128)(2,1)S(1)} %get-tuple-element.174.refs_12_), channel_id=1, source_target_pairs={{0,2},{1,3},{2,0},{3,1},{4,6},{5,7},{6,4},{7,5},{8,10},{9,11},{10,... | collective-permute-start | bytes 1671176 | tf_op jit(solution)/shard_map/ppermute | solution.py:35
  287.2 36.6 %collective-permute-start.47 = (bf16[160,1024]{1,0:T(8,128)(2,1)S(1)}, bf16[160,1024]{1,0:T(8,128)(2,1)S(1)}, u32[]{:S(2)}, u32[]{:S(2)}) collective-permute-start(bf16[160,1024]{1,0:T(8,128)(2,1)S(1)} %get-tuple-element.177), channel_id=1, source_target_pairs={{0,8},{4,12},{8,0},{12,4},{16,24},{20,28},{24,16},{28,20},{1,9},{5... | collective-permute-start | bytes 983048 | tf_op jit(solution)/shard_map/ppermute | solution.py:40
  288.2 35.7 %collective-permute-start.48 = (bf16[160,1024]{1,0:T(8,128)(2,1)S(1)}, bf16[160,1024]{1,0:T(8,128)(2,1)S(1)}, u32[]{:S(2)}, u32[]{:S(2)}) collective-permute-start(bf16[160,1024]{1,0:T(8,128)(2,1)S(1)} %get-tuple-element.178), channel_id=1, source_target_pairs={{0,16},{4,20},{8,24},{12,28},{16,0},{20,4},{24,8},{28,12},{1,17},{... | collective-permute-start | bytes 983048 | tf_op jit(solution)/shard_map/ppermute | solution.py:40
  291.9 32.0 %collective-permute-start.49 = (bf16[160,1024]{1,0:T(8,128)(2,1)S(1)}, bf16[160,1024]{1,0:T(8,128)(2,1)S(1)}, u32[]{:S(2)}, u32[]{:S(2)}) collective-permute-start(bf16[160,1024]{1,0:T(8,128)(2,1)S(1)} %get-tuple-element.179), channel_id=1, source_target_pairs={{0,24},{4,28},{8,16},{12,20},{16,8},{20,12},{24,0},{28,4},{1,25},{... | collective-permute-start | bytes 983048 | tf_op jit(solution)/shard_map/ppermute | solution.py:40
  327.7 13.4 %collective-permute-start.51 = (bf16[256,1024]{1,0:T(8,128)(2,1)S(1)}, bf16[256,1024]{1,0:T(8,128)(2,1)S(1)}, u32[]{:S(2)}, u32[]{:S(2)}) collective-permute-start(bf16[256,1024]{1,0:T(8,128)(2,1)S(1)} %get-tuple-element.184.refs_5_.refs_2_), channel_id=1, source_target_pairs={{0,1},{1,0},{2,3},{3,2},{4,5},{5,4},{6,7},{7,6},{8,9},{9,8},{10,11... | collective-permute-start | bytes 1572872 | tf_op jit(solution)/shard_map/ppermute | solution.py:35
  328.7 14.2 %collective-permute-start.56 = (bf16[144,1024]{1,0:T(8,128)(2,1)S(1)}, bf16[144,1024]{1,0:T(8,128)(2,1)S(1)}, u32[]{:S(2)}, u32[]{:S(2)}) collective-permute-start(bf16[144,1024]{1,0:T(8,128)(2,1)S(1)} %get-tuple-element.186.refs_2_.refs_1_), channel_id=1, source_target_pairs={{0,4},{4,0},{8,12},{12,8},{1,5},{5,1},{9,13},{13,9},{2,6},{6,2},{1... | collective-permute-start | bytes 884744 | tf_op jit(solution)/shard_map/ppermute | solution.py:35
  328.7 16.7 %collective-permute-start.55 = (bf16[144,1024]{1,0:T(8,128)(2,1)S(1)}, bf16[144,1024]{1,0:T(8,128)(2,1)S(1)}, u32[]{:S(2)}, u32[]{:S(2)}) collective-permute-start(bf16[144,1024]{1,0:T(8,128)(2,1)S(1)} %get-tuple-element.186.refs_2_.refs_1_), channel_id=1, source_target_pairs={{0,24},{4,28},{8,16},{12,20},{16,8},{20,12},{24,0},{28,4},{1,25},{... | collective-permute-start | bytes 884744 | tf_op jit(solution)/shard_map/ppermute | solution.py:40
  333.8 19.2 %collective-permute-start.54 = (bf16[144,1024]{1,0:T(8,128)(2,1)S(1)}, bf16[144,1024]{1,0:T(8,128)(2,1)S(1)}, u32[]{:S(2)}, u32[]{:S(2)}) collective-permute-start(bf16[144,1024]{1,0:T(8,128)(2,1)S(1)} %get-tuple-element.186.refs_2_.refs_1_), channel_id=1, source_target_pairs={{0,16},{4,20},{8,24},{12,28},{16,0},{20,4},{24,8},{28,12},{1,17},{... | collective-permute-start | bytes 884744 | tf_op jit(solution)/shard_map/ppermute | solution.py:40
  333.8 19.9 %collective-permute-start.53 = (bf16[144,1024]{1,0:T(8,128)(2,1)S(1)}, bf16[144,1024]{1,0:T(8,128)(2,1)S(1)}, u32[]{:S(2)}, u32[]{:S(2)}) collective-permute-start(bf16[144,1024]{1,0:T(8,128)(2,1)S(1)} %get-tuple-element.186.refs_2_.refs_1_), channel_id=1, source_target_pairs={{0,8},{4,12},{8,0},{12,4},{16,24},{20,28},{24,16},{28,20},{1,9},{5... | collective-permute-start | bytes 884744 | tf_op jit(solution)/shard_map/ppermute | solution.py:40
  341.1 21.7 %collective-permute-start.50 = (bf16[256,1024]{1,0:T(8,128)(2,1)}, bf16[256,1024]{1,0:T(8,128)(2,1)S(1)}, u32[]{:S(2)}, u32[]{:S(2)}) collective-permute-start(bf16[256,1024]{1,0:T(8,128)(2,1)} %get-tuple-element.182), channel_id=1, source_target_pairs={{0,1},{1,0},{2,3},{3,2},{4,5},{5,4},{6,7},{7,6},{8,9},{9,8},{10,11... | collective-permute-start | bytes 1572872 | tf_op jit(solution)/shard_map/ppermute | solution.py:35
  342.8 24.6 %collective-permute-start.52 = (bf16[256,1024]{1,0:T(8,128)(2,1)}, bf16[256,1024]{1,0:T(8,128)(2,1)S(1)}, u32[]{:S(2)}, u32[]{:S(2)}) collective-permute-start(bf16[256,1024]{1,0:T(8,128)(2,1)} %add_split.10), channel_id=1, source_target_pairs={{0,2},{1,3},{2,0},{3,1},{4,6},{5,7},{6,4},{7,5},{8,10},{9,11},{10,... | collective-permute-start | bytes 1572872 | tf_op jit(solution)/shard_map/ppermute | solution.py:35
  345.4 9.0 %collective-permute-start.59 = (bf16[144,1024]{1,0:T(8,128)(2,1)S(1)}, bf16[144,1024]{1,0:T(8,128)(2,1)S(1)}, u32[]{:S(2)}, u32[]{:S(2)}) collective-permute-start(bf16[144,1024]{1,0:T(8,128)(2,1)S(1)} %collective-permute-done.55.refs_4_), channel_id=1, source_target_pairs={{0,4},{4,0},{8,12},{12,8},{1,5},{5,1},{9,13},{13,9},{2,6},{6,2},{1... | collective-permute-start | bytes 884744 | tf_op jit(solution)/shard_map/ppermute | solution.py:35
  353.0 1.6 collective-permute-start.58
  353.7 1.6 collective-permute-start.57
  (120 other events, 879.2 us)
Sparse Core Ops, SparseCore 0:
  11.6 74.1 all-gather.4
  327.8 45.5 all-gather.6
